TPU v7x, 32 devices: a whole 2x2x4 slice. The times are simulated.
32 devices in a mesh: groups: 2 (over y), tensor: 4 (over z), dp: 2 (over x), query: 2 (over core).
Axes of the slice: x: 2, y: 2, z: 4, core: 2. Of those that a mesh axis runs over, the one named last changes fastest.
Arguments:
- inputs: bfloat16 [8, 512, 8192], P(('groups', 'dp', 'query'), None, 'tensor'), parts along dimension 0, may hold values from -6 to 6
- residual: bfloat16 [8, 512, 8192], P(('groups', 'dp', 'query'), 'tensor'), parts along dimension 0, may hold values from -4 to 4
- out_grad: bfloat16 [8, 512, 8192], P(('groups', 'dp', 'query'), 'tensor'), parts along dimension 0, may hold values from -6 to 6
- norm_gain: bfloat16 [8192], replicated, may hold values from 0.099609375 to 1.8984375
- w_out: bfloat16 [8192, 8192], P('tensor'), may hold values from -0.0625 to 0.0625
- proj_in: bfloat16 [64, 8192], P(None, 'tensor'), may hold values from -0.0625 to 0.0625
- proj_out: bfloat16 [64, 8192], replicated, may hold values from -0.0625 to 0.0625
- queries: bfloat16 [1024, 4096], P('query', 'tensor'), may hold values from -0.0078125 to 0.0078125
- segment_ids: int32 [8, 512], P(('groups', 'dp', 'query')), parts along dimension 0, may hold values from 0 to 3, never falling along the last dimension, each value on 1 to 256 neighbouring positions
Outputs:
- input_grad: bfloat16 [8, 512, 8192], P(('groups', 'dp', 'query'), None, 'tensor'), parts along dimension 0
- scores: float32 [32, 1024], P(('groups', 'dp'), 'query'), parts along dimension 0
There are 2 independent parts, one for each index of `groups`. A program takes and returns all parts, laid end to end along the dimension named above; an argument that names none is the same for every part. Nothing has to cross between parts.
Inputs may be any that keep to these rules, and one draw needn't show every extreme that they name: `segment_ids`: within each row of 512 tokens the example numbers never fall and every example number has at least one token.
All inputs are finite; a program needn't handle non-finite values.
Results may differ from a plain program's by a relative error of at most 0.015.
Values may be sent and summed in bfloat16 or wider, within the bound.
No kernel may reach another device: no remote copies, remote signals or barrier semaphores. Data moves between devices by JAX's collectives and lax.ppermute only.
A program may use at most 128 MiB of HBM per device.

v0:
```python
import jax
import jax.numpy as jnp
from jax import lax
from jax.sharding import PartitionSpec as P

EX_DEV = 4


EPS = 1e-05


def norm_backward(proj_rows, resid_rows, grad_rows, norm_gain):
    z = resid_rows.astype(jnp.float32) + proj_rows
    inv = lax.rsqrt(jnp.mean(z * z, axis=-1, keepdims=True) + EPS)
    scaled = norm_gain.astype(jnp.float32) * grad_rows.astype(jnp.float32)
    center = jnp.mean(scaled * z, axis=-1, keepdims=True)
    return (inv * scaled - z * inv * inv * inv * center).astype(jnp.bfloat16)


def project_rows(values, matrix):
    return lax.dot_general(
        values, matrix, (((1,), (1,)), ((), ())), preferred_element_type=jnp.float32
    )


def outer_sums(member, out_side, in_side):
    count = member.shape[1]
    width = out_side.shape[1]
    weighted = (member[:, :, None] * out_side[:, None, :]).reshape(member.shape[0], count * width)
    summed = lax.dot_general(
        weighted, in_side, (((0,), (0,)), ((), ())), precision=lax.Precision.HIGHEST
    )
    return summed.reshape(count, width * in_side.shape[1])


def body(inputs, residual, out_grad, norm_gain, w_out, proj_in, proj_out, queries, segment_ids):
    tok_rows = inputs.reshape(inputs.shape[1], inputs.shape[2])
    parts = lax.axis_size("tensor")
    rank = lax.axis_index("tensor")
    share = tok_rows.shape[0] // parts
    proj_rows = lax.psum_scatter(
        jnp.dot(tok_rows, w_out, preferred_element_type=jnp.float32).astype(jnp.bfloat16),
        "tensor",
        scatter_dimension=0,
        tiled=True,
    ).astype(jnp.float32)
    dproj_rows = norm_backward(proj_rows, residual[0], out_grad[0], norm_gain)
    dproj_all = lax.all_gather(dproj_rows, "tensor", axis=0, tiled=True)
    input_grad = project_rows(dproj_all, w_out).astype(jnp.bfloat16)
    member_all = (segment_ids[0][:, None] == jnp.arange(EX_DEV, dtype=jnp.int32)[None, :]).astype(
        jnp.float32
    )
    partial_in = project_rows(tok_rows, proj_in)
    in_rows = lax.psum_scatter(
        partial_in.astype(jnp.bfloat16), "tensor", scatter_dimension=0, tiled=True
    ).astype(jnp.float32)
    out_rows = project_rows(dproj_rows, proj_out)
    member_rows = lax.dynamic_slice_in_dim(member_all, rank * share, share, 0)
    sketch_part = outer_sums(member_rows, out_rows, in_rows)
    sketch_cols = lax.psum_scatter(
        sketch_part.astype(jnp.bfloat16), "tensor", scatter_dimension=1, tiled=True
    ).astype(jnp.float32)
    paired = lax.all_gather(sketch_cols, "query", axis=0, tiled=True)
    score_part = lax.dot_general(
        paired,
        queries.astype(jnp.float32),
        (((1,), (1,)), ((), ())),
        precision=lax.Precision.HIGHEST,
    )
    scores = lax.psum(score_part, "tensor")
    return (input_grad.reshape(1, input_grad.shape[0], input_grad.shape[1]), scores)


def solution(mesh):
    return jax.shard_map(
        body,
        mesh=mesh,
        in_specs=(
            P(("groups", "dp", "query"), None, "tensor"),
            P(("groups", "dp", "query"), "tensor", None),
            P(("groups", "dp", "query"), "tensor", None),
            P(),
            P("tensor", None),
            P(None, "tensor"),
            P(),
            P("query", "tensor"),
            P(("groups", "dp", "query"), None),
        ),
        out_specs=(P(("groups", "dp", "query"), None, "tensor"), P(("groups", "dp"), "query")),
        check_vma=False,
    )
```

profile of v0, /device:TPU:0, one launch (start us, length us, event | category | flops | bytes accessed | tf_op | source)
XLA Modules:
  0.0 413.8 jit_solution(17632200927118215863)
XLA Ops:
  7.2 1.5 copy-done
  8.8 25.4 %convolution_convert_fusion = bf16[512,8192]{1,0:T(8,128)(2,1)} fusion(bf16[2048,8192]{1,0:T(8,128)(2,1)} %param.13, bf16[1,512,2048]{2,1,0:T(8,128)(2,1)S(1)} %copy-done), kind=kOutput, calls=%fused_computation | convolution fusion | flops 17184063488 | bytes 44040192 | tf_op jit(solution)/shard_map/dot_general | solution.py:42
  34.3 0.9 copy-done.8
  35.1 0.8 fusion.9
  35.9 0.8 copy.15
  36.8 0.8 dynamic-slice
  37.5 144.0 %reduce-scatter.8.cloned.1.call-done = bf16[128,8192]{1,0:T(8,128)(2,1)} async-done(((bf16[512,8192]{1,0:T(8,128)(2,1)}), bf16[128,8192]{1,0:T(8,128)(2,1)}) %reduce-scatter.8.cloned.1.call-update) | async-done | bytes 2097168 | tf_op jit(solution)/shard_map/reduce_scatter | solution.py:41
  181.5 4.5 %multiply_reduce_fusion = (f32[128]{0:T(128)S(1)}, f32[128]{0:T(128)S(1)}) fusion(bf16[128,8192]{1,0:T(8,128)(2,1)} %reduce-scatter.8.cloned.1.call-done, bf16[1,128,8192]{2,1,0:T(8,128)(2,1)} %param.10, bf16[1,128,8192]{2,1,0:T(8,128)(2,1)} %param.11, f32[8192]{0:T(1024)S(1)} %convert_element_type.48), kind=kLoop, calls=%fused_computation.8 | loop fusion | flops 9436928 | bytes 6325248 | tf_op jit(solution)/shard_map/reduce_sum | solution.py:14
  186.1 0.2 copy-done.5
  186.3 1.9 fusion.3
  188.2 0.8 fusion.13
  189.1 14.6 %reduce-scatter.10.cloned.1.call-done = bf16[128,64]{1,0:T(8,128)(2,1)} async-done(((bf16[512,64]{1,0:T(8,128)(2,1)}), bf16[128,64]{1,0:T(8,128)(2,1)}) %reduce-scatter.10.cloned.1.call-update) | async-done | bytes 16400
  203.7 1.0 convolution_convert_fusion.2
  204.7 0.1 copy.14
  204.9 0.1 convert_element_type.56
  205.0 1.5 copy.17
  206.5 0.5 all-gather.3.cloned.1.call-update
  207.1 24.9 %reduce-scatter.12.cloned.1.call-done = bf16[1024,4]{1,0:T(8,128)(2,1)} async-done(((bf16[4096,4]{1,0:T(8,128)(2,1)}), bf16[1024,4]{1,0:T(8,128)(2,1)}) %reduce-scatter.12.cloned.1.call-update) | async-done | bytes 8208
  232.0 1.1 copy.18
  233.1 2.0 all-gather
  235.1 0.9 fusion.14
  236.0 17.4 %psum.7 = f32[8,512]{1,0:T(8,128)} all-reduce(f32[8,512]{1,0:T(8,128)S(1)} %fusion.14), channel_id=1, replica_groups=mesh['groups'=2,'tensor'=4,'dp'=2,'query'=2] {'tensor'}, use_global_device_ids=true, to_apply=%region_5.0 | all-reduce | flops 4096 | bytes 32768 | tf_op jit(solution)/shard_map/psum | solution.py:70
  253.4 129.0 %all-gather.3.cloned.1.call-done = bf16[512,8192]{1,0:T(8,128)(2,1)} async-done(((bf16[128,8192]{1,0:T(8,128)(2,1)}), bf16[512,8192]{1,0:T(8,128)(2,1)}) %all-gather.3.cloned.1.call-update) | async-done | bytes 8388624 | tf_op jit(solution)/shard_map/all_gather | solution.py:48
  382.4 24.8 %fusion.5 = bf16[1,512,2048]{2,1,0:T(8,128)(2,1)} fusion(bf16[512,8192]{1,0:T(8,128)(2,1)} %all-gather.3.cloned.1.call-done, bf16[2048,8192]{1,0:T(8,128)(2,1)} %param.13), kind=kOutput, calls=%fused_computation.10 | convolution fusion | flops 17180917760 | bytes 44040192 | tf_op jit(solution)/shard_map/dot_general | solution.py:21
  (30 shorter events, 0.3 us)
Async XLA Ops:
  7.2 1.6 copy-start
  7.2 174.4 %reduce-scatter.8.cloned.1.call-start = ((), (), s32[]{:S(2)}) async-start(), calls=%async_computation.3 | async-start | bytes 10485760 | tf_op jit(solution)/shard_map/reduce_scatter | solution.py:41
  34.2 0.9 copy-start.8
  34.2 2.6 copy-start.9
  34.2 169.5 %reduce-scatter.10.cloned.1.call-start = ((), (), s32[]{:S(2)}) async-start(), calls=%async_computation.5 | async-start | bytes 163840
  36.7 195.3 %reduce-scatter.12.cloned.1.call-start = ((), (), s32[]{:S(2)}) async-start(), calls=%async_computation.6 | async-start | bytes 1310720
  181.5 4.5 %copy-start.3 = (bf16[1,128,8192]{2,1,0:T(8,128)(2,1)S(1)}, bf16[1,128,8192]{2,1,0:T(8,128)(2,1)}, u32[]{:S(2)}) copy-start(bf16[1,128,8192]{2,1,0:T(8,128)(2,1)} %param.11) | copy-start | bytes 6291460
  181.5 4.5 %copy-start.4 = (bf16[1,128,8192]{2,1,0:T(8,128)(2,1)S(1)}, bf16[1,128,8192]{2,1,0:T(8,128)(2,1)}, u32[]{:S(2)}) copy-start(bf16[1,128,8192]{2,1,0:T(8,128)(2,1)} %param.10) | copy-start | bytes 6291460
  181.5 4.7 %copy-start.5 = (bf16[128,8192]{1,0:T(8,128)(2,1)S(1)}, bf16[128,8192]{1,0:T(8,128)(2,1)}, u32[]{:S(2)}) copy-start(bf16[128,8192]{1,0:T(8,128)(2,1)} %reduce-scatter.8.cloned.1.call-done) | copy-start | bytes 6291460
  186.3 2.0 copy-start.6
  188.2 18.3 %copy-start.2 = (bf16[128,8192]{1,0:T(8,128)(2,1)}, bf16[128,8192]{1,0:T(8,128)(2,1)S(1)}, u32[]{:S(2)}) copy-start(bf16[128,8192]{1,0:T(8,128)(2,1)S(1)} %fusion.3) | copy-start | bytes 6291460
  189.1 46.0 %copy-start.7 = (bf16[512,1024]{1,0:T(8,128)(2,1)S(1)}, bf16[512,1024]{1,0:T(8,128)(2,1)}, u32[]{:S(2)}) copy-start(bf16[512,1024]{1,0:T(8,128)(2,1)} %param.16) | copy-start | bytes 3145732
  206.5 175.9 %all-gather.3.cloned.1.call-start = ((), (), s32[]{:S(2)}) async-start(), calls=%async_computation.4 | async-start | bytes 10485760 | tf_op jit(solution)/shard_map/all_gather | solution.py:48
  382.4 24.8 %copy-start.1 = (bf16[1,512,2048]{2,1,0:T(8,128)(2,1)S(1)}, bf16[1,512,2048]{2,1,0:T(8,128)(2,1)}, u32[]{:S(2)}) copy-start(bf16[1,512,2048]{2,1,0:T(8,128)(2,1)} %param.9) | copy-start | bytes 6291460
Sparse Core Ops, SparseCore 0:
  34.3 147.1 reduce-scatter.7
  183.8 19.9 reduce-scatter.9
  206.6 25.3 reduce-scatter.11
  234.0 148.3 all-gather.2
where the time goes:
time: 414 us
  waiting for transfers between devices  313 us (76%)
  matrix products  53.8 us (13%)
  blocking collectives  19.4 us (5%)
  between operations  13.9 us (3%)
  local copies, waits for them, and re-layouts  6.95 us (2%)
  other arithmetic  6.49 us (2%)
    reduce_scatter x1, waiting for transfers between devices, body(): lax.psum_scatter(jnp.dot(tok_rows, w_out, preferred_element_type=jnp.floa...  144 us
    all_gather x1, waiting for transfers between devices, body(): dproj_all = lax.all_gather(dproj_rows, 'tensor', axis=0, tiled=True)  129 us
    unnamed x6, waiting for transfers between devices  40.1 us
    dot_general x3, matrix products, project_rows(): lax.dot_general(values, matrix, (((1,), (1,)), ((), ())), preferred_eleme...  26.4 us
    dot_general x1, matrix products, body(): jnp.dot(tok_rows, w_out, preferred_element_type=jnp.float32)  25.4 us
    psum x1, blocking collectives, body(): scores = lax.psum(score_part, 'tensor')  17.4 us
  transfers between devices with their start and end apart: 4, of which 4 were waited for; matrix products, arithmetic and copies ran while one was open for 3% of the time, Pallas kernels for 0%

commit v1 on v0

v1 whole, which is shorter than its diff:
```python
import jax
import jax.numpy as jnp
from jax import lax
from jax.sharding import PartitionSpec as P

EX_DEV = 4
EPS = 1e-05
CHUNKS = 4
HALVES = 2


def norm_backward(proj_rows, resid_rows, grad_rows, norm_gain):
    z = resid_rows.astype(jnp.float32) + proj_rows
    inv = lax.rsqrt(jnp.mean(z * z, axis=-1, keepdims=True) + EPS)
    scaled = norm_gain.astype(jnp.float32) * grad_rows.astype(jnp.float32)
    center = jnp.mean(scaled * z, axis=-1, keepdims=True)
    return (inv * scaled - z * inv * inv * inv * center).astype(jnp.bfloat16)


def project_rows(values, matrix):
    return lax.dot_general(
        values, matrix, (((1,), (1,)), ((), ())), preferred_element_type=jnp.float32
    )


def hop(value, pairs):
    return lax.ppermute(value, "tensor", pairs)


def reduce_line(partial, rank, parts):
    def block(index):
        return lax.dynamic_index_in_dim(partial, jnp.clip(index, 0, parts - 1), 0, keepdims=False)

    right = left = None
    for far in range(parts - 1, 0, -1):
        out_right, out_left = block(rank + far), block(rank - far)
        if right is not None:
            out_right = (out_right.astype(jnp.float32) + right.astype(jnp.float32)).astype(jnp.bfloat16)
            out_left = (out_left.astype(jnp.float32) + left.astype(jnp.float32)).astype(jnp.bfloat16)
        right = hop(out_right, [(d, d + 1) for d in range(parts - far)])
        left = hop(out_left, [(d, d - 1) for d in range(far, parts)])
    return (
        block(rank).astype(jnp.float32) + right.astype(jnp.float32) + left.astype(jnp.float32)
    )


def gather_line(own, rank, parts):
    right = left = own
    rights, lefts = [], []
    for far in range(1, parts):
        right = hop(right, [(d, d + 1) for d in range(far - 1, parts - 1)])
        left = hop(left, [(d, d - 1) for d in range(1, parts - far + 1)])
        rights.append(right)
        lefts.append(left)
    blocks = [own]
    for far in range(1, parts):
        blocks.append(jnp.where(rank >= far, rights[far - 1], lefts[parts - far - 1]))
    return blocks


def exchange(value_of, axis, size, rank):
    first = value_of(rank)
    out = jnp.zeros((size,) + first.shape, first.dtype)
    out = lax.dynamic_update_index_in_dim(out, first, rank, 0)
    for shift in range(1, size):
        got = lax.ppermute(
            value_of((rank + shift) % size), axis, [(d, (d + shift) % size) for d in range(size)]
        )
        out = lax.dynamic_update_index_in_dim(out, got, (rank - shift + size) % size, 0)
    return out


def body(inputs, residual, out_grad, norm_gain, w_out, proj_in, proj_out, queries, segment_ids):
    parts = lax.axis_size("tensor")
    rank = lax.axis_index("tensor")
    queriers = lax.axis_size("query")
    q_rank = lax.axis_index("query")
    tok_rows = inputs.reshape(inputs.shape[1], inputs.shape[2])
    tokens, width = tok_rows.shape[0], w_out.shape[1]
    share = tokens // parts
    chunks = max(1, min(CHUNKS, share // 16))
    rows = share // chunks
    by_share = tok_rows.reshape(parts, chunks, rows, tok_rows.shape[1])
    half = width // HALVES

    partial_in = project_rows(tok_rows, proj_in)
    in_rows = lax.psum_scatter(
        partial_in.astype(jnp.bfloat16), "tensor", scatter_dimension=0, tiled=True
    ).astype(jnp.float32)

    grads, outs = [], []
    for c in range(chunks):
        here = by_share[:, c].reshape(parts * rows, -1)
        sums = []
        for h in range(HALVES):
            cols = w_out[:, h * half : (h + 1) * half]
            part = jnp.dot(here, cols, preferred_element_type=jnp.float32).astype(jnp.bfloat16)
            sums.append(reduce_line(part.reshape(parts, rows, half), rank, parts))
        proj_rows = jnp.concatenate(sums, axis=1)
        own = slice(c * rows, (c + 1) * rows)
        dproj_rows = norm_backward(proj_rows, residual[0, own], out_grad[0, own], norm_gain)
        grads.append(dproj_rows)
        halves = [
            gather_line(dproj_rows[:, h * half : (h + 1) * half], rank, parts) for h in range(HALVES)
        ]
        ordered = []
        for h in range(HALVES):
            stack = jnp.zeros((parts, rows, half), jnp.bfloat16)
            for far in range(parts):
                stack = lax.dynamic_update_index_in_dim(
                    stack, halves[h][far], (rank - far + parts) % parts, 0
                )
            ordered.append(stack.reshape(parts * rows, half))
        total = None
        for h in range(HALVES):
            term = project_rows(ordered[h], w_out[:, h * half : (h + 1) * half])
            total = term if total is None else total + term
        outs.append(total.astype(jnp.bfloat16).reshape(parts, 1, rows, -1))
    input_grad = jnp.concatenate(outs, axis=1).reshape(1, tokens, -1)

    dproj_own = jnp.concatenate(grads, axis=0)
    out_rows = project_rows(dproj_own, proj_out)
    kp = out_rows.shape[1]
    segs = lax.dynamic_slice_in_dim(segment_ids[0], rank * share, share, 0)
    member = (segs[None, :] == jnp.arange(EX_DEV, dtype=jnp.int32)[:, None]).astype(jnp.float32)
    weighted = member[:, :, None] * out_rows[None]
    sketch_part = lax.dot_general(
        weighted,
        jnp.broadcast_to(in_rows[None], (EX_DEV,) + in_rows.shape),
        (((1,), (1,)), ((0,), (0,))),
        precision=lax.Precision.HIGHEST,
    )
    sketch_part = sketch_part.reshape(EX_DEV, parts, kp * kp // parts).astype(jnp.bfloat16)
    got = exchange(
        lambda at: lax.dynamic_index_in_dim(sketch_part, at, 1, keepdims=False), "tensor", parts, rank
    )
    sketch_cols = jnp.sum(got.astype(jnp.float32), axis=0)
    paired = exchange(lambda at: sketch_cols, "query", queriers, q_rank)
    paired = paired.reshape(queriers * EX_DEV, sketch_cols.shape[1])
    score_part = lax.dot_general(
        paired,
        queries.astype(jnp.float32),
        (((1,), (1,)), ((), ())),
        precision=lax.Precision.HIGHEST,
    )
    scores = jnp.sum(exchange(lambda at: score_part, "tensor", parts, rank), axis=0)
    return (input_grad, scores)


def solution(mesh):
    return jax.shard_map(
        body,
        mesh=mesh,
        in_specs=(
            P(("groups", "dp", "query"), None, "tensor"),
            P(("groups", "dp", "query"), "tensor", None),
            P(("groups", "dp", "query"), "tensor", None),
            P(),
            P("tensor", None),
            P(None, "tensor"),
            P(),
            P("query", "tensor"),
            P(("groups", "dp", "query"), None),
        ),
        out_specs=(P(("groups", "dp", "query"), None, "tensor"), P(("groups", "dp"), "query")),
        check_vma=False,
    )
```

time: 414 us -> 657 us (1.59)
  the two profiles are of different devices: /device:TPU:0 before, /device:TPU:8 now
where the time goes in v1:
time: 657 us; the launch traced here: 648 us
  starting transfers between devices  247 us (38%)
  matrix products  167 us (25%)
  waiting for transfers between devices  136 us (21%)
  other arithmetic  55.4 us (8%)
  local copies, waits for them, and re-layouts  25.9 us (4%)
  between operations  16.4 us (2%)
    ppermute x96, starting transfers between devices, hop(): return lax.ppermute(value, 'tensor', pairs)  226 us
    ppermute x96, waiting for transfers between devices, hop(): return lax.ppermute(value, 'tensor', pairs)  127 us
    dot_general x10, matrix products, project_rows(): lax.dot_general(values, matrix, (((1,), (1,)), ((), ())), preferred_eleme...  98.5 us
    dot_general x8, matrix products, body(): jnp.dot(here, cols, preferred_element_type=jnp.float32).astype(jnp.bfloat16)  66.9 us
    dynamic_update_slice x24, other arithmetic, body(): lax.dynamic_update_index_in_dim(stack, halves[h][far], (rank - far + part...  35.7 us
    ppermute x7, starting transfers between devices, exchange(): lax.ppermute(value_of((rank + shift) % size), axis, [(d, (d + shift) % si...  20.6 us
    convert_element_type x16, other arithmetic, reduce_line(): (out_right.astype(jnp.float32) + right.astype(jnp.float32)).astype(jnp.bf...  14.3 us
  transfers between devices with their start and end apart: 104, of which 31 were waited for; matrix products, arithmetic and copies ran while one was open for 33% of the time, Pallas kernels for 0%

profile of v1, /device:TPU:8, one launch (start us, length us, event | category | flops | bytes accessed | tf_op | source)
XLA Modules:
  0.0 647.6 jit_solution(16665551874220144513)
XLA Ops:
  9.0 8.3 %convolution_convert_fusion.5 = bf16[128,4096]{1,0:T(8,128)(2,1)S(1)} fusion(bf16[128,2048]{1,0:T(8,128)(2,1)S(1)} %bitcast.409, bf16[2048,8192]{1,0:T(8,128)(2,1)} %param.13), kind=kOutput, calls=%fused_computation.5 | convolution fusion | flops 2148007936 | bytes 18350080 | tf_op jit(solution)/shard_map/dot_general | solution.py:97
  21.0 8.1 %convolution_convert_fusion.4 = bf16[128,4096]{1,0:T(8,128)(2,1)S(1)} fusion(bf16[128,2048]{1,0:T(8,128)(2,1)S(1)} %bitcast.410, bf16[2048,8192]{1,0:T(8,128)(2,1)} %param.13), kind=kOutput, calls=%fused_computation.4 | convolution fusion | flops 2148007936 | bytes 18350080 | tf_op jit(solution)/shard_map/dot_general | solution.py:97
  32.7 8.3 %convolution_convert_fusion.3 = bf16[128,4096]{1,0:T(8,128)(2,1)S(1)} fusion(bf16[128,2048]{1,0:T(8,128)(2,1)S(1)} %bitcast.407, bf16[2048,8192]{1,0:T(8,128)(2,1)} %param.13), kind=kOutput, calls=%fused_computation.3 | convolution fusion | flops 2148007936 | bytes 18350080 | tf_op jit(solution)/shard_map/dot_general | solution.py:97
  45.9 8.1 %convolution_convert_fusion.2 = bf16[128,4096]{1,0:T(8,128)(2,1)S(1)} fusion(bf16[128,2048]{1,0:T(8,128)(2,1)S(1)} %bitcast.408, bf16[2048,8192]{1,0:T(8,128)(2,1)} %param.13), kind=kOutput, calls=%fused_computation.2 | convolution fusion | flops 2148007936 | bytes 18350080 | tf_op jit(solution)/shard_map/dot_general | solution.py:97
  54.0 8.5 %convolution_convert_fusion.1 = bf16[128,4096]{1,0:T(8,128)(2,1)S(1)} fusion(bf16[128,2048]{1,0:T(8,128)(2,1)S(1)} %bitcast.404, bf16[2048,8192]{1,0:T(8,128)(2,1)} %param.13), kind=kOutput, calls=%fused_computation.1 | convolution fusion | flops 2148007936 | bytes 18350080 | tf_op jit(solution)/shard_map/dot_general | solution.py:97
  62.6 8.5 %convolution_convert_fusion = bf16[128,4096]{1,0:T(8,128)(2,1)S(1)} fusion(bf16[128,2048]{1,0:T(8,128)(2,1)S(1)} %bitcast.405, bf16[2048,8192]{1,0:T(8,128)(2,1)} %param.13), kind=kOutput, calls=%fused_computation | convolution fusion | flops 2148007936 | bytes 18350080 | tf_op jit(solution)/shard_map/dot_general | solution.py:97
  71.1 8.5 %convolution_convert_fusion.7 = bf16[128,4096]{1,0:T(8,128)(2,1)S(1)} fusion(bf16[128,2048]{1,0:T(8,128)(2,1)S(1)} %bitcast.402, bf16[2048,8192]{1,0:T(8,128)(2,1)} %param.13), kind=kOutput, calls=%fused_computation.7 | convolution fusion | flops 2148007936 | bytes 18350080 | tf_op jit(solution)/shard_map/dot_general | solution.py:97
  79.6 8.5 %convolution_convert_fusion.6 = bf16[128,4096]{1,0:T(8,128)(2,1)S(1)} fusion(bf16[128,2048]{1,0:T(8,128)(2,1)} %bitcast.403, bf16[2048,8192]{1,0:T(8,128)(2,1)} %param.13), kind=kOutput, calls=%fused_computation.6 | convolution fusion | flops 2148007936 | bytes 18350080 | tf_op jit(solution)/shard_map/dot_general | solution.py:97
  100.5 8.0 %collective-permute-done.54 = bf16[32,4096]{1,0:T(8,128)(2,1)S(1)} collective-permute-done((bf16[32,4096]{1,0:T(8,128)(2,1)}, bf16[32,4096]{1,0:T(8,128)(2,1)S(1)}, u32[]{:S(2)}, u32[]{:S(2)}) %collective-permute-start.54) | collective-permute-done | bytes 262176 | tf_op jit(solution)/shard_map/ppermute | solution.py:27
  110.8 6.9 %collective-permute-done.72 = bf16[32,4096]{1,0:T(8,128)(2,1)S(1)} collective-permute-done((bf16[32,4096]{1,0:T(8,128)(2,1)}, bf16[32,4096]{1,0:T(8,128)(2,1)S(1)}, u32[]{:S(2)}, u32[]{:S(2)}) %collective-permute-start.72) | collective-permute-done | bytes 262176 | tf_op jit(solution)/shard_map/ppermute | solution.py:27
  136.0 8.0 %collective-permute-done.6 = bf16[32,4096]{1,0:T(8,128)(2,1)S(1)} collective-permute-done((bf16[32,4096]{1,0:T(8,128)(2,1)}, bf16[32,4096]{1,0:T(8,128)(2,1)S(1)}, u32[]{:S(2)}, u32[]{:S(2)}) %collective-permute-start.6) | collective-permute-done | bytes 262176 | tf_op jit(solution)/shard_map/ppermute | solution.py:27
  146.7 7.7 %collective-permute-done.25 = bf16[32,4096]{1,0:T(8,128)(2,1)S(1)} collective-permute-done((bf16[32,4096]{1,0:T(8,128)(2,1)S(1)}, bf16[32,4096]{1,0:T(8,128)(2,1)S(1)}, u32[]{:S(2)}, u32[]{:S(2)}) %collective-permute-start.25) | collective-permute-done | bytes 262176 | tf_op jit(solution)/shard_map/ppermute | solution.py:27
  232.4 7.2 %collective-permute-done.76 = bf16[32,4096]{1,0:T(8,128)(2,1)S(1)} collective-permute-done((bf16[32,4096]{1,0:T(8,128)(2,1)S(1)}, bf16[32,4096]{1,0:T(8,128)(2,1)S(1)}, u32[]{:S(2)}, u32[]{:S(2)}) %collective-permute-start.76) | collective-permute-done | bytes 262176 | tf_op jit(solution)/shard_map/ppermute | solution.py:27
  275.2 7.4 %collective-permute-start.80 = (bf16[32,4096]{1,0:T(8,128)(2,1)S(1)}, bf16[32,4096]{1,0:T(8,128)(2,1)S(1)}, u32[]{:S(2)}, u32[]{:S(2)}) collective-permute-start(bf16[32,4096]{1,0:T(8,128)(2,1)S(1)} %get-tuple-element.37), channel_id=1, source_target_pairs={{0,4},{4,8},{8,12},{1,5},{5,9},{9,13},{2,6},{6,10},{10,14},{3,7},{... | collective-permute-start | bytes 786440 | tf_op jit(solution)/shard_map/ppermute | solution.py:27
  304.1 7.0 %collective-permute-start.83 = (bf16[32,4096]{1,0:T(8,128)(2,1)S(1)}, bf16[32,4096]{1,0:T(8,128)(2,1)S(1)}, u32[]{:S(2)}, u32[]{:S(2)}) collective-permute-start(bf16[32,4096]{1,0:T(8,128)(2,1)S(1)} %fusion.82), channel_id=1, source_target_pairs={{4,0},{8,4},{12,8},{5,1},{9,5},{13,9},{6,2},{10,6},{14,10},{7,3},{... | collective-permute-start | bytes 786440 | tf_op jit(solution)/shard_map/ppermute | solution.py:27
  369.4 7.3 %collective-permute-start.99 = (f32[4,1024]{1,0:T(4,128)S(1)}, f32[4,1024]{1,0:T(4,128)S(1)}, u32[]{:S(2)}, u32[]{:S(2)}) collective-permute-start(f32[4,1024]{1,0:T(4,128)S(1)} %convert_reduce_fusion), channel_id=1, source_target_pairs={{0,1},{1,0},{2,3},{3,2},{4,5},{5,4},{6,7},{7,6},{8,9},{9,8},{10,11... | collective-permute-start | bytes 49160 | tf_op jit(solution)/shard_map/ppermute | solution.py:66
  422.2 12.7 %fusion.9 = f32[128,2048]{1,0:T(8,128)} fusion(bf16[128,4096]{1,0:T(8,128)(2,1)} %bitcast.396, bf16[2048,8192]{1,0:T(8,128)(2,1)} %param.13), kind=kOutput, calls=%fused_computation.17 | convolution fusion | flops 2147483648 | bytes 18874368 | tf_op jit(solution)/shard_map/dot_general | solution.py:21
  455.2 11.9 %fusion.45 = bf16[128,2048]{1,0:T(8,128)(2,1)S(1)} fusion(f32[128,2048]{1,0:T(8,128)} %fusion.9, bf16[128,4096]{1,0:T(8,128)(2,1)} %bitcast.24, bf16[2048,8192]{1,0:T(8,128)(2,1)} %param.13), kind=kOutput, calls=%fused_computation.39 | convolution fusion | flops 2148007936 | bytes 19398656 | tf_op jit(solution)/shard_map/dot_general | solution.py:21
  487.5 12.7 %fusion.6 = f32[128,2048]{1,0:T(8,128)} fusion(bf16[128,4096]{1,0:T(8,128)(2,1)} %bitcast.397, bf16[2048,8192]{1,0:T(8,128)(2,1)} %param.13), kind=kOutput, calls=%fused_computation.14 | convolution fusion | flops 2147483648 | bytes 18874368 | tf_op jit(solution)/shard_map/dot_general | solution.py:21
  520.5 12.0 %fusion.42 = bf16[128,2048]{1,0:T(8,128)(2,1)S(1)} fusion(f32[128,2048]{1,0:T(8,128)} %fusion.6, bf16[128,4096]{1,0:T(8,128)(2,1)} %bitcast.54, bf16[2048,8192]{1,0:T(8,128)(2,1)} %param.13), kind=kOutput, calls=%fused_computation.38 | convolution fusion | flops 2148007936 | bytes 19398656 | tf_op jit(solution)/shard_map/dot_general | solution.py:21
  570.7 12.7 %fusion.3 = f32[128,2048]{1,0:T(8,128)} fusion(bf16[128,4096]{1,0:T(8,128)(2,1)} %bitcast.398, bf16[2048,8192]{1,0:T(8,128)(2,1)} %param.13), kind=kOutput, calls=%fused_computation.11 | convolution fusion | flops 2147483648 | bytes 18874368 | tf_op jit(solution)/shard_map/dot_general | solution.py:21
  595.3 12.7 %fusion.39 = bf16[128,2048]{1,0:T(8,128)(2,1)} fusion(f32[128,2048]{1,0:T(8,128)} %fusion.3, bf16[128,4096]{1,0:T(8,128)(2,1)} %bitcast.84, bf16[2048,8192]{1,0:T(8,128)(2,1)} %param.13), kind=kOutput, calls=%fused_computation.37 | convolution fusion | flops 2148007936 | bytes 19398656 | tf_op jit(solution)/shard_map/dot_general | solution.py:21
  611.2 10.1 %fusion = f32[128,2048]{1,0:T(8,128)} fusion(bf16[128,4096]{1,0:T(8,128)(2,1)S(1)} %bitcast.395, bf16[2048,8192]{1,0:T(8,128)(2,1)} %param.13), kind=kOutput, calls=%fused_computation.8 | convolution fusion | flops 2147483648 | bytes 18874368 | tf_op jit(solution)/shard_map/dot_general | solution.py:21
  626.6 12.0 %fusion.36 = bf16[128,2048]{1,0:T(8,128)(2,1)S(1)} fusion(f32[128,2048]{1,0:T(8,128)} %fusion, bf16[128,4096]{1,0:T(8,128)(2,1)} %bitcast.399, bf16[2048,8192]{1,0:T(8,128)(2,1)} %param.13), kind=kOutput, calls=%fused_computation.36 | convolution fusion | flops 2148007936 | bytes 19398656 | tf_op jit(solution)/shard_map/dot_general | solution.py:21
  (380 shorter events, 408.0 us)
Async XLA Ops:
  7.2 85.8 %reduce-scatter.4.cloned.1.call-start = ((), (), s32[]{:S(2)}) async-start(), calls=%async_computation.1 | async-start | bytes 163840
  18.3 75.6 %collective-permute-start.24 = (bf16[32,4096]{1,0:T(8,128)(2,1)}, bf16[32,4096]{1,0:T(8,128)(2,1)}, u32[]{:S(2)}, u32[]{:S(2)}) collective-permute-start(bf16[32,4096]{1,0:T(8,128)(2,1)} %get-tuple-element.19), channel_id=1, source_target_pairs={{0,4},{1,5},{2,6},{3,7},{16,20},{17,21},{18,22},{19,23}} | collective-permute-start | bytes 786440 | tf_op jit(solution)/shard_map/ppermute | solution.py:27
  19.6 126.4 %collective-permute-start.27 = (bf16[32,4096]{1,0:T(8,128)(2,1)}, bf16[32,4096]{1,0:T(8,128)(2,1)}, u32[]{:S(2)}, u32[]{:S(2)}) collective-permute-start(bf16[32,4096]{1,0:T(8,128)(2,1)} %get-tuple-element.20), channel_id=1, source_target_pairs={{12,8},{13,9},{14,10},{15,11},{28,24},{29,25},{30,26},{31,27}} | collective-permute-start | bytes 786440 | tf_op jit(solution)/shard_map/ppermute | solution.py:27
  30.1 66.2 %collective-permute-start.30 = (bf16[32,4096]{1,0:T(8,128)(2,1)}, bf16[32,4096]{1,0:T(8,128)(2,1)}, u32[]{:S(2)}, u32[]{:S(2)}) collective-permute-start(bf16[32,4096]{1,0:T(8,128)(2,1)} %get-tuple-element.23), channel_id=1, source_target_pairs={{0,4},{1,5},{2,6},{3,7},{16,20},{17,21},{18,22},{19,23}} | collective-permute-start | bytes 786440 | tf_op jit(solution)/shard_map/ppermute | solution.py:27
  31.4 126.1 %collective-permute-start.33 = (bf16[32,4096]{1,0:T(8,128)(2,1)}, bf16[32,4096]{1,0:T(8,128)(2,1)}, u32[]{:S(2)}, u32[]{:S(2)}) collective-permute-start(bf16[32,4096]{1,0:T(8,128)(2,1)} %get-tuple-element.24), channel_id=1, source_target_pairs={{12,8},{13,9},{14,10},{15,11},{28,24},{29,25},{30,26},{31,27}} | collective-permute-start | bytes 786440 | tf_op jit(solution)/shard_map/ppermute | solution.py:27
  42.9 55.8 %collective-permute-start.48 = (bf16[32,4096]{1,0:T(8,128)(2,1)}, bf16[32,4096]{1,0:T(8,128)(2,1)}, u32[]{:S(2)}, u32[]{:S(2)}) collective-permute-start(bf16[32,4096]{1,0:T(8,128)(2,1)} %get-tuple-element.27), channel_id=1, source_target_pairs={{0,4},{1,5},{2,6},{3,7},{16,20},{17,21},{18,22},{19,23}} | collective-permute-start | bytes 786440 | tf_op jit(solution)/shard_map/ppermute | solution.py:27
  93.9 74.5 %collective-permute-start.51 = (bf16[32,4096]{1,0:T(8,128)(2,1)}, bf16[32,4096]{1,0:T(8,128)(2,1)S(1)}, u32[]{:S(2)}, u32[]{:S(2)}) collective-permute-start(bf16[32,4096]{1,0:T(8,128)(2,1)} %get-tuple-element.28), channel_id=1, source_target_pairs={{12,8},{13,9},{14,10},{15,11},{28,24},{29,25},{30,26},{31,27}} | collective-permute-start | bytes 786440 | tf_op jit(solution)/shard_map/ppermute | solution.py:27
  98.7 79.7 %collective-permute-start.57 = (bf16[32,4096]{1,0:T(8,128)(2,1)}, bf16[32,4096]{1,0:T(8,128)(2,1)S(1)}, u32[]{:S(2)}, u32[]{:S(2)}) collective-permute-start(bf16[32,4096]{1,0:T(8,128)(2,1)} %get-tuple-element.32), channel_id=1, source_target_pairs={{12,8},{13,9},{14,10},{15,11},{28,24},{29,25},{30,26},{31,27}} | collective-permute-start | bytes 786440 | tf_op jit(solution)/shard_map/ppermute | solution.py:27
  146.0 43.5 %collective-permute-start.75 = (bf16[32,4096]{1,0:T(8,128)(2,1)}, bf16[32,4096]{1,0:T(8,128)(2,1)S(1)}, u32[]{:S(2)}, u32[]{:S(2)}) collective-permute-start(bf16[32,4096]{1,0:T(8,128)(2,1)} %get-tuple-element.36), channel_id=1, source_target_pairs={{12,8},{13,9},{14,10},{15,11},{28,24},{29,25},{30,26},{31,27}} | collective-permute-start | bytes 786440 | tf_op jit(solution)/shard_map/ppermute | solution.py:27
  157.5 42.3 %collective-permute-start.81 = (bf16[32,4096]{1,0:T(8,128)(2,1)}, bf16[32,4096]{1,0:T(8,128)(2,1)S(1)}, u32[]{:S(2)}, u32[]{:S(2)}) collective-permute-start(bf16[32,4096]{1,0:T(8,128)(2,1)} %get-tuple-element.40), channel_id=1, source_target_pairs={{12,8},{13,9},{14,10},{15,11},{28,24},{29,25},{30,26},{31,27}} | collective-permute-start | bytes 786440 | tf_op jit(solution)/shard_map/ppermute | solution.py:27
  204.8 61.6 %collective-permute-start.26 = (bf16[32,4096]{1,0:T(8,128)(2,1)S(1)}, bf16[32,4096]{1,0:T(8,128)(2,1)S(1)}, u32[]{:S(2)}, u32[]{:S(2)}) collective-permute-start(bf16[32,4096]{1,0:T(8,128)(2,1)S(1)} %get-tuple-element.17), channel_id=1, source_target_pairs={{0,4},{4,8},{8,12},{1,5},{5,9},{9,13},{2,6},{6,10},{10,14},{3,7},{... | collective-permute-start | bytes 786440 | tf_op jit(solution)/shard_map/ppermute | solution.py:27
  210.8 64.4 %collective-permute-start.32 = (bf16[32,4096]{1,0:T(8,128)(2,1)S(1)}, bf16[32,4096]{1,0:T(8,128)(2,1)S(1)}, u32[]{:S(2)}, u32[]{:S(2)}) collective-permute-start(bf16[32,4096]{1,0:T(8,128)(2,1)S(1)} %get-tuple-element.21), channel_id=1, source_target_pairs={{0,4},{4,8},{8,12},{1,5},{5,9},{9,13},{2,6},{6,10},{10,14},{3,7},{... | collective-permute-start | bytes 786440 | tf_op jit(solution)/shard_map/ppermute | solution.py:27
  216.8 68.8 %collective-permute-start.50 = (bf16[32,4096]{1,0:T(8,128)(2,1)S(1)}, bf16[32,4096]{1,0:T(8,128)(2,1)S(1)}, u32[]{:S(2)}, u32[]{:S(2)}) collective-permute-start(bf16[32,4096]{1,0:T(8,128)(2,1)S(1)} %get-tuple-element.25), channel_id=1, source_target_pairs={{0,4},{4,8},{8,12},{1,5},{5,9},{9,13},{2,6},{6,10},{10,14},{3,7},{... | collective-permute-start | bytes 786440 | tf_op jit(solution)/shard_map/ppermute | solution.py:27
  223.7 71.7 %collective-permute-start.56 = (bf16[32,4096]{1,0:T(8,128)(2,1)S(1)}, bf16[32,4096]{1,0:T(8,128)(2,1)S(1)}, u32[]{:S(2)}, u32[]{:S(2)}) collective-permute-start(bf16[32,4096]{1,0:T(8,128)(2,1)S(1)} %get-tuple-element.29), channel_id=1, source_target_pairs={{0,4},{4,8},{8,12},{1,5},{5,9},{9,13},{2,6},{6,10},{10,14},{3,7},{... | collective-permute-start | bytes 786440 | tf_op jit(solution)/shard_map/ppermute | solution.py:27
  275.2 37.9 %collective-permute-start.80 = (bf16[32,4096]{1,0:T(8,128)(2,1)S(1)}, bf16[32,4096]{1,0:T(8,128)(2,1)S(1)}, u32[]{:S(2)}, u32[]{:S(2)}) collective-permute-start(bf16[32,4096]{1,0:T(8,128)(2,1)S(1)} %get-tuple-element.37), channel_id=1, source_target_pairs={{0,4},{4,8},{8,12},{1,5},{5,9},{9,13},{2,6},{6,10},{10,14},{3,7},{... | collective-permute-start | bytes 786440 | tf_op jit(solution)/shard_map/ppermute | solution.py:27
  334.2 64.8 %collective-permute-start.13 = (bf16[32,4096]{1,0:T(8,128)(2,1)}, bf16[32,4096]{1,0:T(8,128)(2,1)S(1)}, u32[]{:S(2)}, u32[]{:S(2)}) collective-permute-start(bf16[32,4096]{1,0:T(8,128)(2,1)} %get-tuple-element.49), channel_id=1, source_target_pairs={{4,0},{8,4},{12,8},{5,1},{9,5},{13,9},{6,2},{10,6},{14,10},{7,3},{... | collective-permute-start | bytes 786440 | tf_op jit(solution)/shard_map/ppermute | solution.py:27
  336.7 73.0 %collective-permute-start.12 = (bf16[32,4096]{1,0:T(8,128)(2,1)}, bf16[32,4096]{1,0:T(8,128)(2,1)}, u32[]{:S(2)}, u32[]{:S(2)}) collective-permute-start(bf16[32,4096]{1,0:T(8,128)(2,1)} %get-tuple-element.49), channel_id=1, source_target_pairs={{0,4},{4,8},{8,12},{1,5},{5,9},{9,13},{2,6},{6,10},{10,14},{3,7},{... | collective-permute-start | bytes 786440 | tf_op jit(solution)/shard_map/ppermute | solution.py:27
  340.0 39.9 %collective-permute-start.19 = (bf16[32,4096]{1,0:T(8,128)(2,1)}, bf16[32,4096]{1,0:T(8,128)(2,1)}, u32[]{:S(2)}, u32[]{:S(2)}) collective-permute-start(bf16[32,4096]{1,0:T(8,128)(2,1)} %get-tuple-element.50), channel_id=1, source_target_pairs={{4,0},{8,4},{12,8},{5,1},{9,5},{13,9},{6,2},{10,6},{14,10},{7,3},{... | collective-permute-start | bytes 786440 | tf_op jit(solution)/shard_map/ppermute | solution.py:27
  343.2 49.5 %collective-permute-start.18 = (bf16[32,4096]{1,0:T(8,128)(2,1)}, bf16[32,4096]{1,0:T(8,128)(2,1)}, u32[]{:S(2)}, u32[]{:S(2)}) collective-permute-start(bf16[32,4096]{1,0:T(8,128)(2,1)} %get-tuple-element.50), channel_id=1, source_target_pairs={{0,4},{4,8},{8,12},{1,5},{5,9},{9,13},{2,6},{6,10},{10,14},{3,7},{... | collective-permute-start | bytes 786440 | tf_op jit(solution)/shard_map/ppermute | solution.py:27
  396.0 71.1 %collective-permute-start.37 = (bf16[32,4096]{1,0:T(8,128)(2,1)}, bf16[32,4096]{1,0:T(8,128)(2,1)S(1)}, u32[]{:S(2)}, u32[]{:S(2)}) collective-permute-start(bf16[32,4096]{1,0:T(8,128)(2,1)} %get-tuple-element.51), channel_id=1, source_target_pairs={{4,0},{8,4},{12,8},{5,1},{9,5},{13,9},{6,2},{10,6},{14,10},{7,3},{... | collective-permute-start | bytes 786440 | tf_op jit(solution)/shard_map/ppermute | solution.py:27
  399.0 78.2 %collective-permute-start.36 = (bf16[32,4096]{1,0:T(8,128)(2,1)}, bf16[32,4096]{1,0:T(8,128)(2,1)}, u32[]{:S(2)}, u32[]{:S(2)}) collective-permute-start(bf16[32,4096]{1,0:T(8,128)(2,1)} %get-tuple-element.51), channel_id=1, source_target_pairs={{0,4},{4,8},{8,12},{1,5},{5,9},{9,13},{2,6},{6,10},{10,14},{3,7},{... | collective-permute-start | bytes 786440 | tf_op jit(solution)/shard_map/ppermute | solution.py:27
  444.7 94.6 %collective-permute-start.61 = (bf16[32,4096]{1,0:T(8,128)(2,1)}, bf16[32,4096]{1,0:T(8,128)(2,1)}, u32[]{:S(2)}, u32[]{:S(2)}) collective-permute-start(bf16[32,4096]{1,0:T(8,128)(2,1)} %get-tuple-element.53), channel_id=1, source_target_pairs={{4,0},{8,4},{12,8},{5,1},{9,5},{13,9},{6,2},{10,6},{14,10},{7,3},{... | collective-permute-start | bytes 786440 | tf_op jit(solution)/shard_map/ppermute | solution.py:27
  467.2 75.9 %collective-permute-start.60 = (bf16[32,4096]{1,0:T(8,128)(2,1)}, bf16[32,4096]{1,0:T(8,128)(2,1)S(1)}, u32[]{:S(2)}, u32[]{:S(2)}) collective-permute-start(bf16[32,4096]{1,0:T(8,128)(2,1)} %get-tuple-element.53), channel_id=1, source_target_pairs={{0,4},{4,8},{8,12},{1,5},{5,9},{9,13},{2,6},{6,10},{10,14},{3,7},{... | collective-permute-start | bytes 786440 | tf_op jit(solution)/shard_map/ppermute | solution.py:27
  586.1 38.8 %collective-permute-start.89 = (bf16[32,4096]{1,0:T(8,128)(2,1)}, bf16[32,4096]{1,0:T(8,128)(2,1)}, u32[]{:S(2)}, u32[]{:S(2)}) collective-permute-start(bf16[32,4096]{1,0:T(8,128)(2,1)} %collective-permute-done.88), channel_id=1, source_target_pairs={{8,12},{9,13},{10,14},{11,15},{24,28},{25,29},{26,30},{27,31}} | collective-permute-start | bytes 786440 | tf_op jit(solution)/shard_map/ppermute | solution.py:27
  (107 other events, 3121.2 us)
Sparse Core Ops, SparseCore 0:
  46.0 20.0 reduce-scatter.3

commit v2 on v1

v2 whole, which is shorter than its diff:
```python
import functools

import jax
import jax.numpy as jnp
from jax import lax
from jax.experimental import pallas as pl
from jax.experimental.pallas import tpu as pltpu
from jax.sharding import PartitionSpec as P

EX_DEV = 4
EPS = 1e-05
CHUNKS = 4
PIECES = 4
LIMIT = 48 * 1024 * 1024

F32, BF16 = jnp.float32, jnp.bfloat16
ANY = pl.BlockSpec(memory_space=pl.ANY)
TOKEN = jax.ShapeDtypeStruct((8, 128), F32)
TOKEN_SPEC = pl.BlockSpec((8, 128), lambda *_: (0, 0))


def divisor(total, wanted):
    size = min(total, wanted)
    while total % size:
        size //= 2
    return size


def cost(flops, moved):
    return pl.CostEstimate(flops=flops, bytes_accessed=moved, transcendentals=0)


def project_rows(values, matrix):
    return lax.dot_general(
        values, matrix, (((1,), (1,)), ((), ())), preferred_element_type=F32
    )


def forward_piece(by_share, w_out, chunk, piece, pieces, held, after):
    parts, _, rows, depth = by_share.shape
    width = w_out.shape[1]
    span = width // pieces
    cols = divisor(span, 512)
    steps = span // cols

    def kernel(x_ref, w_ref, *refs):
        out_ref, tok_ref = refs[-2:]
        x = x_ref[...].reshape(parts * rows, depth)
        y = jnp.dot(x, w_ref[...], preferred_element_type=F32).astype(BF16)
        out_ref[...] = y.reshape(parts, rows, cols)
        tok_ref[...] = jnp.zeros_like(tok_ref)

    extra = ([] if held is None else [held]) + after
    return pl.pallas_call(
        kernel,
        grid=(steps,),
        in_specs=[
            pl.BlockSpec((parts, None, rows, depth), lambda i: (0, chunk, 0, 0)),
            pl.BlockSpec((depth, cols), lambda i: (0, piece * steps + i)),
        ]
        + [ANY] * len(extra),
        out_specs=[pl.BlockSpec((parts, rows, cols), lambda i: (0, 0, piece * steps + i)), TOKEN_SPEC],
        out_shape=[jax.ShapeDtypeStruct((parts, rows, width), BF16), TOKEN],
        input_output_aliases={} if held is None else {2: 0},
        compiler_params=pltpu.CompilerParams(vmem_limit_bytes=LIMIT),
        cost_estimate=cost(2 * parts * rows * depth * span, 2 * depth * span),
        name="forward_piece",
    )(by_share, w_out, *extra)


def backward_piece(gathered, w_out, chunk, chunks, piece, pieces, held, after):
    parts, rows, width = gathered.shape
    depth = w_out.shape[0]
    span = depth // pieces
    cols = divisor(span, 256)
    steps = span // cols

    def kernel(g_ref, w_ref, *refs):
        out_ref, tok_ref = refs[-2:]
        g = g_ref[...].reshape(parts * rows, width)
        y = project_rows(g, w_ref[...]).astype(BF16)
        out_ref[...] = y.reshape(parts, rows, cols)
        tok_ref[...] = jnp.zeros_like(tok_ref)

    extra = ([] if held is None else [held]) + after
    return pl.pallas_call(
        kernel,
        grid=(steps,),
        in_specs=[
            pl.BlockSpec((parts, rows, width), lambda i: (0, 0, 0)),
            pl.BlockSpec((cols, width), lambda i: (piece * steps + i, 0)),
        ]
        + [ANY] * len(extra),
        out_specs=[
            pl.BlockSpec((parts, None, rows, cols), lambda i: (0, chunk, 0, piece * steps + i)),
            TOKEN_SPEC,
        ],
        out_shape=[jax.ShapeDtypeStruct((parts, chunks, rows, depth), BF16), TOKEN],
        input_output_aliases={} if held is None else {2: 0},
        compiler_params=pltpu.CompilerParams(vmem_limit_bytes=LIMIT),
        cost_estimate=cost(2 * parts * rows * width * span, 2 * width * span),
        name="backward_piece",
    )(gathered, w_out, *extra)


def add_term(where, partial, came, after):
    parts, rows, width = partial.shape
    cols = divisor(width, 4096)

    def kernel(where_ref, p_ref, *refs):
        out_ref = refs[-1]
        if came is None:
            out_ref[...] = p_ref[...]
            return
        came_ref = refs[0]

        @pl.when(where_ref[1] == 1)
        def _():
            out_ref[...] = (came_ref[...].astype(F32) + p_ref[...].astype(F32)).astype(BF16)

        @pl.when(where_ref[1] == 0)
        def _():
            out_ref[...] = came_ref[...]

    line = pl.BlockSpec((rows, cols), lambda i, w: (0, i))
    first = [] if came is None else [came]
    return pl.pallas_call(
        kernel,
        grid_spec=pltpu.PrefetchScalarGridSpec(
            num_scalar_prefetch=1,
            grid=(width // cols,),
            in_specs=[pl.BlockSpec((None, rows, cols), lambda i, w: (w[0], 0, i))]
            + [line] * len(first)
            + [ANY] * len(after),
            out_specs=line,
        ),
        out_shape=jax.ShapeDtypeStruct((rows, width), BF16),
        compiler_params=pltpu.CompilerParams(vmem_limit_bytes=LIMIT),
        cost_estimate=cost(rows * width, 6 * rows * width),
        name="add_term",
    )(where, partial, *first, *after)


def norm_backward(rank, partial, from_a, from_b, residual, out_grad, norm_gain, chunk, after):
    parts, rows, width = partial.shape
    cols = divisor(width, 1024)
    count = width // cols

    def kernel(rank_ref, p_ref, a_ref, b_ref, res_ref, grad_ref, gain_ref, *refs):
        out_ref, z_ref, s_ref = refs[-3:]

        def first(i, sums):
            at = pl.ds(pl.multiple_of(i * cols, cols), cols)
            proj = p_ref[:, at].astype(F32) + a_ref[:, at].astype(F32) + b_ref[:, at].astype(F32)
            z = res_ref[:, at].astype(F32) + proj
            scaled = gain_ref[:, at].astype(F32) * grad_ref[:, at].astype(F32)
            z_ref[:, at] = z
            s_ref[:, at] = scaled
            square, cross = sums
            for j in range(0, cols, 128):
                zj = z[:, j : j + 128]
                square = square + zj * zj
                cross = cross + zj * scaled[:, j : j + 128]
            return square, cross

        zero = jnp.zeros((rows, 128), F32)
        square, cross = lax.fori_loop(0, count, first, (zero, zero))
        inv = lax.rsqrt(jnp.sum(square, axis=-1, keepdims=True) / width + EPS)
        center = jnp.sum(cross, axis=-1, keepdims=True) / width
        slope = inv * inv * inv * center

        def second(i, carry):
            at = pl.ds(pl.multiple_of(i * cols, cols), cols)
            out_ref[:, at] = (inv * s_ref[:, at] - z_ref[:, at] * slope).astype(BF16)
            return carry

        lax.fori_loop(0, count, second, 0)

    whole = pl.BlockSpec((rows, width), lambda i, r: (0, 0))
    own = pl.BlockSpec((None, rows, width), lambda i, r: (0, chunk, 0))
    return pl.pallas_call(
        kernel,
        grid_spec=pltpu.PrefetchScalarGridSpec(
            num_scalar_prefetch=1,
            grid=(1,),
            in_specs=[
                pl.BlockSpec((None, rows, width), lambda i, r: (r[0], 0, 0)),
                whole,
                whole,
                own,
                own,
                pl.BlockSpec((1, width), lambda i, r: (0, 0)),
            ]
            + [ANY] * len(after),
            out_specs=whole,
            scratch_shapes=[pltpu.VMEM((rows, width), F32), pltpu.VMEM((rows, width), F32)],
        ),
        out_shape=jax.ShapeDtypeStruct((rows, width), BF16),
        compiler_params=pltpu.CompilerParams(vmem_limit_bytes=LIMIT),
        cost_estimate=cost(20 * rows * width, 12 * rows * width),
        name="norm_backward",
    )(rank, partial, from_a, from_b, residual, out_grad, norm_gain, *after)


def put_in_order(place, own, from_a, from_b):
    rows, width = own.shape
    parts = len(from_a) + 1

    def kernel(place_ref, *refs):
        own_ref, a_refs, b_refs = refs[0], refs[1:parts], refs[parts : 2 * parts - 1]
        out_ref, sems = refs[-2:]
        rank, way, behind = place_ref[0], place_ref[1], place_ref[2]
        copies = [(None, pltpu.make_async_copy(own_ref, out_ref.at[rank], sems.at[0]))]
        for j in range(1, parts):
            low = lax.clamp(0, rank - way * j, parts - 1)
            high = lax.clamp(0, rank + way * j, parts - 1)
            copies.append(
                (j <= behind, pltpu.make_async_copy(a_refs[j - 1], out_ref.at[low], sems.at[j]))
            )
            copies.append(
                (
                    j <= parts - 1 - behind,
                    pltpu.make_async_copy(b_refs[j - 1], out_ref.at[high], sems.at[parts - 1 + j]),
                )
            )
        for phase in ("start", "wait"):
            for test, copy in copies:
                if test is None:
                    getattr(copy, phase)()
                else:
                    pl.when(test)(getattr(copy, phase))

    return pl.pallas_call(
        kernel,
        grid_spec=pltpu.PrefetchScalarGridSpec(
            num_scalar_prefetch=1,
            grid=(1,),
            in_specs=[ANY] * (2 * parts - 1),
            out_specs=ANY,
            scratch_shapes=[pltpu.SemaphoreType.DMA((2 * parts - 1,))],
        ),
        out_shape=jax.ShapeDtypeStruct((parts, rows, width), BF16),
        compiler_params=pltpu.CompilerParams(vmem_limit_bytes=LIMIT),
        cost_estimate=cost(0, 4 * parts * rows * width),
        name="put_in_order",
    )(place, own, *from_a, *from_b)


def exchange(value_of, axis, size, rank):
    first = value_of(rank)
    out = jnp.zeros((size,) + first.shape, first.dtype)
    out = lax.dynamic_update_index_in_dim(out, first, rank, 0)
    for shift in range(1, size):
        got = lax.ppermute(
            value_of((rank + shift) % size), axis, [(d, (d + shift) % size) for d in range(size)]
        )
        out = lax.dynamic_update_index_in_dim(out, got, (rank - shift + size) % size, 0)
    return out


def body(inputs, residual, out_grad, norm_gain, w_out, proj_in, proj_out, queries, segment_ids):
    parts = lax.axis_size("tensor")
    rank = lax.axis_index("tensor")
    queriers = lax.axis_size("query")
    q_rank = lax.axis_index("query")
    tokens = inputs.shape[1]
    share = tokens // parts
    chunks = max(1, min(CHUNKS, share // 16))
    rows = share // chunks
    by_share = inputs.reshape(parts, chunks, rows, inputs.shape[2])
    gain = norm_gain.reshape(1, -1)

    partial_in = project_rows(inputs.reshape(tokens, -1), proj_in)
    in_rows = lax.psum_scatter(
        partial_in.astype(BF16), "tensor", scatter_dimension=0, tiled=True
    ).astype(F32)

    up = 1 - 2 * (q_rank % 2)
    ways = (up, -up)
    spots = [jnp.where(way == 1, rank, parts - 1 - rank) for way in ways]
    rank_at = jnp.stack([rank]).astype(jnp.int32)
    place = jnp.stack([rank, ways[0], spots[0]]).astype(jnp.int32)

    def pairs(flow, low, high):
        out = []
        for q in range(queriers):
            way = 1 if (q % 2 == 0) == (flow == 0) else -1
            for t in range(parts):
                spot = t if way == 1 else parts - 1 - t
                if low <= spot <= min(high, parts - 2):
                    out.append((t * queriers + q, (t + way) * queriers + q))
        return out

    work, tokens_made = [], []
    partials = {}
    result = [None]

    def forward(chunk, piece, pieces, after):
        partials[chunk], tok = forward_piece(
            by_share, w_out, chunk, piece, pieces, partials.get(chunk), after
        )
        return tok

    def backward(chunk, gathered, piece, pieces, after):
        result[0], tok = backward_piece(
            gathered, w_out, chunk, chunks, piece, pieces, result[0], after
        )
        return tok

    def do_one(x):
        if work:
            tokens_made[:] = [work.pop(0)([x])]

    forward(0, 0, 1, [])
    for c in range(1, chunks):
        for piece in range(PIECES):
            work.append(functools.partial(forward, c, piece, PIECES))
    grads = []
    for slot in range(chunks + 1):
        rs = slot < chunks
        ag = slot > 0
        came = [None, None]
        gathered = [[], []]
        if rs:
            while slot not in partials or any(
                w.func is forward and w.args[0] <= slot for w in work
            ):
                tokens_made[:] = [work.pop(0)([])]
        for k in range(parts):
            gather_now = ag and k <= parts - 2
            reduce_now = rs and k >= 1
            if not gather_now and not reduce_now:
                continue
            for flow in range(2):
                if k == 0:
                    x = grads[slot - 1]
                elif reduce_now:
                    at = jnp.clip(rank + ways[flow] * (parts - k), 0, parts - 1)
                    adds = spots[flow] <= k - 1
                    x = add_term(
                        jnp.stack([at, adds.astype(at.dtype)]).astype(jnp.int32),
                        partials[slot],
                        came[flow],
                        list(tokens_made),
                    )
                else:
                    x = came[flow]
                low = 0 if reduce_now else k
                high = parts - 2 if gather_now else k - 1
                came[flow] = lax.ppermute(x, ("tensor", "query"), pairs(flow, low, high))
                if gather_now:
                    gathered[flow].append(came[flow])
                do_one(x)
        if rs:
            grads.append(
                norm_backward(
                    rank_at, partials[slot], *came, residual, out_grad, gain, slot, list(tokens_made)
                )
            )
        if ag:
            ready = put_in_order(place, grads[slot - 1], *gathered)
            if slot == chunks:
                while work:
                    work.pop(0)([])
                backward(slot - 1, ready, 0, 1, [])
            else:
                for piece in range(PIECES):
                    work.append(functools.partial(backward, slot - 1, ready, piece, PIECES))
    input_grad = result[0].reshape(1, tokens, -1)

    dproj_own = jnp.concatenate(grads, axis=0)
    out_rows = project_rows(dproj_own, proj_out)
    kp = out_rows.shape[1]
    segs = lax.dynamic_slice_in_dim(segment_ids[0], rank * share, share, 0)
    member = (segs[None, :] == jnp.arange(EX_DEV, dtype=jnp.int32)[:, None]).astype(F32)
    weighted = member[:, :, None] * out_rows[None]
    sketch_part = lax.dot_general(
        weighted,
        jnp.broadcast_to(in_rows[None], (EX_DEV,) + in_rows.shape),
        (((1,), (1,)), ((0,), (0,))),
        precision=lax.Precision.HIGHEST,
    )
    sketch_part = sketch_part.reshape(EX_DEV, parts, kp * kp // parts).astype(BF16)
    got = exchange(
        lambda at: lax.dynamic_index_in_dim(sketch_part, at, 1, keepdims=False), "tensor", parts, rank
    )
    sketch_cols = jnp.sum(got.astype(F32), axis=0)
    paired = exchange(lambda at: sketch_cols, "query", queriers, q_rank)
    paired = paired.reshape(queriers * EX_DEV, sketch_cols.shape[1])
    score_part = lax.dot_general(
        paired,
        queries.astype(F32),
        (((1,), (1,)), ((), ())),
        precision=lax.Precision.HIGHEST,
    )
    scores = jnp.sum(exchange(lambda at: score_part, "tensor", parts, rank), axis=0)
    return (input_grad, scores)


def solution(mesh):
    return jax.shard_map(
        body,
        mesh=mesh,
        in_specs=(
            P(("groups", "dp", "query"), None, "tensor"),
            P(("groups", "dp", "query"), "tensor", None),
            P(("groups", "dp", "query"), "tensor", None),
            P(),
            P("tensor", None),
            P(None, "tensor"),
            P(),
            P("query", "tensor"),
            P(("groups", "dp", "query"), None),
        ),
        out_specs=(P(("groups", "dp", "query"), None, "tensor"), P(("groups", "dp"), "query")),
        check_vma=False,
    )
```

time: 657 us -> 430 us (0.65)
  the two profiles are of different devices: /device:TPU:8 before, /device:TPU:0 now
where the time goes in v2:
time: 430 us; the launch traced here: 427 us
  Pallas kernels  208 us (48%)
  starting transfers between devices  105 us (24%)
  waiting for transfers between devices  65.3 us (15%)
  local copies, waits for them, and re-layouts  27.8 us (6%)
  between operations  15.4 us (4%)
    ppermute x36, starting transfers between devices, body(): came[flow] = lax.ppermute(x, ('tensor', 'query'), pairs(flow, low, high))  91.2 us
    pallas_call x13, Pallas kernels, backward_piece(): pl.pallas_call(kernel, grid=(steps,), in_specs=[pl.BlockSpec((parts, rows...  87.8 us
    pallas_call x13, Pallas kernels, forward_piece(): pl.pallas_call(kernel, grid=(steps,), in_specs=[pl.BlockSpec((parts, None...  79.4 us
    ppermute x36, waiting for transfers between devices, body(): came[flow] = lax.ppermute(x, ('tensor', 'query'), pairs(flow, low, high))  42.8 us
    pallas_call x24, Pallas kernels, add_term(): pl.pallas_call(kernel, grid_spec=pltpu.PrefetchScalarGridSpec(num_scalar_...  28.1 us
    unnamed x129, local copies, waits for them, and re-layouts  26.8 us
    unnamed x2, waiting for transfers between devices  21.4 us
    ppermute x7, starting transfers between devices, exchange(): lax.ppermute(value_of((rank + shift) % size), axis, [(d, (d + shift) % si...  13.6 us
  transfers between devices with their start and end apart: 44, of which 9 were waited for; matrix products, arithmetic and copies ran while one was open for 2% of the time, Pallas kernels for 37%

profile of v2, /device:TPU:0, one launch (start us, length us, event | category | flops | bytes accessed | tf_op | source)
XLA Modules:
  0.0 426.5 jit_solution(6207039955426376122)
XLA Ops:
  8.9 18.9 %forward_piece.13 = (bf16[4,32,8192]{2,1,0:T(8,128)(2,1)S(1)}, f32[8,128]{1,0:T(8,128)}) custom-call(bf16[4,4,32,2048]{3,2,1,0:T(8,128)(2,1)S(1)} %bitcast.60, bf16[2048,8192]{1,0:T(8,128)(2,1)} %w_ref.51), custom_call_target="tpu_custom_call" | custom-call | flops 4294967296 | bytes 33554432 | tf_op jit(solution)/shard_map/forward_piece/pallas_call | solution.py:54
  29.3 5.9 %collective-permute-start = (bf16[32,8192]{1,0:T(8,128)(2,1)}, bf16[32,8192]{1,0:T(8,128)(2,1)}, u32[]{:S(2)}, u32[]{:S(2)}) collective-permute-start(bf16[32,8192]{1,0:T(8,128)(2,1)} %add_term.24.refs_0_), channel_id=1, source_target_pairs={{0,4},{13,9},{2,6},{15,11},{16,20},{29,25},{18,22},{31,27}} | collective-permute-start | bytes 1572872 | tf_op jit(solution)/shard_map/ppermute | solution.py:350
  86.8 5.1 %forward_piece.19 = (bf16[4,32,8192]{2,1,0:T(8,128)(2,1)S(1)}, f32[8,128]{1,0:T(8,128)S(1)}) custom-call(bf16[4,4,32,2048]{3,2,1,0:T(8,128)(2,1)S(1)} %bitcast.66, bf16[2048,8192]{1,0:T(8,128)(2,1)} %w_ref.51, bf16[4,32,8192]{2,1,0:T(8,128)(2,1)S(1)} %get-tuple-element.55.refs_0_, bf16[32,8192]{1,0:T(8,128)(2,1)S(1)} %add_term.29.refs_1_), custom_call_target="tpu_custom_call", output_to_operand_aliasing={{0}: (2, {})} | custom-call | flops 1073741824 | bytes 8388608 | tf_op jit(solution)/shard_map/forward_piece/pallas_call | solution.py:54
  91.9 5.3 %collective-permute-done.5.b_ref = bf16[32,8192]{1,0:T(8,128)(2,1)S(1)} collective-permute-done((bf16[32,8192]{1,0:T(8,128)(2,1)S(1)}, bf16[32,8192]{1,0:T(8,128)(2,1)S(1)}, u32[]{:S(2)}, u32[]{:S(2)}) %collective-permute-start.5) | collective-permute-done | bytes 524320 | tf_op jit(solution)/shard_map/ppermute | solution.py:350
  104.3 5.5 %forward_piece.20 = (bf16[4,32,8192]{2,1,0:T(8,128)(2,1)S(1)}, f32[8,128]{1,0:T(8,128)}) custom-call(bf16[4,4,32,2048]{3,2,1,0:T(8,128)(2,1)S(1)} %bitcast.67, bf16[2048,8192]{1,0:T(8,128)(2,1)} %w_ref.51, bf16[4,32,8192]{2,1,0:T(8,128)(2,1)S(1)} %get-tuple-element.57.refs_0_, ...), custom_call_target="tpu_custom_call", output_to_operand_aliasing={{0}: (2, {})} | custom-call | flops 1073741824 | bytes 8388608 | tf_op jit(solution)/shard_map/forward_piece/pallas_call | solution.py:54
  158.4 8.5 %collective-permute-done.11.a_ref = bf16[32,8192]{1,0:T(8,128)(2,1)S(1)} collective-permute-done((bf16[32,8192]{1,0:T(8,128)(2,1)}, bf16[32,8192]{1,0:T(8,128)(2,1)S(1)}, u32[]{:S(2)}, u32[]{:S(2)}) %collective-permute-start.11) | collective-permute-done | bytes 524320 | tf_op jit(solution)/shard_map/ppermute | solution.py:350
  179.5 5.9 %backward_piece.13 = (bf16[4,4,32,2048]{3,2,1,0:T(8,128)(2,1)}, f32[8,128]{1,0:T(8,128)}) custom-call(bf16[4,32,8192]{2,1,0:T(8,128)(2,1)S(1)} %put_in_order.4.g_ref, bf16[2048,8192]{1,0:T(8,128)(2,1)} %w_ref.51, bf16[32,8192]{1,0:T(8,128)(2,1)S(1)} %norm_backward.5.refs_0_.refs_1_), custom_call_target="tpu_custom_call" | custom-call | flops 1073741824 | bytes 8388608 | tf_op jit(solution)/shard_map/backward_piece/pallas_call | solution.py:86
  185.4 5.8 %backward_piece.14 = (bf16[4,4,32,2048]{3,2,1,0:T(8,128)(2,1)}, f32[8,128]{1,0:T(8,128)S(1)}) custom-call(bf16[4,32,8192]{2,1,0:T(8,128)(2,1)S(1)} %put_in_order.4.g_ref, bf16[2048,8192]{1,0:T(8,128)(2,1)} %w_ref.51, bf16[4,4,32,2048]{3,2,1,0:T(8,128)(2,1)} %get-tuple-element.69.refs_0_, ...), custom_call_target="tpu_custom_call", output_to_operand_aliasing={{0}: (2, {})} | custom-call | flops 1073741824 | bytes 8388608 | tf_op jit(solution)/shard_map/backward_piece/pallas_call | solution.py:86
  196.8 5.9 %backward_piece.15 = (bf16[4,4,32,2048]{3,2,1,0:T(8,128)(2,1)}, f32[8,128]{1,0:T(8,128)S(1)}) custom-call(bf16[4,32,8192]{2,1,0:T(8,128)(2,1)S(1)} %put_in_order.4.g_ref, bf16[2048,8192]{1,0:T(8,128)(2,1)} %w_ref.51, bf16[4,4,32,2048]{3,2,1,0:T(8,128)(2,1)} %get-tuple-element.71.refs_0_, ...), custom_call_target="tpu_custom_call", output_to_operand_aliasing={{0}: (2, {})} | custom-call | flops 1073741824 | bytes 8388608 | tf_op jit(solution)/shard_map/backward_piece/pallas_call | solution.py:86
  204.7 5.9 %backward_piece.16 = (bf16[4,4,32,2048]{3,2,1,0:T(8,128)(2,1)}, f32[8,128]{1,0:T(8,128)S(1)}) custom-call(bf16[4,32,8192]{2,1,0:T(8,128)(2,1)S(1)} %put_in_order.4.g_ref, bf16[2048,8192]{1,0:T(8,128)(2,1)} %w_ref.51, bf16[4,4,32,2048]{3,2,1,0:T(8,128)(2,1)} %get-tuple-element.72.refs_0_, ...), custom_call_target="tpu_custom_call", output_to_operand_aliasing={{0}: (2, {})} | custom-call | flops 1073741824 | bytes 8388608 | tf_op jit(solution)/shard_map/backward_piece/pallas_call | solution.py:86
  218.2 9.0 %collective-permute-done.17.refs_0_.refs_3_ = bf16[32,8192]{1,0:T(8,128)(2,1)S(1)} collective-permute-done((bf16[32,8192]{1,0:T(8,128)(2,1)S(1)}, bf16[32,8192]{1,0:T(8,128)(2,1)S(1)}, u32[]{:S(2)}, u32[]{:S(2)}) %collective-permute-start.17) | collective-permute-done | bytes 524320 | tf_op jit(solution)/shard_map/ppermute | solution.py:350
  234.9 7.9 %collective-permute-done.18.a_ref = bf16[32,8192]{1,0:T(8,128)(2,1)S(1)} collective-permute-done((bf16[32,8192]{1,0:T(8,128)(2,1)S(1)}, bf16[32,8192]{1,0:T(8,128)(2,1)S(1)}, u32[]{:S(2)}, u32[]{:S(2)}) %collective-permute-start.18) | collective-permute-done | bytes 524320 | tf_op jit(solution)/shard_map/ppermute | solution.py:350
  254.5 5.9 %backward_piece.17 = (bf16[4,4,32,2048]{3,2,1,0:T(8,128)(2,1)}, f32[8,128]{1,0:T(8,128)}) custom-call(bf16[4,32,8192]{2,1,0:T(8,128)(2,1)S(1)} %put_in_order.5.g_ref, bf16[2048,8192]{1,0:T(8,128)(2,1)} %w_ref.51, bf16[4,4,32,2048]{3,2,1,0:T(8,128)(2,1)} %get-tuple-element.75.refs_0_, ...), custom_call_target="tpu_custom_call", output_to_operand_aliasing={{0}: (2, {})} | custom-call | flops 1073741824 | bytes 8388608 | tf_op jit(solution)/shard_map/backward_piece/pallas_call | solution.py:86
  260.3 5.8 %backward_piece.18 = (bf16[4,4,32,2048]{3,2,1,0:T(8,128)(2,1)}, f32[8,128]{1,0:T(8,128)S(1)}) custom-call(bf16[4,32,8192]{2,1,0:T(8,128)(2,1)S(1)} %put_in_order.5.g_ref, bf16[2048,8192]{1,0:T(8,128)(2,1)} %w_ref.51, bf16[4,4,32,2048]{3,2,1,0:T(8,128)(2,1)} %get-tuple-element.76.refs_0_, ...), custom_call_target="tpu_custom_call", output_to_operand_aliasing={{0}: (2, {})} | custom-call | flops 1073741824 | bytes 8388608 | tf_op jit(solution)/shard_map/backward_piece/pallas_call | solution.py:86
  271.6 5.9 %backward_piece.19 = (bf16[4,4,32,2048]{3,2,1,0:T(8,128)(2,1)}, f32[8,128]{1,0:T(8,128)S(1)}) custom-call(bf16[4,32,8192]{2,1,0:T(8,128)(2,1)S(1)} %put_in_order.5.g_ref, bf16[2048,8192]{1,0:T(8,128)(2,1)} %w_ref.51, bf16[4,4,32,2048]{3,2,1,0:T(8,128)(2,1)} %get-tuple-element.78.refs_0_, ...), custom_call_target="tpu_custom_call", output_to_operand_aliasing={{0}: (2, {})} | custom-call | flops 1073741824 | bytes 8388608 | tf_op jit(solution)/shard_map/backward_piece/pallas_call | solution.py:86
  279.5 5.9 %backward_piece.20 = (bf16[4,4,32,2048]{3,2,1,0:T(8,128)(2,1)}, f32[8,128]{1,0:T(8,128)S(1)}) custom-call(bf16[4,32,8192]{2,1,0:T(8,128)(2,1)S(1)} %put_in_order.5.g_ref, bf16[2048,8192]{1,0:T(8,128)(2,1)} %w_ref.51, bf16[4,4,32,2048]{3,2,1,0:T(8,128)(2,1)} %get-tuple-element.79.refs_0_, ...), custom_call_target="tpu_custom_call", output_to_operand_aliasing={{0}: (2, {})} | custom-call | flops 1073741824 | bytes 8388608 | tf_op jit(solution)/shard_map/backward_piece/pallas_call | solution.py:86
  293.0 8.9 %collective-permute-done.25.refs_0_.refs_3_ = bf16[32,8192]{1,0:T(8,128)(2,1)S(1)} collective-permute-done((bf16[32,8192]{1,0:T(8,128)(2,1)S(1)}, bf16[32,8192]{1,0:T(8,128)(2,1)S(1)}, u32[]{:S(2)}, u32[]{:S(2)}) %collective-permute-start.25) | collective-permute-done | bytes 524320 | tf_op jit(solution)/shard_map/ppermute | solution.py:350
  303.5 5.3 %collective-permute-start.26 = (bf16[32,8192]{1,0:T(8,128)(2,1)}, bf16[32,8192]{1,0:T(8,128)(2,1)}, u32[]{:S(2)}, u32[]{:S(2)}) collective-permute-start(bf16[32,8192]{1,0:T(8,128)(2,1)} %add_term.45), channel_id=1, source_target_pairs={{0,4},{4,8},{8,12},{5,1},{9,5},{13,9},{2,6},{6,10},{10,14},{7,3},{... | collective-permute-start | bytes 1572872 | tf_op jit(solution)/shard_map/ppermute | solution.py:350
  313.9 21.4 %reduce-scatter.4.cloned.1.call-done = bf16[128,64]{1,0:T(8,128)(2,1)} async-done(((bf16[512,64]{1,0:T(8,128)(2,1)}), bf16[128,64]{1,0:T(8,128)(2,1)}) %reduce-scatter.4.cloned.1.call-update) | async-done | bytes 16400
  360.5 5.9 %backward_piece.21 = (bf16[4,4,32,2048]{3,2,1,0:T(8,128)(2,1)}, f32[8,128]{1,0:T(8,128)}) custom-call(bf16[4,32,8192]{2,1,0:T(8,128)(2,1)S(1)} %put_in_order.7.g_ref, bf16[2048,8192]{1,0:T(8,128)(2,1)} %w_ref.51, bf16[4,4,32,2048]{3,2,1,0:T(8,128)(2,1)} %get-tuple-element.82.refs_0_, ...), custom_call_target="tpu_custom_call", output_to_operand_aliasing={{0}: (2, {})} | custom-call | flops 1073741824 | bytes 8388608 | tf_op jit(solution)/shard_map/backward_piece/pallas_call | solution.py:86
  374.2 5.9 %backward_piece.22 = (bf16[4,4,32,2048]{3,2,1,0:T(8,128)(2,1)}, f32[8,128]{1,0:T(8,128)}) custom-call(bf16[4,32,8192]{2,1,0:T(8,128)(2,1)S(1)} %put_in_order.7.g_ref, bf16[2048,8192]{1,0:T(8,128)(2,1)} %w_ref.51, bf16[4,4,32,2048]{3,2,1,0:T(8,128)(2,1)} %get-tuple-element.83.refs_0_, ...), custom_call_target="tpu_custom_call", output_to_operand_aliasing={{0}: (2, {})} | custom-call | flops 1073741824 | bytes 8388608 | tf_op jit(solution)/shard_map/backward_piece/pallas_call | solution.py:86
  388.3 5.9 %backward_piece.23 = (bf16[4,4,32,2048]{3,2,1,0:T(8,128)(2,1)}, f32[8,128]{1,0:T(8,128)}) custom-call(bf16[4,32,8192]{2,1,0:T(8,128)(2,1)S(1)} %put_in_order.7.g_ref, bf16[2048,8192]{1,0:T(8,128)(2,1)} %w_ref.51, bf16[4,4,32,2048]{3,2,1,0:T(8,128)(2,1)} %get-tuple-element.84.refs_0_, ...), custom_call_target="tpu_custom_call", output_to_operand_aliasing={{0}: (2, {})} | custom-call | flops 1073741824 | bytes 8388608 | tf_op jit(solution)/shard_map/backward_piece/pallas_call | solution.py:86
  394.1 5.9 %backward_piece.24 = (bf16[4,4,32,2048]{3,2,1,0:T(8,128)(2,1)}, f32[8,128]{1,0:T(8,128)}) custom-call(bf16[4,32,8192]{2,1,0:T(8,128)(2,1)S(1)} %put_in_order.7.g_ref, bf16[2048,8192]{1,0:T(8,128)(2,1)} %w_ref.51, bf16[4,4,32,2048]{3,2,1,0:T(8,128)(2,1)} %get-tuple-element.85.refs_0_, ...), custom_call_target="tpu_custom_call", output_to_operand_aliasing={{0}: (2, {})} | custom-call | flops 1073741824 | bytes 8388608 | tf_op jit(solution)/shard_map/backward_piece/pallas_call | solution.py:86
  402.2 17.5 %backward_piece.25 = (bf16[4,4,32,2048]{3,2,1,0:T(8,128)(2,1)}, f32[8,128]{1,0:T(8,128)}) custom-call(bf16[4,32,8192]{2,1,0:T(8,128)(2,1)S(1)} %put_in_order.6.g_ref, bf16[2048,8192]{1,0:T(8,128)(2,1)} %w_ref.51, bf16[4,4,32,2048]{3,2,1,0:T(8,128)(2,1)} %get-tuple-element.86.refs_0_), custom_call_target="tpu_custom_call", output_to_operand_aliasing={{0}: (2, {})} | custom-call | flops 4294967296 | bytes 33554432 | tf_op jit(solution)/shard_map/backward_piece/pallas_call | solution.py:86
  (283 shorter events, 221.6 us)
Async XLA Ops:
  7.2 328.0 %reduce-scatter.4.cloned.1.call-start = ((), (), s32[]{:S(2)}) async-start(), calls=%async_computation.1 | async-start | bytes 163840
  29.3 23.2 %collective-permute-start = (bf16[32,8192]{1,0:T(8,128)(2,1)}, bf16[32,8192]{1,0:T(8,128)(2,1)}, u32[]{:S(2)}, u32[]{:S(2)}) collective-permute-start(bf16[32,8192]{1,0:T(8,128)(2,1)} %add_term.24.refs_0_), channel_id=1, source_target_pairs={{0,4},{13,9},{2,6},{15,11},{16,20},{29,25},{18,22},{31,27}} | collective-permute-start | bytes 1572872 | tf_op jit(solution)/shard_map/ppermute | solution.py:350
  42.9 20.4 %collective-permute-start.1 = (bf16[32,8192]{1,0:T(8,128)(2,1)}, bf16[32,8192]{1,0:T(8,128)(2,1)}, u32[]{:S(2)}, u32[]{:S(2)}) collective-permute-start(bf16[32,8192]{1,0:T(8,128)(2,1)} %add_term.25.refs_1_), channel_id=1, source_target_pairs={{12,8},{1,5},{14,10},{3,7},{28,24},{17,21},{30,26},{19,23}} | collective-permute-start | bytes 1572872 | tf_op jit(solution)/shard_map/ppermute | solution.py:350
  54.9 20.3 %collective-permute-start.2 = (bf16[32,8192]{1,0:T(8,128)(2,1)}, bf16[32,8192]{1,0:T(8,128)(2,1)}, u32[]{:S(2)}, u32[]{:S(2)}) collective-permute-start(bf16[32,8192]{1,0:T(8,128)(2,1)} %add_term.26.refs_1_), channel_id=1, source_target_pairs={{0,4},{4,8},{9,5},{13,9},{2,6},{6,10},{11,7},{15,11},{16,20},{20,2... | collective-permute-start | bytes 1572872 | tf_op jit(solution)/shard_map/ppermute | solution.py:350
  65.6 18.1 %collective-permute-start.4 = (bf16[32,8192]{1,0:T(8,128)(2,1)}, bf16[32,8192]{1,0:T(8,128)(2,1)}, u32[]{:S(2)}, u32[]{:S(2)}) collective-permute-start(bf16[32,8192]{1,0:T(8,128)(2,1)} %add_term.27.refs_1_), channel_id=1, source_target_pairs={{8,4},{12,8},{1,5},{5,9},{10,6},{14,10},{3,7},{7,11},{24,20},{28,2... | collective-permute-start | bytes 1572872 | tf_op jit(solution)/shard_map/ppermute | solution.py:350
  99.0 15.9 %collective-permute-start.6 = (bf16[32,8192]{1,0:T(8,128)(2,1)S(1)}, bf16[32,8192]{1,0:T(8,128)(2,1)S(1)}, u32[]{:S(2)}, u32[]{:S(2)}) collective-permute-start(bf16[32,8192]{1,0:T(8,128)(2,1)S(1)} %norm_backward.4.refs_1_.refs_0_), channel_id=1, source_target_pairs={{0,4},{4,8},{8,12},{5,1},{9,5},{13,9},{2,6},{6,10},{10,14},{7,3},{... | collective-permute-start | bytes 1572872 | tf_op jit(solution)/shard_map/ppermute | solution.py:350
  103.0 22.3 %collective-permute-start.7 = (bf16[32,8192]{1,0:T(8,128)(2,1)S(1)}, bf16[32,8192]{1,0:T(8,128)(2,1)S(1)}, u32[]{:S(2)}, u32[]{:S(2)}) collective-permute-start(bf16[32,8192]{1,0:T(8,128)(2,1)S(1)} %norm_backward.4.refs_1_.refs_0_), channel_id=1, source_target_pairs={{4,0},{8,4},{12,8},{1,5},{5,9},{9,13},{6,2},{10,6},{14,10},{3,7},{... | collective-permute-start | bytes 1572872 | tf_op jit(solution)/shard_map/ppermute | solution.py:350
  115.8 16.6 %collective-permute-start.8 = (bf16[32,8192]{1,0:T(8,128)(2,1)S(1)}, bf16[32,8192]{1,0:T(8,128)(2,1)S(1)}, u32[]{:S(2)}, u32[]{:S(2)}) collective-permute-start(bf16[32,8192]{1,0:T(8,128)(2,1)S(1)} %add_term.30.refs_0_), channel_id=1, source_target_pairs={{0,4},{4,8},{8,12},{5,1},{9,5},{13,9},{2,6},{6,10},{10,14},{7,3},{... | collective-permute-start | bytes 1572872 | tf_op jit(solution)/shard_map/ppermute | solution.py:350
  126.1 16.7 %collective-permute-start.9 = (bf16[32,8192]{1,0:T(8,128)(2,1)S(1)}, bf16[32,8192]{1,0:T(8,128)(2,1)S(1)}, u32[]{:S(2)}, u32[]{:S(2)}) collective-permute-start(bf16[32,8192]{1,0:T(8,128)(2,1)S(1)} %add_term.31.refs_1_), channel_id=1, source_target_pairs={{4,0},{8,4},{12,8},{1,5},{5,9},{9,13},{6,2},{10,6},{14,10},{3,7},{... | collective-permute-start | bytes 1572872 | tf_op jit(solution)/shard_map/ppermute | solution.py:350
  133.3 16.7 %collective-permute-start.10 = (bf16[32,8192]{1,0:T(8,128)(2,1)S(1)}, bf16[32,8192]{1,0:T(8,128)(2,1)S(1)}, u32[]{:S(2)}, u32[]{:S(2)}) collective-permute-start(bf16[32,8192]{1,0:T(8,128)(2,1)S(1)} %add_term.32.refs_1_), channel_id=1, source_target_pairs={{0,4},{4,8},{8,12},{5,1},{9,5},{13,9},{2,6},{6,10},{10,14},{7,3},{... | collective-permute-start | bytes 1572872 | tf_op jit(solution)/shard_map/ppermute | solution.py:350
  170.0 21.2 %collective-permute-start.14 = (bf16[32,8192]{1,0:T(8,128)(2,1)S(1)}, bf16[32,8192]{1,0:T(8,128)(2,1)S(1)}, u32[]{:S(2)}, u32[]{:S(2)}) collective-permute-start(bf16[32,8192]{1,0:T(8,128)(2,1)S(1)} %norm_backward.5.refs_0_.refs_1_), channel_id=1, source_target_pairs={{0,4},{4,8},{8,12},{5,1},{9,5},{13,9},{2,6},{6,10},{10,14},{7,3},{... | collective-permute-start | bytes 1572872 | tf_op jit(solution)/shard_map/ppermute | solution.py:350
  173.2 29.5 %collective-permute-start.16 = (bf16[32,8192]{1,0:T(8,128)(2,1)S(1)}, bf16[32,8192]{1,0:T(8,128)(2,1)S(1)}, u32[]{:S(2)}, u32[]{:S(2)}) collective-permute-start(bf16[32,8192]{1,0:T(8,128)(2,1)S(1)} %norm_backward.5.refs_0_.refs_1_), channel_id=1, source_target_pairs={{4,0},{8,4},{12,8},{1,5},{5,9},{9,13},{6,2},{10,6},{14,10},{3,7},{... | collective-permute-start | bytes 1572872 | tf_op jit(solution)/shard_map/ppermute | solution.py:350
  192.1 18.5 %collective-permute-start.15 = (bf16[32,8192]{1,0:T(8,128)(2,1)S(1)}, bf16[32,8192]{1,0:T(8,128)(2,1)S(1)}, u32[]{:S(2)}, u32[]{:S(2)}) collective-permute-start(bf16[32,8192]{1,0:T(8,128)(2,1)S(1)} %add_term.36.refs_1_), channel_id=1, source_target_pairs={{0,4},{4,8},{8,12},{5,1},{9,5},{13,9},{2,6},{6,10},{10,14},{7,3},{... | collective-permute-start | bytes 1572872 | tf_op jit(solution)/shard_map/ppermute | solution.py:350
  216.9 15.7 %collective-permute-start.20 = (bf16[32,8192]{1,0:T(8,128)(2,1)S(1)}, bf16[32,8192]{1,0:T(8,128)(2,1)S(1)}, u32[]{:S(2)}, u32[]{:S(2)}) collective-permute-start(bf16[32,8192]{1,0:T(8,128)(2,1)S(1)} %add_term.40), channel_id=1, source_target_pairs={{4,0},{8,4},{12,8},{1,5},{5,9},{9,13},{6,2},{10,6},{14,10},{3,7},{... | collective-permute-start | bytes 1572872 | tf_op jit(solution)/shard_map/ppermute | solution.py:350
  246.5 19.7 %collective-permute-start.22 = (bf16[32,8192]{1,0:T(8,128)(2,1)S(1)}, bf16[32,8192]{1,0:T(8,128)(2,1)S(1)}, u32[]{:S(2)}, u32[]{:S(2)}) collective-permute-start(bf16[32,8192]{1,0:T(8,128)(2,1)S(1)} %norm_backward.6.refs_1_.refs_0_), channel_id=1, source_target_pairs={{0,4},{4,8},{8,12},{5,1},{9,5},{13,9},{2,6},{6,10},{10,14},{7,3},{... | collective-permute-start | bytes 1572872 | tf_op jit(solution)/shard_map/ppermute | solution.py:350
  250.3 27.2 %collective-permute-start.24 = (bf16[32,8192]{1,0:T(8,128)(2,1)S(1)}, bf16[32,8192]{1,0:T(8,128)(2,1)S(1)}, u32[]{:S(2)}, u32[]{:S(2)}) collective-permute-start(bf16[32,8192]{1,0:T(8,128)(2,1)S(1)} %norm_backward.6.refs_1_.refs_0_), channel_id=1, source_target_pairs={{4,0},{8,4},{12,8},{1,5},{5,9},{9,13},{6,2},{10,6},{14,10},{3,7},{... | collective-permute-start | bytes 1572872 | tf_op jit(solution)/shard_map/ppermute | solution.py:350
  267.1 18.3 %collective-permute-start.23 = (bf16[32,8192]{1,0:T(8,128)(2,1)S(1)}, bf16[32,8192]{1,0:T(8,128)(2,1)S(1)}, u32[]{:S(2)}, u32[]{:S(2)}) collective-permute-start(bf16[32,8192]{1,0:T(8,128)(2,1)S(1)} %add_term.42.refs_1_), channel_id=1, source_target_pairs={{0,4},{4,8},{8,12},{5,1},{9,5},{13,9},{2,6},{6,10},{10,14},{7,3},{... | collective-permute-start | bytes 1572872 | tf_op jit(solution)/shard_map/ppermute | solution.py:350
  291.7 17.1 %collective-permute-start.28 = (bf16[32,8192]{1,0:T(8,128)(2,1)S(1)}, bf16[32,8192]{1,0:T(8,128)(2,1)S(1)}, u32[]{:S(2)}, u32[]{:S(2)}) collective-permute-start(bf16[32,8192]{1,0:T(8,128)(2,1)S(1)} %add_term.46), channel_id=1, source_target_pairs={{4,0},{8,4},{12,8},{1,5},{5,9},{9,13},{6,2},{10,6},{14,10},{3,7},{... | collective-permute-start | bytes 1572872 | tf_op jit(solution)/shard_map/ppermute | solution.py:350
  303.5 40.8 %collective-permute-start.26 = (bf16[32,8192]{1,0:T(8,128)(2,1)}, bf16[32,8192]{1,0:T(8,128)(2,1)}, u32[]{:S(2)}, u32[]{:S(2)}) collective-permute-start(bf16[32,8192]{1,0:T(8,128)(2,1)} %add_term.45), channel_id=1, source_target_pairs={{0,4},{4,8},{8,12},{5,1},{9,5},{13,9},{2,6},{6,10},{10,14},{7,3},{... | collective-permute-start | bytes 1572872 | tf_op jit(solution)/shard_map/ppermute | solution.py:350
  310.3 34.0 %collective-permute-start.29 = (bf16[32,8192]{1,0:T(8,128)(2,1)}, bf16[32,8192]{1,0:T(8,128)(2,1)}, u32[]{:S(2)}, u32[]{:S(2)}) collective-permute-start(bf16[32,8192]{1,0:T(8,128)(2,1)} %add_term.47), channel_id=1, source_target_pairs={{4,0},{8,4},{12,8},{1,5},{5,9},{9,13},{6,2},{10,6},{14,10},{3,7},{... | collective-permute-start | bytes 1572872 | tf_op jit(solution)/shard_map/ppermute | solution.py:350
  348.5 19.3 %collective-permute-start.30 = (bf16[32,8192]{1,0:T(8,128)(2,1)}, bf16[32,8192]{1,0:T(8,128)(2,1)}, u32[]{:S(2)}, u32[]{:S(2)}) collective-permute-start(bf16[32,8192]{1,0:T(8,128)(2,1)} %norm_backward.7.refs_0_.refs_1_), channel_id=1, source_target_pairs={{0,4},{4,8},{8,12},{5,1},{9,5},{13,9},{2,6},{6,10},{10,14},{7,3},{... | collective-permute-start | bytes 1572872 | tf_op jit(solution)/shard_map/ppermute | solution.py:350
  350.6 18.7 %collective-permute-start.33 = (bf16[32,8192]{1,0:T(8,128)(2,1)}, bf16[32,8192]{1,0:T(8,128)(2,1)}, u32[]{:S(2)}, u32[]{:S(2)}) collective-permute-start(bf16[32,8192]{1,0:T(8,128)(2,1)} %norm_backward.7.refs_0_.refs_1_), channel_id=1, source_target_pairs={{4,0},{8,4},{12,8},{1,5},{5,9},{9,13},{6,2},{10,6},{14,10},{3,7},{... | collective-permute-start | bytes 1572872 | tf_op jit(solution)/shard_map/ppermute | solution.py:350
  367.8 17.1 %collective-permute-start.31 = (bf16[32,8192]{1,0:T(8,128)(2,1)}, bf16[32,8192]{1,0:T(8,128)(2,1)}, u32[]{:S(2)}, u32[]{:S(2)}) collective-permute-start(bf16[32,8192]{1,0:T(8,128)(2,1)} %collective-permute-done.30.refs_1_), channel_id=1, source_target_pairs={{4,8},{8,12},{5,1},{9,5},{6,10},{10,14},{7,3},{11,7},{20,24},{24,2... | collective-permute-start | bytes 1572872 | tf_op jit(solution)/shard_map/ppermute | solution.py:350
  369.3 17.0 %collective-permute-start.34 = (bf16[32,8192]{1,0:T(8,128)(2,1)}, bf16[32,8192]{1,0:T(8,128)(2,1)}, u32[]{:S(2)}, u32[]{:S(2)}) collective-permute-start(bf16[32,8192]{1,0:T(8,128)(2,1)} %collective-permute-done.33.refs_4_.refs_1_), channel_id=1, source_target_pairs={{4,0},{8,4},{5,9},{9,13},{6,2},{10,6},{7,11},{11,15},{20,16},{24,2... | collective-permute-start | bytes 1572872 | tf_op jit(solution)/shard_map/ppermute | solution.py:350
  (82 other events, 1281.7 us)
Sparse Core Ops, SparseCore 0:
  313.2 21.9 reduce-scatter.3

commit v3 on v0

v3 whole, which is shorter than its diff:
```python
import functools

import jax
import jax.numpy as jnp
from jax import lax
from jax.experimental import pallas as pl
from jax.experimental.pallas import tpu as pltpu
from jax.sharding import PartitionSpec as P

EX_DEV = 4
EPS = 1e-05
CHUNKS = 2
HALVES = 2
PIECES = 4
SPLIT = 4
SHORT, LONG = 0.2, 5.0
LIMIT = 28 * 1024 * 1024

F32, BF16 = jnp.float32, jnp.bfloat16
ANY = pl.BlockSpec(memory_space=pl.ANY)
TOKEN = jax.ShapeDtypeStruct((8, 128), F32)
TOKEN_SPEC = pl.BlockSpec((8, 128), lambda *_: (0, 0))


def divisor(total, wanted):
    size = min(total, wanted)
    while total % size:
        size //= 2
    return size


def cost(microseconds):
    return pl.CostEstimate(flops=0, bytes_accessed=int(microseconds * 3.6e6), transcendentals=0)


def project_rows(values, matrix):
    return lax.dot_general(
        values, matrix, (((1,), (1,)), ((), ())), preferred_element_type=F32
    )


def project_inputs(tok_rows, proj_in, after):
    tokens, depth = tok_rows.shape
    width = proj_in.shape[0]

    def kernel(x_ref, p_ref, *refs):
        refs[-1][...] = project_rows(x_ref[...], p_ref[...]).astype(BF16)

    return pl.pallas_call(
        kernel,
        grid=(1,),
        in_specs=[
            pl.BlockSpec((tokens, depth), lambda i: (0, 0)),
            pl.BlockSpec((width, depth), lambda i: (0, 0)),
        ]
        + [ANY] * len(after),
        out_specs=pl.BlockSpec((tokens, width), lambda i: (0, 0)),
        out_shape=jax.ShapeDtypeStruct((tokens, width), BF16),
        compiler_params=pltpu.CompilerParams(vmem_limit_bytes=LIMIT),
        cost_estimate=cost(SHORT),
        name="project_inputs",
    )(tok_rows, proj_in, *after)


def forward_piece(by_share, w_out, chunk, halves, half_at, piece, pieces, held, after):
    parts, _, rows, depth = by_share.shape
    half = w_out.shape[1] // halves
    span = half // pieces
    cols = divisor(span, 512)
    steps = span // cols
    base = (half_at * half + piece * span) // cols
    cut = depth // SPLIT

    def kernel(x_ref, *refs):
        out_ref, tok_ref = refs[-2:]
        x = x_ref[...].reshape(parts * rows, depth)
        y = None
        for s in range(SPLIT):
            term = jnp.dot(x[:, s * cut : (s + 1) * cut], refs[s][...], preferred_element_type=F32)
            y = term if y is None else y + term
        out_ref[...] = y.astype(BF16).reshape(parts, rows, cols)
        tok_ref[...] = jnp.zeros_like(tok_ref)

    extra = ([] if held is None else [held]) + after
    return pl.pallas_call(
        kernel,
        grid=(steps,),
        in_specs=[pl.BlockSpec((parts, None, rows, depth), lambda i: (0, chunk, 0, 0))]
        + [pl.BlockSpec((cut, cols), lambda i, s=s: (s, base + i)) for s in range(SPLIT)]
        + [ANY] * len(extra),
        out_specs=[
            pl.BlockSpec((parts, rows, cols), lambda i: (0, 0, piece * steps + i)),
            TOKEN_SPEC,
        ],
        out_shape=[jax.ShapeDtypeStruct((parts, rows, half), BF16), TOKEN],
        input_output_aliases={} if held is None else {1 + SPLIT: 0},
        compiler_params=pltpu.CompilerParams(vmem_limit_bytes=LIMIT),
        cost_estimate=cost(SHORT),
        name="forward_piece",
    )(by_share, *([w_out] * SPLIT), *extra)


def backward_piece(blocks, w_out, chunk, chunks, halves, piece, pieces, total, last, held, after):
    parts, rows, half = blocks[0][1].shape
    depth = w_out.shape[0]
    span = depth // pieces
    cols = divisor(span, 256)
    steps = span // cols
    cut = half // SPLIT
    n = len(blocks)

    def kernel(*refs):
        out_ref, tok_ref = refs[-2:]
        y = None if total is None else refs[n + n * SPLIT][...].reshape(parts * rows, cols)
        for b in range(n):
            g = refs[b][...].reshape(parts * rows, half)
            for s in range(SPLIT):
                term = project_rows(g[:, s * cut : (s + 1) * cut], refs[n + b * SPLIT + s][...])
                y = term if y is None else y + term
        out_ref[...] = y.astype(out_ref.dtype).reshape(parts, rows, cols)
        tok_ref[...] = jnp.zeros_like(tok_ref)

    here = pl.BlockSpec((parts, rows, cols), lambda i: (0, 0, piece * steps + i))
    if last:
        out_spec = pl.BlockSpec((parts, None, rows, cols), lambda i: (0, chunk, 0, piece * steps + i))
        out_shape = jax.ShapeDtypeStruct((parts, chunks, rows, depth), BF16)
    else:
        out_spec, out_shape = here, jax.ShapeDtypeStruct((parts, rows, depth), F32)
    weights = [
        pl.BlockSpec((cols, cut), lambda i, at=at * SPLIT + s: (piece * steps + i, at))
        for at, _ in blocks
        for s in range(SPLIT)
    ]
    sums = [] if total is None else [total]
    extra = ([] if held is None else [held]) + after
    return pl.pallas_call(
        kernel,
        grid=(steps,),
        in_specs=[pl.BlockSpec((parts, rows, half), lambda i: (0, 0, 0))] * n
        + weights
        + [here] * len(sums)
        + [ANY] * len(extra),
        out_specs=[out_spec, TOKEN_SPEC],
        out_shape=[out_shape, TOKEN],
        input_output_aliases={} if held is None else {n + n * SPLIT + len(sums): 0},
        compiler_params=pltpu.CompilerParams(vmem_limit_bytes=LIMIT),
        cost_estimate=cost(SHORT),
        name="backward_piece",
    )(*[g for _, g in blocks], *([w_out] * (n * SPLIT)), *sums, *extra)


def relay(where, partial, came, held, after):
    rows, width = came.shape
    n_in = 1 + (partial is not None) + (held is not None) + len(after)

    def kernel(where_ref, *refs):
        came_ref, x_ref = refs[0], refs[n_in]
        if held is not None:
            store = pltpu.make_async_copy(came_ref, refs[n_in + 1].at[where_ref[2]], refs[-1])
            pl.when(where_ref[3] == 1)(store.start)
        if partial is not None:

            @pl.when(where_ref[1] == 1)
            def _():
                x_ref[...] = (came_ref[...].astype(F32) + refs[1][...].astype(F32)).astype(BF16)

            @pl.when(where_ref[1] == 0)
            def _():
                x_ref[...] = came_ref[...]

        if held is not None:
            pl.when(where_ref[3] == 1)(store.wait)

    line = jax.ShapeDtypeStruct((rows, width), BF16)
    args, out_shape, alias = [came], [line], {}
    if partial is not None:
        whole = pl.BlockSpec((rows, width), lambda i, w: (0, 0))
        specs, out_specs = [whole, pl.BlockSpec((None, rows, width), lambda i, w: (w[0], 0, 0))], [whole]
        args.append(partial)
    else:
        specs, out_specs, alias = [ANY], [ANY], {1: 0}
    if held is not None:
        alias[1 + len(args)] = 1
        specs.append(ANY)
        args.append(held)
        out_specs.append(ANY)
        out_shape.append(jax.ShapeDtypeStruct(held.shape, BF16))
    outs = pl.pallas_call(
        kernel,
        grid_spec=pltpu.PrefetchScalarGridSpec(
            num_scalar_prefetch=1,
            grid=(1,),
            in_specs=specs + [ANY] * len(after),
            out_specs=out_specs,
            scratch_shapes=[pltpu.SemaphoreType.DMA] if held is not None else [],
        ),
        out_shape=out_shape,
        input_output_aliases=alias,
        compiler_params=pltpu.CompilerParams(vmem_limit_bytes=LIMIT),
        cost_estimate=cost(LONG),
        name="relay",
    )(where, *args, *after)
    return outs[0], (outs[1] if held is not None else None)


def take_block(partial, at):
    return lax.dynamic_index_in_dim(partial, at, 0, keepdims=False)


def norm_terms(p_ref, a_ref, b_ref, res_ref, grad_ref, gain_ref, at):
    proj = p_ref[:, at].astype(F32) + a_ref[:, at].astype(F32) + b_ref[:, at].astype(F32)
    z = res_ref[:, at].astype(F32) + proj
    scaled = gain_ref[:, at].astype(F32) * grad_ref[:, at].astype(F32)
    return z, scaled


def norm_specs(rows, half, chunk, at):
    whole = pl.BlockSpec((rows, half), lambda i, r: (0, 0))
    own = pl.BlockSpec((None, rows, half), lambda i, r: (0, chunk, at))
    mine = pl.BlockSpec((None, rows, half), lambda i, r: (r[0], 0, 0))
    return [mine, whole, whole, own, own, pl.BlockSpec((1, half), lambda i, r: (0, at))]


def norm_sums(rank, ins, chunk, at, sums, after):
    parts, rows, half = ins[0].shape
    cols = divisor(half, 1024)

    def kernel(rank_ref, *refs):
        square_ref, cross_ref = refs[-2:]

        def step(i, sums):
            z, scaled = norm_terms(*refs[:6], pl.ds(pl.multiple_of(i * cols, cols), cols))
            square, cross = sums
            for j in range(0, cols, 128):
                zj = z[:, j : j + 128]
                square = square + zj * zj
                cross = cross + zj * scaled[:, j : j + 128]
            return square, cross

        zero = jnp.zeros((rows, 128), F32)
        start = (zero, zero) if sums is None else (refs[6][...], refs[7][...])
        square_ref[...], cross_ref[...] = lax.fori_loop(0, half // cols, step, start)

    stat = pl.BlockSpec((rows, 128), lambda i, r: (0, 0))
    before = [] if sums is None else list(sums)
    return pl.pallas_call(
        kernel,
        grid_spec=pltpu.PrefetchScalarGridSpec(
            num_scalar_prefetch=1,
            grid=(1,),
            in_specs=norm_specs(rows, half, chunk, at) + [stat] * len(before) + [ANY] * len(after),
            out_specs=[stat, stat],
        ),
        out_shape=[jax.ShapeDtypeStruct((rows, 128), F32)] * 2,
        compiler_params=pltpu.CompilerParams(vmem_limit_bytes=LIMIT),
        cost_estimate=cost(LONG),
        name="norm_sums",
    )(rank, *ins, *before, *after)


def norm_out(rank, ins, chunk, at, sums, width, after):
    parts, rows, half = ins[0].shape
    cols = divisor(half, 1024)

    def kernel(rank_ref, *refs):
        out_ref, held_ref, sem = refs[-3:]
        inv = lax.rsqrt(jnp.sum(refs[6][...], axis=-1, keepdims=True) / width + EPS)
        slope = inv * inv * inv * (jnp.sum(refs[7][...], axis=-1, keepdims=True) / width)

        def step(i, carry):
            here = pl.ds(pl.multiple_of(i * cols, cols), cols)
            z, scaled = norm_terms(*refs[:6], here)
            out_ref[:, here] = (inv * scaled - z * slope).astype(BF16)
            return carry

        lax.fori_loop(0, half // cols, step, 0)
        own = pltpu.make_async_copy(out_ref, held_ref.at[rank_ref[0]], sem)
        own.start()
        own.wait()

    stat = pl.BlockSpec((rows, 128), lambda i, r: (0, 0))
    return pl.pallas_call(
        kernel,
        grid_spec=pltpu.PrefetchScalarGridSpec(
            num_scalar_prefetch=1,
            grid=(1,),
            in_specs=norm_specs(rows, half, chunk, at) + [stat, stat] + [ANY] * len(after),
            out_specs=[pl.BlockSpec((rows, half), lambda i, r: (0, 0)), ANY],
            scratch_shapes=[pltpu.SemaphoreType.DMA],
        ),
        out_shape=[
            jax.ShapeDtypeStruct((rows, half), BF16),
            jax.ShapeDtypeStruct((parts, rows, half), BF16),
        ],
        compiler_params=pltpu.CompilerParams(vmem_limit_bytes=LIMIT),
        cost_estimate=cost(SHORT),
        name="norm_out",
    )(rank, *ins, *sums, *after)


def project_grads(grads, proj_out, after):
    blocks = [block for grad in grads for block in grad]
    rows, half = blocks[0].shape
    halves = len(grads[0])
    width = proj_out.shape[0]

    def kernel(*refs):
        out_ref, p_ref = refs[-1], refs[len(blocks)]
        for c in range(len(grads)):
            y = None
            for h in range(halves):
                term = project_rows(refs[c * halves + h][...], p_ref[:, h * half : (h + 1) * half])
                y = term if y is None else y + term
            out_ref[c * rows : (c + 1) * rows, :] = y

    return pl.pallas_call(
        kernel,
        grid=(1,),
        in_specs=[pl.BlockSpec((rows, half), lambda i: (0, 0))] * len(blocks)
        + [pl.BlockSpec(proj_out.shape, lambda i: (0, 0))]
        + [ANY] * len(after),
        out_specs=pl.BlockSpec((len(grads) * rows, width), lambda i: (0, 0)),
        out_shape=jax.ShapeDtypeStruct((len(grads) * rows, width), F32),
        compiler_params=pltpu.CompilerParams(vmem_limit_bytes=LIMIT),
        cost_estimate=cost(SHORT),
        name="project_grads",
    )(*blocks, proj_out, *after)


def tie(value, after):
    def kernel(value_ref, *refs):
        refs[-1][...] = value_ref[...]

    whole = pl.BlockSpec(value.shape, lambda i: (0,) * value.ndim)
    return pl.pallas_call(
        kernel,
        grid=(1,),
        in_specs=[whole] + [ANY] * len(after),
        out_specs=whole,
        out_shape=jax.ShapeDtypeStruct(value.shape, value.dtype),
        compiler_params=pltpu.CompilerParams(vmem_limit_bytes=LIMIT),
        cost_estimate=cost(SHORT),
        name="tie",
    )(value, *after)


def exchange(value_of, axis, size, rank):
    first = value_of(rank)
    out = jnp.zeros((size,) + first.shape, first.dtype)
    out = lax.dynamic_update_index_in_dim(out, first, rank, 0)
    for shift in range(1, size):
        got = lax.ppermute(
            value_of((rank + shift) % size), axis, [(d, (d + shift) % size) for d in range(size)]
        )
        out = lax.dynamic_update_index_in_dim(out, got, (rank - shift + size) % size, 0)
    return out


def body(inputs, residual, out_grad, norm_gain, w_out, proj_in, proj_out, queries, segment_ids):
    parts = lax.axis_size("tensor")
    rank = lax.axis_index("tensor")
    queriers = lax.axis_size("query")
    q_rank = lax.axis_index("query")
    tokens = inputs.shape[1]
    share = tokens // parts
    chunks = max(1, min(CHUNKS, share // 16))
    rows = share // chunks
    by_share = inputs.reshape(parts, chunks, rows, inputs.shape[2])
    gain = norm_gain.reshape(1, -1)
    half = w_out.shape[1] // HALVES

    up = 1 - 2 * (q_rank % 2)
    ways = (up, -up)
    spots = [jnp.where(way == 1, rank, parts - 1 - rank) for way in ways]
    rank_at = jnp.stack([rank]).astype(jnp.int32)

    def pairs(flow, low, high):
        out = []
        for q in range(queriers):
            way = 1 if (q % 2 == 0) == (flow == 0) else -1
            for t in range(parts):
                spot = t if way == 1 else parts - 1 - t
                if low <= spot <= min(high, parts - 2):
                    out.append((t * queriers + q, (t + way) * queriers + q))
        return out

    def where(flow, k):
        at = jnp.clip(rank + ways[flow] * (parts - k), 0, parts - 1)
        origin = jnp.clip(rank - ways[flow] * k, 0, parts - 1)
        return jnp.stack([at, spots[flow] <= k - 1, origin, spots[flow] >= k]).astype(jnp.int32)

    work, marks = [], []
    partials, totals, result = {}, {}, [None]

    def forward(c, h, piece, pieces, after):
        partials[c, h], mark = forward_piece(
            by_share, w_out, c, HALVES, h, piece, pieces, partials.get((c, h)), after
        )
        return mark

    def backward(c, blocks, total, last, piece, pieces, after):
        held = result[0] if last else totals.get(c)
        done, mark = backward_piece(
            blocks, w_out, c, chunks, HALVES, piece, pieces, total, last, held, after
        )
        if last:
            result[0] = done
        else:
            totals[c] = done
        return mark

    def do_one(x):
        if work:
            marks[:] = [work.pop(0)[1]([x])]

    def finish(key):
        while any(k == key for k, _ in work):
            marks[:] = [work.pop(0)[1](list(marks))]

    def add_forward(c, h, pieces):
        for piece in range(pieces):
            work.append(((c, h), functools.partial(forward, c, h, piece, pieces)))

    add_forward(0, 0, 1)
    finish((0, 0))
    in_rows = None
    grads = []
    for slot in range(chunks + 1):
        rs, ag = slot < chunks, slot > 0
        came, held, sent, marked, before = {}, {}, {}, {}, None
        if ag:
            grad = [None] * HALVES
            ins = [
                [partials[slot - 1, h], arrived[h, 0], arrived[h, 1], residual, out_grad, gain]
                for h in range(HALVES)
            ]
            sums = None
            for h in range(HALVES):
                extra = [in_rows] if slot == chunks and h == 0 else []
                sums = norm_sums(rank_at, ins[h], slot - 1, h, sums, list(marks) + extra)
            grad[0], held[0] = norm_out(rank_at, ins[0], slot - 1, 0, sums, w_out.shape[1], [])
        for k in range(parts):
            gather_now, reduce_now = ag and k <= parts - 2, rs and k >= 1
            if not gather_now and not reduce_now:
                continue
            for h in range(HALVES):
                if k == 0 and h > 0:
                    if rs:
                        add_forward(slot, h, PIECES)
                    for _ in range(PIECES):
                        do_one(sent[h - 1, 1])
                    grad[h], held[h] = norm_out(
                        rank_at, ins[h], slot - 1, h, sums, w_out.shape[1], list(marks)
                    )
                if reduce_now:
                    if slot == 0 and k == 1 and h > 0:
                        add_forward(0, h, 1)
                        marks[:] = [work.pop(0)[1]([sent[h - 1, 1]])]
                    finish((slot, h))
                for flow in range(2):
                    if k == 0:
                        x = grad[h]
                    elif (h, flow) not in came:
                        x = take_block(
                            partials[slot, h], jnp.clip(rank + ways[flow] * (parts - k), 0, parts - 1)
                        )
                    else:
                        after = list(marks) + ([] if before is None else [before])
                        if slot == 1 and k == 2 and h == 0 and flow == 0:
                            in_part = project_inputs(inputs.reshape(tokens, -1), proj_in, [before])
                            in_part = in_part.reshape(parts, share, -1)
                            in_rows = jnp.sum(
                                exchange(lambda at: take_block(in_part, at), "tensor", parts, rank).astype(F32),
                                axis=0,
                            )
                        x, held[h] = relay(
                            where(flow, k),
                            partials[slot, h] if reduce_now else None,
                            came[h, flow],
                            held.get(h),
                            after,
                        )
                        before = x
                    came[h, flow] = lax.ppermute(
                        x,
                        ("tensor", "query"),
                        pairs(flow, 0 if reduce_now else k, parts - 2 if gather_now else k - 1),
                    )
                    sent[h, flow] = x
                    marked[k] = x
                    if not (k == 0 or (slot == 0 and k == 1 and h == 0)):
                        do_one(x)
            if slot == 0 and k == 1:
                add_forward(1, 0, PIECES) if chunks > 1 else None
        if ag:
            grads.append(grad)
            if slot + 1 < chunks:
                add_forward(slot + 1, 0, PIECES)
            if rs:
                blocks = list(enumerate(held[h] for h in range(HALVES)))
                pieces = min(PIECES * HALVES, max(1, w_out.shape[0] // 128))
                for piece in range(pieces):
                    work.append(
                        (
                            ("b", slot - 1),
                            functools.partial(backward, slot - 1, blocks, None, True, piece, pieces),
                        )
                    )
            else:
                while work:
                    marks[:] = [work.pop(0)[1](list(marks))]
                for h in range(HALVES):
                    for flow in range(2):
                        _, held[h] = relay(where(flow, parts - 1), None, came[h, flow], held[h], list(marks))
                    backward(
                        slot - 1, [(h, held[h])], totals.get(slot - 1), h == HALVES - 1, 0, 1, list(marks)
                    )
        arrived = came
    input_grad = result[0].reshape(1, tokens, -1)

    out_rows = project_grads(grads, proj_out, [marked[1]])
    in_rows = in_rows.astype(F32)
    kp = out_rows.shape[1]
    segs = lax.dynamic_slice_in_dim(segment_ids[0], rank * share, share, 0)
    member = (segs[None, :] == jnp.arange(EX_DEV, dtype=jnp.int32)[:, None]).astype(F32)
    weighted = member[:, :, None] * out_rows[None]
    sketch_part = lax.dot_general(
        weighted,
        jnp.broadcast_to(in_rows[None], (EX_DEV,) + in_rows.shape),
        (((1,), (1,)), ((0,), (0,))),
        precision=lax.Precision.HIGHEST,
    )
    sketch_part = sketch_part.reshape(EX_DEV, parts, kp * kp // parts).astype(BF16)
    got = exchange(
        lambda at: lax.dynamic_index_in_dim(sketch_part, at, 1, keepdims=False), "tensor", parts, rank
    )
    sketch_cols = jnp.sum(tie(got, [marked[parts - 2]]).astype(F32), axis=0)
    paired = exchange(lambda at: sketch_cols, "query", queriers, q_rank)
    paired = tie(paired, [came[0, 0]]).reshape(queriers * EX_DEV, sketch_cols.shape[1])
    score_part = lax.dot_general(
        paired,
        queries.astype(F32),
        (((1,), (1,)), ((), ())),
        precision=lax.Precision.HIGHEST,
    )
    scores = jnp.sum(exchange(lambda at: score_part, "tensor", parts, rank), axis=0)
    return (input_grad, scores)


def solution(mesh):
    return jax.shard_map(
        body,
        mesh=mesh,
        in_specs=(
            P(("groups", "dp", "query"), None, "tensor"),
            P(("groups", "dp", "query"), "tensor", None),
            P(("groups", "dp", "query"), "tensor", None),
            P(),
            P("tensor", None),
            P(None, "tensor"),
            P(),
            P("query", "tensor"),
            P(("groups", "dp", "query"), None),
        ),
        out_specs=(P(("groups", "dp", "query"), None, "tensor"), P(("groups", "dp"), "query")),
        check_vma=False,
    )
```

time: 414 us -> 378 us (0.913)
  waiting for transfers between devices: 313 us -> 37.7 us
  Pallas kernels: 0 us -> 164 us
  starting transfers between devices: 0.16 us -> 133 us
  matrix products: 53.8 us -> 1.25 us
  local copies, waits for them, and re-layouts: 6.95 us -> 35.3 us
  blocking collectives: 19.4 us -> 0 us
  between operations: 13.9 us -> 2.29 us
  other arithmetic: 6.49 us -> 1.71 us
    pallas_call x0 -> x64, Pallas kernels: none -> 164 us  [the longest x10 55.4 us: backward_piece(): pl.pallas_call(kernel, grid=(steps,), in_specs=[pl.BlockSpec((parts, rows...]
    reduce_scatter x1 -> x0, waiting for transfers between devices: 144 us -> none  [body(): lax.psum_scatter(jnp.dot(tok_rows, w_out, preferred_element_type=jnp.floa...]
    ppermute x0 -> x50, starting transfers between devices: none -> 133 us  [the longest x40 99.5 us: body(): lax.ppermute(x, ('tensor', 'query'), pairs(flow, 0 if reduce_now else k,...]
    all_gather x1 -> x0, waiting for transfers between devices: 129 us -> none  [body(): dproj_all = lax.all_gather(dproj_rows, 'tensor', axis=0, tiled=True)]
    dot_general x6 -> x2, matrix products: 53.8 us -> 1.25 us  [the longest x1 0.92 us: body(): lax.dot_general(paired, queries.astype(F32), (((1,), (1,)), ((), ())), pr...]
    unnamed x6 -> x0, waiting for transfers between devices: 40.1 us -> none
    ppermute x0 -> x50, waiting for transfers between devices: none -> 37.7 us  [the longest x40 23.6 us: body(): lax.ppermute(x, ('tensor', 'query'), pairs(flow, 0 if reduce_now else k,...]
    unnamed x24 -> x183, local copies, waits for them, and re-layouts: 5.96 us -> 31.1 us
  transfers between devices with their start and end apart: 4 -> 50, of which waited for: 4 -> 10; matrix products, arithmetic and copies ran while one was open for 3% -> 1% of each run, Pallas kernels for 0% -> 39%
where the time goes in v3:
time: 378 us; the launch traced here: 375 us
  Pallas kernels  164 us (43%)
  starting transfers between devices  133 us (35%)
  waiting for transfers between devices  37.7 us (10%)
  local copies, waits for them, and re-layouts  35.3 us (9%)
    ppermute x40, starting transfers between devices, body(): lax.ppermute(x, ('tensor', 'query'), pairs(flow, 0 if reduce_now else k,...  99.5 us
    pallas_call x10, Pallas kernels, backward_piece(): pl.pallas_call(kernel, grid=(steps,), in_specs=[pl.BlockSpec((parts, rows...  55.4 us
    pallas_call x32, Pallas kernels, relay(): pl.pallas_call(kernel, grid_spec=pltpu.PrefetchScalarGridSpec(num_scalar_...  50 us
    pallas_call x10, Pallas kernels, forward_piece(): pl.pallas_call(kernel, grid=(steps,), in_specs=[pl.BlockSpec((parts, None...  47.4 us
    ppermute x10, starting transfers between devices, exchange(): lax.ppermute(value_of((rank + shift) % size), axis, [(d, (d + shift) % si...  33.9 us
    unnamed x183, local copies, waits for them, and re-layouts  31.1 us
    ppermute x40, waiting for transfers between devices, body(): lax.ppermute(x, ('tensor', 'query'), pairs(flow, 0 if reduce_now else k,...  23.6 us
    ppermute x10, waiting for transfers between devices, exchange(): lax.ppermute(value_of((rank + shift) % size), axis, [(d, (d + shift) % si...  14 us
  transfers between devices with their start and end apart: 50, of which 10 were waited for; matrix products, arithmetic and copies ran while one was open for 1% of the time, Pallas kernels for 39%

profile of v3, /device:TPU:0, one launch (start us, length us, event | category | flops | bytes accessed | tf_op | source)
XLA Modules:
  0.0 375.4 jit_solution(3567885813627952381)
XLA Ops:
  2.3 10.8 %forward_piece.10 = (bf16[4,64,4096]{2,1,0:T(8,128)(2,1)S(1)}, f32[8,128]{1,0:T(8,128)}) custom-call(bf16[4,2,64,2048]{3,2,1,0:T(8,128)(2,1)S(1)} %bitcast.84, bf16[2048,8192]{1,0:T(8,128)(2,1)} %refs_4_.36, bf16[2048,8192]{1,0:T(8,128)(2,1)} %refs_4_.36, bf16[2048,8192]{1,0:T(8,128)(2,1)} %refs_4_.36, bf16[2048,8192]{1,0:T(8,128)(2,1)} %refs_4_.36), custom_call_target="tpu_custom_call" | custom-call | bytes 720000 | tf_op jit(solution)/shard_map/forward_piece/pallas_call | solution.py:85
  14.4 5.7 %collective-permute-start = (bf16[64,4096]{1,0:T(8,128)(2,1)}, bf16[64,4096]{1,0:T(8,128)(2,1)}, u32[]{:S(2)}, u32[]{:S(2)}) collective-permute-start(bf16[64,4096]{1,0:T(8,128)(2,1)} %get-tuple-element.187), channel_id=1, source_target_pairs={{0,4},{13,9},{2,6},{15,11},{16,20},{29,25},{18,22},{31,27}} | collective-permute-start | bytes 1572872 | tf_op jit(solution)/shard_map/ppermute | solution.py:484
  21.6 10.2 %forward_piece.11 = (bf16[4,64,4096]{2,1,0:T(8,128)(2,1)S(1)}, f32[8,128]{1,0:T(8,128)S(1)}) custom-call(bf16[4,2,64,2048]{3,2,1,0:T(8,128)(2,1)S(1)} %bitcast.85, bf16[2048,8192]{1,0:T(8,128)(2,1)} %refs_4_.36, bf16[2048,8192]{1,0:T(8,128)(2,1)} %refs_4_.36, bf16[2048,8192]{1,0:T(8,128)(2,1)} %refs_4_.36, bf16[2048,8192]{1,0:T(8,128)(2,1)} %refs_4_.36, ...), custom_call_target="tpu_custom_call" | custom-call | bytes 720000 | tf_op jit(solution)/shard_map/forward_piece/pallas_call | solution.py:85
  78.5 4.6 %collective-permute-start.5 = (bf16[64,4096]{1,0:T(8,128)(2,1)S(1)}, bf16[64,4096]{1,0:T(8,128)(2,1)S(1)}, u32[]{:S(2)}, u32[]{:S(2)}) collective-permute-start(bf16[64,4096]{1,0:T(8,128)(2,1)S(1)} %relay.36.refs_3_), channel_id=1, source_target_pairs={{0,4},{4,8},{8,12},{5,1},{9,5},{13,9},{2,6},{6,10},{10,14},{7,3},{... | collective-permute-start | bytes 1572872 | tf_op jit(solution)/shard_map/ppermute | solution.py:484
  88.0 4.6 %collective-permute-start.9 = (bf16[64,4096]{1,0:T(8,128)(2,1)S(1)}, bf16[64,4096]{1,0:T(8,128)(2,1)S(1)}, u32[]{:S(2)}, u32[]{:S(2)}) collective-permute-start(bf16[64,4096]{1,0:T(8,128)(2,1)S(1)} %relay.38.refs_3_), channel_id=1, source_target_pairs={{0,4},{4,8},{8,12},{5,1},{9,5},{13,9},{2,6},{6,10},{10,14},{7,3},{... | collective-permute-start | bytes 1572872 | tf_op jit(solution)/shard_map/ppermute | solution.py:484
  94.4 9.1 %collective-permute-done.11.refs_2_ = bf16[64,4096]{1,0:T(8,128)(2,1)S(1)} collective-permute-done((bf16[64,4096]{1,0:T(8,128)(2,1)S(1)}, bf16[64,4096]{1,0:T(8,128)(2,1)S(1)}, u32[]{:S(2)}, u32[]{:S(2)}) %collective-permute-start.11) | collective-permute-done | bytes 524320 | tf_op jit(solution)/shard_map/ppermute | solution.py:484
  109.7 6.2 %collective-permute-start.14 = (bf16[64,4096]{1,0:T(8,128)(2,1)}, bf16[64,4096]{1,0:T(8,128)(2,1)}, u32[]{:S(2)}, u32[]{:S(2)}) collective-permute-start(bf16[64,4096]{1,0:T(8,128)(2,1)} %get-tuple-element.107.refs_4_.refs_5_.refs_0_), channel_id=1, source_target_pairs={{0,4},{4,8},{8,12},{5,1},{9,5},{13,9},{2,6},{6,10},{10,14},{7,3},{... | collective-permute-start | bytes 1572872 | tf_op jit(solution)/shard_map/ppermute | solution.py:484
  132.0 5.4 %collective-permute-start.12 = (bf16[64,4096]{1,0:T(8,128)(2,1)}, bf16[64,4096]{1,0:T(8,128)(2,1)}, u32[]{:S(2)}, u32[]{:S(2)}) collective-permute-start(bf16[64,4096]{1,0:T(8,128)(2,1)} %get-tuple-element.113.refs_1_), channel_id=1, source_target_pairs={{0,4},{4,8},{8,12},{5,1},{9,5},{13,9},{2,6},{6,10},{10,14},{7,3},{... | collective-permute-start | bytes 1572872 | tf_op jit(solution)/shard_map/ppermute | solution.py:484
  142.2 4.5 %collective-permute-start.18 = (bf16[64,4096]{1,0:T(8,128)(2,1)S(1)}, bf16[64,4096]{1,0:T(8,128)(2,1)S(1)}, u32[]{:S(2)}, u32[]{:S(2)}) collective-permute-start(bf16[64,4096]{1,0:T(8,128)(2,1)S(1)} %get-tuple-element.118.refs_4_), channel_id=1, source_target_pairs={{0,4},{4,8},{8,12},{5,1},{9,5},{13,9},{2,6},{6,10},{10,14},{7,3},{... | collective-permute-start | bytes 1572872 | tf_op jit(solution)/shard_map/ppermute | solution.py:484
  151.7 4.5 %collective-permute-start.15 = (bf16[64,4096]{1,0:T(8,128)(2,1)S(1)}, bf16[64,4096]{1,0:T(8,128)(2,1)S(1)}, u32[]{:S(2)}, u32[]{:S(2)}) collective-permute-start(bf16[64,4096]{1,0:T(8,128)(2,1)S(1)} %get-tuple-element.120.refs_4_), channel_id=1, source_target_pairs={{0,4},{4,8},{8,12},{5,1},{9,5},{13,9},{2,6},{6,10},{10,14},{7,3},{... | collective-permute-start | bytes 1572872 | tf_op jit(solution)/shard_map/ppermute | solution.py:484
  161.3 5.2 %collective-permute-start.22 = (bf16[64,4096]{1,0:T(8,128)(2,1)}, bf16[64,4096]{1,0:T(8,128)(2,1)}, u32[]{:S(2)}, u32[]{:S(2)}) collective-permute-start(bf16[64,4096]{1,0:T(8,128)(2,1)} %get-tuple-element.126.refs_4_), channel_id=1, source_target_pairs={{0,4},{4,8},{8,12},{5,1},{9,5},{13,9},{2,6},{6,10},{10,14},{7,3},{... | collective-permute-start | bytes 1572872 | tf_op jit(solution)/shard_map/ppermute | solution.py:484
  172.6 5.2 %collective-permute-start.19 = (bf16[64,4096]{1,0:T(8,128)(2,1)}, bf16[64,4096]{1,0:T(8,128)(2,1)}, u32[]{:S(2)}, u32[]{:S(2)}) collective-permute-start(bf16[64,4096]{1,0:T(8,128)(2,1)} %get-tuple-element.128.refs_4_), channel_id=1, source_target_pairs={{0,4},{4,8},{8,12},{5,1},{9,5},{13,9},{2,6},{6,10},{10,14},{7,3},{... | collective-permute-start | bytes 1572872 | tf_op jit(solution)/shard_map/ppermute | solution.py:484
  188.1 8.2 %collective-permute-done.28 = bf16[128,64]{1,0:T(8,128)(2,1)S(1)} collective-permute-done((bf16[128,64]{1,0:T(8,128)(2,1)S(1)}, bf16[128,64]{1,0:T(8,128)(2,1)S(1)}, u32[]{:S(2)}, u32[]{:S(2)}) %collective-permute-start.28) | collective-permute-done | bytes 16416 | tf_op jit(solution)/shard_map/ppermute | solution.py:352
  207.5 4.6 %collective-permute-start.23 = (bf16[64,4096]{1,0:T(8,128)(2,1)S(1)}, bf16[64,4096]{1,0:T(8,128)(2,1)S(1)}, u32[]{:S(2)}, u32[]{:S(2)}) collective-permute-start(bf16[64,4096]{1,0:T(8,128)(2,1)S(1)} %get-tuple-element.136.refs_4_), channel_id=1, source_target_pairs={{0,4},{4,8},{8,12},{5,1},{9,5},{13,9},{2,6},{6,10},{10,14},{7,3},{... | collective-permute-start | bytes 1572872 | tf_op jit(solution)/shard_map/ppermute | solution.py:484
  219.0 8.5 %collective-permute-done.25.refs_2_ = bf16[64,4096]{1,0:T(8,128)(2,1)S(1)} collective-permute-done((bf16[64,4096]{1,0:T(8,128)(2,1)S(1)}, bf16[64,4096]{1,0:T(8,128)(2,1)S(1)}, u32[]{:S(2)}, u32[]{:S(2)}) %collective-permute-start.25) | collective-permute-done | bytes 524320 | tf_op jit(solution)/shard_map/ppermute | solution.py:484
  246.8 4.3 %backward_piece.13 = (bf16[4,2,64,2048]{3,2,1,0:T(8,128)(2,1)}, f32[8,128]{1,0:T(8,128)S(1)}) custom-call(bf16[4,64,4096]{2,1,0:T(8,128)(2,1)S(1)} %get-tuple-element.143.refs_0_, bf16[4,64,4096]{2,1,0:T(8,128)(2,1)S(1)} %get-tuple-element.144.refs_1_, bf16[2048,8192]{1,0:T(8,128)(2,1)} %refs_4_.36, ...), custom_call_target="tpu_custom_call", output_to_operand_aliasing={{0}: (10, {})} | custom-call | bytes 720000 | tf_op jit(solution)/shard_map/backward_piece/pallas_call | solution.py:136
  253.9 5.4 %collective-permute-start.32 = (bf16[64,4096]{1,0:T(8,128)(2,1)}, bf16[64,4096]{1,0:T(8,128)(2,1)}, u32[]{:S(2)}, u32[]{:S(2)}) collective-permute-start(bf16[64,4096]{1,0:T(8,128)(2,1)} %get-tuple-element.150.refs_3_), channel_id=1, source_target_pairs={{0,4},{4,8},{8,12},{5,1},{9,5},{13,9},{2,6},{6,10},{10,14},{7,3},{... | collective-permute-start | bytes 1572872 | tf_op jit(solution)/shard_map/ppermute | solution.py:484
  273.4 4.3 %backward_piece.15 = (bf16[4,2,64,2048]{3,2,1,0:T(8,128)(2,1)}, f32[8,128]{1,0:T(8,128)S(1)}) custom-call(bf16[4,64,4096]{2,1,0:T(8,128)(2,1)S(1)} %get-tuple-element.143.refs_0_, bf16[4,64,4096]{2,1,0:T(8,128)(2,1)S(1)} %copy-done.6, bf16[2048,8192]{1,0:T(8,128)(2,1)} %refs_4_.36, bf16[2048,8192]{1,0:T(8,128)(2,1)} %refs_4_.36, ...), custom_call_target="tpu_custom_call", output_to_operand_aliasing={{0}: (10, {})} | custom-call | bytes 720000 | tf_op jit(solution)/shard_map/backward_piece/pallas_call | solution.py:136
  291.3 11.7 %collective-permute-start.43 = (bf16[4,1024]{1,0:T(4,128)(2,1)S(1)}, bf16[4,1024]{1,0:T(4,128)(2,1)S(1)}, u32[]{:S(2)}, u32[]{:S(2)}) collective-permute-start(bf16[4,1024]{1,0:T(4,128)(2,1)S(1)} %bitcast.98), channel_id=1, source_target_pairs={{0,4},{4,8},{8,12},{12,0},{1,5},{5,9},{9,13},{13,1},{2,6},{6,10},{... | collective-permute-start | bytes 24584 | tf_op jit(solution)/shard_map/ppermute | solution.py:352
  304.6 4.2 %backward_piece.17 = (bf16[4,2,64,2048]{3,2,1,0:T(8,128)(2,1)}, f32[8,128]{1,0:T(8,128)S(1)}) custom-call(bf16[4,64,4096]{2,1,0:T(8,128)(2,1)S(1)} %get-tuple-element.143.refs_0_, bf16[4,64,4096]{2,1,0:T(8,128)(2,1)S(1)} %copy-done.7, bf16[2048,8192]{1,0:T(8,128)(2,1)} %refs_4_.36, bf16[2048,8192]{1,0:T(8,128)(2,1)} %refs_4_.36, ...), custom_call_target="tpu_custom_call", output_to_operand_aliasing={{0}: (10, {})} | custom-call | bytes 720000 | tf_op jit(solution)/shard_map/backward_piece/pallas_call | solution.py:136
  330.1 4.2 %collective-permute-start.47 = (f32[8,512]{1,0:T(8,128)S(1)}, f32[8,512]{1,0:T(8,128)S(1)}, u32[]{:S(2)}, u32[]{:S(2)}) collective-permute-start(f32[8,512]{1,0:T(8,128)S(1)} %get-tuple-element.197), channel_id=1, source_target_pairs={{0,4},{4,8},{8,12},{12,0},{1,5},{5,9},{9,13},{13,1},{2,6},{6,10},{... | collective-permute-start | bytes 49160 | tf_op jit(solution)/shard_map/ppermute | solution.py:352
  334.4 7.7 %collective-permute-start.48 = (f32[8,512]{1,0:T(8,128)S(1)}, f32[8,512]{1,0:T(8,128)S(1)}, u32[]{:S(2)}, u32[]{:S(2)}) collective-permute-start(f32[8,512]{1,0:T(8,128)S(1)} %get-tuple-element.197), channel_id=1, source_target_pairs={{0,8},{4,12},{8,0},{12,4},{1,9},{5,13},{9,1},{13,5},{2,10},{6,14},... | collective-permute-start | bytes 49160 | tf_op jit(solution)/shard_map/ppermute | solution.py:352
  350.5 10.9 %backward_piece.18 = (f32[4,64,2048]{2,1,0:T(8,128)S(1)}, f32[8,128]{1,0:T(8,128)}) custom-call(bf16[4,64,4096]{2,1,0:T(8,128)(2,1)S(1)} %copy-done.39, bf16[2048,8192]{1,0:T(8,128)(2,1)} %refs_4_.36, bf16[2048,8192]{1,0:T(8,128)(2,1)} %refs_4_.36, bf16[2048,8192]{1,0:T(8,128)(2,1)} %refs_4_.36, bf16[2048,8192]{1,0:T(8,128)(2,1)} %refs_4_.36, ...), custom_call_target="tpu_custom_call" | custom-call | bytes 720000 | tf_op jit(solution)/shard_map/backward_piece/pallas_call | solution.py:136
  363.6 11.2 %backward_piece.19 = (bf16[4,2,64,2048]{3,2,1,0:T(8,128)(2,1)}, f32[8,128]{1,0:T(8,128)}) custom-call(bf16[4,64,4096]{2,1,0:T(8,128)(2,1)S(1)} %get-tuple-element.177.refs_0_, bf16[2048,8192]{1,0:T(8,128)(2,1)} %refs_4_.36, bf16[2048,8192]{1,0:T(8,128)(2,1)} %refs_4_.36, bf16[2048,8192]{1,0:T(8,128)(2,1)} %refs_4_.36, ...), custom_call_target="tpu_custom_call", output_to_operand_aliasing={{0}: (6, {})} | custom-call | bytes 720000 | tf_op jit(solution)/shard_map/backward_piece/pallas_call | solution.py:136
  (361 shorter events, 211.9 us)
Async XLA Ops:
  20.1 27.3 %collective-permute-start.2 = (bf16[64,4096]{1,0:T(8,128)(2,1)}, bf16[64,4096]{1,0:T(8,128)(2,1)}, u32[]{:S(2)}, u32[]{:S(2)}) collective-permute-start(bf16[64,4096]{1,0:T(8,128)(2,1)} %get-tuple-element.186.refs_4_), channel_id=1, source_target_pairs={{12,8},{1,5},{14,10},{3,7},{28,24},{17,21},{30,26},{19,23}} | collective-permute-start | bytes 1572872 | tf_op jit(solution)/shard_map/ppermute | solution.py:484
  36.6 26.9 %collective-permute-start.4 = (bf16[64,4096]{1,0:T(8,128)(2,1)}, bf16[64,4096]{1,0:T(8,128)(2,1)}, u32[]{:S(2)}, u32[]{:S(2)}) collective-permute-start(bf16[64,4096]{1,0:T(8,128)(2,1)} %get-tuple-element.184), channel_id=1, source_target_pairs={{12,8},{1,5},{14,10},{3,7},{28,24},{17,21},{30,26},{19,23}} | collective-permute-start | bytes 1572872 | tf_op jit(solution)/shard_map/ppermute | solution.py:484
  45.4 28.4 %collective-permute-start.1 = (bf16[64,4096]{1,0:T(8,128)(2,1)}, bf16[64,4096]{1,0:T(8,128)(2,1)}, u32[]{:S(2)}, u32[]{:S(2)}) collective-permute-start(bf16[64,4096]{1,0:T(8,128)(2,1)} %relay.32.refs_4_.refs_3_), channel_id=1, source_target_pairs={{0,4},{4,8},{9,5},{13,9},{2,6},{6,10},{11,7},{15,11},{16,20},{20,2... | collective-permute-start | bytes 1572872 | tf_op jit(solution)/shard_map/ppermute | solution.py:484
  49.9 25.6 %collective-permute-start.6 = (bf16[64,4096]{1,0:T(8,128)(2,1)}, bf16[64,4096]{1,0:T(8,128)(2,1)}, u32[]{:S(2)}, u32[]{:S(2)}) collective-permute-start(bf16[64,4096]{1,0:T(8,128)(2,1)} %relay.33.refs_5_.refs_3_), channel_id=1, source_target_pairs={{8,4},{12,8},{1,5},{5,9},{10,6},{14,10},{3,7},{7,11},{24,20},{28,2... | collective-permute-start | bytes 1572872 | tf_op jit(solution)/shard_map/ppermute | solution.py:484
  57.1 26.0 %collective-permute-start.8 = (bf16[64,4096]{1,0:T(8,128)(2,1)}, bf16[64,4096]{1,0:T(8,128)(2,1)}, u32[]{:S(2)}, u32[]{:S(2)}) collective-permute-start(bf16[64,4096]{1,0:T(8,128)(2,1)} %relay.34.refs_5_.refs_3_), channel_id=1, source_target_pairs={{0,4},{4,8},{9,5},{13,9},{2,6},{6,10},{11,7},{15,11},{16,20},{20,2... | collective-permute-start | bytes 1572872 | tf_op jit(solution)/shard_map/ppermute | solution.py:484
  109.7 29.1 %collective-permute-start.14 = (bf16[64,4096]{1,0:T(8,128)(2,1)}, bf16[64,4096]{1,0:T(8,128)(2,1)}, u32[]{:S(2)}, u32[]{:S(2)}) collective-permute-start(bf16[64,4096]{1,0:T(8,128)(2,1)} %get-tuple-element.107.refs_4_.refs_5_.refs_0_), channel_id=1, source_target_pairs={{0,4},{4,8},{8,12},{5,1},{9,5},{13,9},{2,6},{6,10},{10,14},{7,3},{... | collective-permute-start | bytes 1572872 | tf_op jit(solution)/shard_map/ppermute | solution.py:484
  116.0 30.7 %collective-permute-start.13 = (bf16[64,4096]{1,0:T(8,128)(2,1)}, bf16[64,4096]{1,0:T(8,128)(2,1)}, u32[]{:S(2)}, u32[]{:S(2)}) collective-permute-start(bf16[64,4096]{1,0:T(8,128)(2,1)} %get-tuple-element.107.refs_4_.refs_5_.refs_0_), channel_id=1, source_target_pairs={{4,0},{8,4},{12,8},{1,5},{5,9},{9,13},{6,2},{10,6},{14,10},{3,7},{... | collective-permute-start | bytes 1572872 | tf_op jit(solution)/shard_map/ppermute | solution.py:484
  161.3 35.4 %collective-permute-start.22 = (bf16[64,4096]{1,0:T(8,128)(2,1)}, bf16[64,4096]{1,0:T(8,128)(2,1)}, u32[]{:S(2)}, u32[]{:S(2)}) collective-permute-start(bf16[64,4096]{1,0:T(8,128)(2,1)} %get-tuple-element.126.refs_4_), channel_id=1, source_target_pairs={{0,4},{4,8},{8,12},{5,1},{9,5},{13,9},{2,6},{6,10},{10,14},{7,3},{... | collective-permute-start | bytes 1572872 | tf_op jit(solution)/shard_map/ppermute | solution.py:484
  168.0 32.9 %collective-permute-start.21 = (bf16[64,4096]{1,0:T(8,128)(2,1)}, bf16[64,4096]{1,0:T(8,128)(2,1)}, u32[]{:S(2)}, u32[]{:S(2)}) collective-permute-start(bf16[64,4096]{1,0:T(8,128)(2,1)} %get-tuple-element.127.refs_4_), channel_id=1, source_target_pairs={{4,0},{8,4},{12,8},{1,5},{5,9},{9,13},{6,2},{10,6},{14,10},{3,7},{... | collective-permute-start | bytes 1572872 | tf_op jit(solution)/shard_map/ppermute | solution.py:484
  172.6 31.9 %collective-permute-start.19 = (bf16[64,4096]{1,0:T(8,128)(2,1)}, bf16[64,4096]{1,0:T(8,128)(2,1)}, u32[]{:S(2)}, u32[]{:S(2)}) collective-permute-start(bf16[64,4096]{1,0:T(8,128)(2,1)} %get-tuple-element.128.refs_4_), channel_id=1, source_target_pairs={{0,4},{4,8},{8,12},{5,1},{9,5},{13,9},{2,6},{6,10},{10,14},{7,3},{... | collective-permute-start | bytes 1572872 | tf_op jit(solution)/shard_map/ppermute | solution.py:484
  180.5 27.0 %collective-permute-start.24 = (bf16[64,4096]{1,0:T(8,128)(2,1)}, bf16[64,4096]{1,0:T(8,128)(2,1)}, u32[]{:S(2)}, u32[]{:S(2)}) collective-permute-start(bf16[64,4096]{1,0:T(8,128)(2,1)} %get-tuple-element.132.refs_4_), channel_id=1, source_target_pairs={{4,0},{8,4},{12,8},{1,5},{5,9},{9,13},{6,2},{10,6},{14,10},{3,7},{... | collective-permute-start | bytes 1572872 | tf_op jit(solution)/shard_map/ppermute | solution.py:484
  230.0 32.5 %collective-permute-start.33 = (bf16[64,4096]{1,0:T(8,128)(2,1)}, bf16[64,4096]{1,0:T(8,128)(2,1)}, u32[]{:S(2)}, u32[]{:S(2)}) collective-permute-start(bf16[64,4096]{1,0:T(8,128)(2,1)} %get-tuple-element.145.refs_10_.refs_11_.refs_2_), channel_id=1, source_target_pairs={{0,4},{4,8},{8,12},{5,1},{9,5},{13,9},{2,6},{6,10},{10,14},{7,3},{... | collective-permute-start | bytes 1572872 | tf_op jit(solution)/shard_map/ppermute | solution.py:484
  233.1 37.3 %collective-permute-start.34 = (bf16[64,4096]{1,0:T(8,128)(2,1)}, bf16[64,4096]{1,0:T(8,128)(2,1)}, u32[]{:S(2)}, u32[]{:S(2)}) collective-permute-start(bf16[64,4096]{1,0:T(8,128)(2,1)} %get-tuple-element.145.refs_10_.refs_11_.refs_2_), channel_id=1, source_target_pairs={{4,0},{8,4},{12,8},{1,5},{5,9},{9,13},{6,2},{10,6},{14,10},{3,7},{... | collective-permute-start | bytes 1572872 | tf_op jit(solution)/shard_map/ppermute | solution.py:484
  259.2 24.6 %collective-permute-start.31 = (bf16[64,4096]{1,0:T(8,128)(2,1)}, bf16[64,4096]{1,0:T(8,128)(2,1)}, u32[]{:S(2)}, u32[]{:S(2)}) collective-permute-start(bf16[64,4096]{1,0:T(8,128)(2,1)} %get-tuple-element.150.refs_3_), channel_id=1, source_target_pairs={{4,0},{8,4},{12,8},{1,5},{5,9},{9,13},{6,2},{10,6},{14,10},{3,7},{... | collective-permute-start | bytes 1572872 | tf_op jit(solution)/shard_map/ppermute | solution.py:484
  264.8 52.9 %collective-permute-start.38 = (bf16[64,4096]{1,0:T(8,128)(2,1)}, bf16[64,4096]{1,0:T(8,128)(2,1)}, u32[]{:S(2)}, u32[]{:S(2)}) collective-permute-start(bf16[64,4096]{1,0:T(8,128)(2,1)} %get-tuple-element.154.refs_11_.refs_3_), channel_id=1, source_target_pairs={{4,8},{8,12},{5,1},{9,5},{6,10},{10,14},{7,3},{11,7},{20,24},{24,2... | collective-permute-start | bytes 1572872 | tf_op jit(solution)/shard_map/ppermute | solution.py:484
  272.1 47.1 %collective-permute-start.37 = (bf16[64,4096]{1,0:T(8,128)(2,1)}, bf16[64,4096]{1,0:T(8,128)(2,1)}, u32[]{:S(2)}, u32[]{:S(2)}) collective-permute-start(bf16[64,4096]{1,0:T(8,128)(2,1)} %get-tuple-element.158.refs_11_.refs_3_), channel_id=1, source_target_pairs={{4,0},{8,4},{5,9},{9,13},{6,2},{10,6},{7,11},{11,15},{20,16},{24,2... | collective-permute-start | bytes 1572872 | tf_op jit(solution)/shard_map/ppermute | solution.py:484
  278.2 43.8 %collective-permute-start.36 = (bf16[64,4096]{1,0:T(8,128)(2,1)}, bf16[64,4096]{1,0:T(8,128)(2,1)}, u32[]{:S(2)}, u32[]{:S(2)}) collective-permute-start(bf16[64,4096]{1,0:T(8,128)(2,1)} %get-tuple-element.162.refs_11_.refs_3_), channel_id=1, source_target_pairs={{4,8},{8,12},{5,1},{9,5},{6,10},{10,14},{7,3},{11,7},{20,24},{24,2... | collective-permute-start | bytes 1572872 | tf_op jit(solution)/shard_map/ppermute | solution.py:484
  286.8 37.4 %collective-permute-start.35 = (bf16[64,4096]{1,0:T(8,128)(2,1)}, bf16[64,4096]{1,0:T(8,128)(2,1)}, u32[]{:S(2)}, u32[]{:S(2)}) collective-permute-start(bf16[64,4096]{1,0:T(8,128)(2,1)} %get-tuple-element.164.refs_11_.refs_3_.refs_5_), channel_id=1, source_target_pairs={{4,0},{8,4},{5,9},{9,13},{6,2},{10,6},{7,11},{11,15},{20,16},{24,2... | collective-permute-start | bytes 1572872 | tf_op jit(solution)/shard_map/ppermute | solution.py:484
  320.8 24.5 %collective-permute-start.41 = (bf16[64,4096]{1,0:T(8,128)(2,1)}, bf16[64,4096]{1,0:T(8,128)(2,1)}, u32[]{:S(2)}, u32[]{:S(2)}) collective-permute-start(bf16[64,4096]{1,0:T(8,128)(2,1)} %get-tuple-element.171.refs_3_), channel_id=1, source_target_pairs={{4,0},{9,13},{6,2},{11,15},{20,16},{25,29},{22,18},{27,31}} | collective-permute-start | bytes 1572872 | tf_op jit(solution)/shard_map/ppermute | solution.py:484
  322.7 38.7 %collective-permute-start.40 = (bf16[64,4096]{1,0:T(8,128)(2,1)}, bf16[64,4096]{1,0:T(8,128)(2,1)}, u32[]{:S(2)}, u32[]{:S(2)}) collective-permute-start(bf16[64,4096]{1,0:T(8,128)(2,1)} %get-tuple-element.173.refs_3_), channel_id=1, source_target_pairs={{8,12},{5,1},{10,14},{7,3},{24,28},{21,17},{26,30},{23,19}} | collective-permute-start | bytes 1572872 | tf_op jit(solution)/shard_map/ppermute | solution.py:484
  325.8 36.2 %collective-permute-start.39 = (bf16[64,4096]{1,0:T(8,128)(2,1)}, bf16[64,4096]{1,0:T(8,128)(2,1)}, u32[]{:S(2)}, u32[]{:S(2)}) collective-permute-start(bf16[64,4096]{1,0:T(8,128)(2,1)} %get-tuple-element.174.refs_0_), channel_id=1, source_target_pairs={{4,0},{9,13},{6,2},{11,15},{20,16},{25,29},{22,18},{27,31}} | collective-permute-start | bytes 1572872 | tf_op jit(solution)/shard_map/ppermute | solution.py:484
  330.1 44.6 %collective-permute-start.47 = (f32[8,512]{1,0:T(8,128)S(1)}, f32[8,512]{1,0:T(8,128)S(1)}, u32[]{:S(2)}, u32[]{:S(2)}) collective-permute-start(f32[8,512]{1,0:T(8,128)S(1)} %get-tuple-element.197), channel_id=1, source_target_pairs={{0,4},{4,8},{8,12},{12,0},{1,5},{5,9},{9,13},{13,1},{2,6},{6,10},{... | collective-permute-start | bytes 49160 | tf_op jit(solution)/shard_map/ppermute | solution.py:352
  334.4 40.4 %collective-permute-start.48 = (f32[8,512]{1,0:T(8,128)S(1)}, f32[8,512]{1,0:T(8,128)S(1)}, u32[]{:S(2)}, u32[]{:S(2)}) collective-permute-start(f32[8,512]{1,0:T(8,128)S(1)} %get-tuple-element.197), channel_id=1, source_target_pairs={{0,8},{4,12},{8,0},{12,4},{1,9},{5,13},{9,1},{13,5},{2,10},{6,14},... | collective-permute-start | bytes 49160 | tf_op jit(solution)/shard_map/ppermute | solution.py:352
  345.3 29.5 %collective-permute-start.49 = (f32[8,512]{1,0:T(8,128)S(1)}, f32[8,512]{1,0:T(8,128)S(1)}, u32[]{:S(2)}, u32[]{:S(2)}) collective-permute-start(f32[8,512]{1,0:T(8,128)S(1)} %get-tuple-element.197), channel_id=1, source_target_pairs={{0,12},{4,0},{8,4},{12,8},{1,13},{5,1},{9,5},{13,9},{2,14},{6,2},{... | collective-permute-start | bytes 49160 | tf_op jit(solution)/shard_map/ppermute | solution.py:352
  (116 other events, 1253.3 us)

commit v4 on v3

v4 whole, which is shorter than its diff:
```python
import functools

import jax
import jax.numpy as jnp
from jax import lax
from jax.experimental import pallas as pl
from jax.experimental.pallas import tpu as pltpu
from jax.sharding import PartitionSpec as P

EX_DEV = 4
EPS = 1e-05
CHUNKS = 2
HALVES = 2
PIECES = 2
SPLIT = 4
SHORT, LONG = 0.2, 5.0
LIMIT = 28 * 1024 * 1024

F32, BF16 = jnp.float32, jnp.bfloat16
ANY = pl.BlockSpec(memory_space=pl.ANY)
TOKEN = jax.ShapeDtypeStruct((8, 128), F32)
TOKEN_SPEC = pl.BlockSpec((8, 128), lambda *_: (0, 0))


def divisor(total, wanted):
    size = min(total, wanted)
    while total % size:
        size //= 2
    return size


def cost(microseconds):
    return pl.CostEstimate(flops=0, bytes_accessed=int(microseconds * 3.6e6), transcendentals=0)


def project_rows(values, matrix):
    return lax.dot_general(
        values, matrix, (((1,), (1,)), ((), ())), preferred_element_type=F32
    )


def spread(values, first):
    k = values.shape[1]
    row = lax.broadcasted_iota(jnp.int32, (k, 2 * k), 0)
    col = lax.broadcasted_iota(jnp.int32, (k, 2 * k), 1)
    return jnp.dot(values, jnp.where(col == row + first, 1.0, 0.0).astype(BF16), preferred_element_type=F32)


def forward_extra(by_share, proj_in, chunk, held, after):
    parts, _, rows, depth = by_share.shape
    extra = 2 * proj_in.shape[0]
    at = held.shape[2] // extra - 1

    def kernel(x_ref, p_ref, *refs):
        part = project_rows(x_ref[...].reshape(parts * rows, depth), p_ref[...]).astype(BF16)
        refs[-1][...] = spread(part, 0).astype(BF16).reshape(parts, rows, extra)

    return pl.pallas_call(
        kernel,
        grid=(1,),
        in_specs=[
            pl.BlockSpec((parts, None, rows, depth), lambda i: (0, chunk, 0, 0)),
            pl.BlockSpec(proj_in.shape, lambda i: (0, 0)),
        ]
        + [ANY] * (1 + len(after)),
        out_specs=pl.BlockSpec((parts, rows, extra), lambda i: (0, 0, at)),
        out_shape=jax.ShapeDtypeStruct(held.shape, BF16),
        input_output_aliases={2: 0},
        compiler_params=pltpu.CompilerParams(vmem_limit_bytes=LIMIT),
        cost_estimate=cost(SHORT),
        name="forward_extra",
    )(by_share, proj_in, held, *after)


def forward_piece(by_share, w_out, chunk, halves, half_at, extra, piece, pieces, held, after):
    parts, _, rows, depth = by_share.shape
    half = w_out.shape[1] // halves
    span = half // pieces
    cols = divisor(span, 512)
    steps = span // cols
    base = (half_at * half + piece * span) // cols
    cut = depth // SPLIT

    def kernel(x_ref, *refs):
        out_ref, tok_ref = refs[-2:]
        x = x_ref[...].reshape(parts * rows, depth)
        y = None
        for s in range(SPLIT):
            term = jnp.dot(x[:, s * cut : (s + 1) * cut], refs[s][...], preferred_element_type=F32)
            y = term if y is None else y + term
        out_ref[...] = y.astype(BF16).reshape(parts, rows, cols)
        tok_ref[...] = jnp.zeros_like(tok_ref)

    more = ([] if held is None else [held]) + after
    return pl.pallas_call(
        kernel,
        grid=(steps,),
        in_specs=[pl.BlockSpec((parts, None, rows, depth), lambda i: (0, chunk, 0, 0))]
        + [pl.BlockSpec((cut, cols), lambda i, s=s: (s, base + i)) for s in range(SPLIT)]
        + [ANY] * len(more),
        out_specs=[
            pl.BlockSpec((parts, rows, cols), lambda i: (0, 0, piece * steps + i)),
            TOKEN_SPEC,
        ],
        out_shape=[jax.ShapeDtypeStruct((parts, rows, half + extra), BF16), TOKEN],
        input_output_aliases={} if held is None else {1 + SPLIT: 0},
        compiler_params=pltpu.CompilerParams(vmem_limit_bytes=LIMIT),
        cost_estimate=cost(SHORT),
        name="forward_piece",
    )(by_share, *([w_out] * SPLIT), *more)


def backward_piece(blocks, w_out, chunk, chunks, halves, piece, pieces, total, last, held, after):
    parts, rows, _ = blocks[0][1].shape
    half = w_out.shape[1] // halves
    depth = w_out.shape[0]
    span = depth // pieces
    cols = divisor(span, 256)
    steps = span // cols
    cut = half // SPLIT
    n = len(blocks)

    def kernel(*refs):
        out_ref, tok_ref = refs[-2:]
        y = None if total is None else refs[n + n * SPLIT][...].reshape(parts * rows, cols)
        for b in range(n):
            g = refs[b][...].reshape(parts * rows, half)
            for s in range(SPLIT):
                term = project_rows(g[:, s * cut : (s + 1) * cut], refs[n + b * SPLIT + s][...])
                y = term if y is None else y + term
        out_ref[...] = y.astype(out_ref.dtype).reshape(parts, rows, cols)
        tok_ref[...] = jnp.zeros_like(tok_ref)

    here = pl.BlockSpec((parts, rows, cols), lambda i: (0, 0, piece * steps + i))
    if last:
        out_spec = pl.BlockSpec((parts, None, rows, cols), lambda i: (0, chunk, 0, piece * steps + i))
        out_shape = jax.ShapeDtypeStruct((parts, chunks, rows, depth), BF16)
    else:
        out_spec, out_shape = here, jax.ShapeDtypeStruct((parts, rows, depth), F32)
    weights = [
        pl.BlockSpec((cols, cut), lambda i, at=at * SPLIT + s: (piece * steps + i, at))
        for at, _ in blocks
        for s in range(SPLIT)
    ]
    sums = [] if total is None else [total]
    extra = ([] if held is None else [held]) + after
    return pl.pallas_call(
        kernel,
        grid=(steps,),
        in_specs=[pl.BlockSpec((parts, rows, half), lambda i: (0, 0, 0))] * n
        + weights
        + [here] * len(sums)
        + [ANY] * len(extra),
        out_specs=[out_spec, TOKEN_SPEC],
        out_shape=[out_shape, TOKEN],
        input_output_aliases={} if held is None else {n + n * SPLIT + len(sums): 0},
        compiler_params=pltpu.CompilerParams(vmem_limit_bytes=LIMIT),
        cost_estimate=cost(SHORT),
        name="backward_piece",
    )(*[g for _, g in blocks], *([w_out] * (n * SPLIT)), *sums, *extra)


def relay(pos, flow, k, partial, came, held, after):
    rows, width = came.shape
    parts = (partial if held is None else held).shape[0]
    n_in = 1 + (partial is not None) + (held is not None) + len(after)

    def far(pos_ref, steps):
        way = pos_ref[1] if flow == 0 else -pos_ref[1]
        return lax.clamp(0, pos_ref[0] + way * steps, parts - 1)

    def kernel(pos_ref, *refs):
        came_ref, x_ref = refs[0], refs[n_in]
        place = pos_ref[2] if flow == 0 else parts - 1 - pos_ref[2]
        if held is not None:
            store = pltpu.make_async_copy(came_ref, refs[n_in + 1].at[far(pos_ref, -k)], refs[-1])
            pl.when(place >= k)(store.start)
        if partial is not None:

            @pl.when(place < k)
            def _():
                x_ref[...] = (came_ref[...].astype(F32) + refs[1][...].astype(F32)).astype(BF16)

            @pl.when(place >= k)
            def _():
                x_ref[...] = came_ref[...]

        if held is not None:
            pl.when(place >= k)(store.wait)

    line = jax.ShapeDtypeStruct((rows, width), BF16)
    args, out_shape, alias = [came], [line], {}
    if partial is not None:
        whole = pl.BlockSpec((rows, width), lambda i, w: (0, 0))
        term = pl.BlockSpec((None, rows, width), lambda i, w: (far(w, parts - k), 0, 0))
        specs, out_specs = [whole, term], [whole]
        args.append(partial)
    else:
        specs, out_specs, alias = [ANY], [ANY], {1: 0}
    if held is not None:
        alias[1 + len(args)] = 1
        specs.append(ANY)
        args.append(held)
        out_specs.append(ANY)
        out_shape.append(jax.ShapeDtypeStruct(held.shape, BF16))
    outs = pl.pallas_call(
        kernel,
        grid_spec=pltpu.PrefetchScalarGridSpec(
            num_scalar_prefetch=1,
            grid=(1,),
            in_specs=specs + [ANY] * len(after),
            out_specs=out_specs,
            scratch_shapes=[pltpu.SemaphoreType.DMA] if held is not None else [],
        ),
        out_shape=out_shape,
        input_output_aliases=alias,
        compiler_params=pltpu.CompilerParams(vmem_limit_bytes=LIMIT),
        cost_estimate=cost(LONG),
        name="relay",
    )(pos, *args, *after)
    return outs[0], (outs[1] if held is not None else None)


def take_block(partial, at):
    return lax.dynamic_index_in_dim(partial, at, 0, keepdims=False)


def norm_terms(p_ref, a_ref, b_ref, res_ref, grad_ref, gain_ref, at):
    proj = p_ref[:, at].astype(F32) + a_ref[:, at].astype(F32) + b_ref[:, at].astype(F32)
    z = res_ref[:, at].astype(F32) + proj
    scaled = gain_ref[:, at].astype(F32) * grad_ref[:, at].astype(F32)
    return z, scaled


def norm_specs(ins, half, chunk, at):
    _, rows, wide = ins[0].shape
    whole = pl.BlockSpec((rows, wide), lambda i, r: (0, 0))
    own = pl.BlockSpec((None, rows, half), lambda i, r: (0, chunk, at))
    mine = pl.BlockSpec((None, rows, wide), lambda i, r: (r[0], 0, 0))
    return [mine, whole, whole, own, own, pl.BlockSpec((1, half), lambda i, r: (0, at))]


def norm_sums(pos, ins, half, chunk, at, sums, after):
    rows = ins[0].shape[1]
    cols = divisor(half, 1024)

    def kernel(pos_ref, *refs):
        square_ref, cross_ref = refs[-2:]

        def step(i, sums):
            z, scaled = norm_terms(*refs[:6], pl.ds(pl.multiple_of(i * cols, cols), cols))
            square, cross = sums
            for j in range(0, cols, 128):
                zj = z[:, j : j + 128]
                square = square + zj * zj
                cross = cross + zj * scaled[:, j : j + 128]
            return square, cross

        zero = jnp.zeros((rows, 128), F32)
        start = (zero, zero) if sums is None else (refs[6][...], refs[7][...])
        square_ref[...], cross_ref[...] = lax.fori_loop(0, half // cols, step, start)

    stat = pl.BlockSpec((rows, 128), lambda i, r: (0, 0))
    before = [] if sums is None else list(sums)
    return pl.pallas_call(
        kernel,
        grid_spec=pltpu.PrefetchScalarGridSpec(
            num_scalar_prefetch=1,
            grid=(1,),
            in_specs=norm_specs(ins, half, chunk, at) + [stat] * len(before) + [ANY] * len(after),
            out_specs=[stat, stat],
        ),
        out_shape=[jax.ShapeDtypeStruct((rows, 128), F32)] * 2,
        compiler_params=pltpu.CompilerParams(vmem_limit_bytes=LIMIT),
        cost_estimate=cost(LONG),
        name="norm_sums",
    )(pos, *ins, *before, *after)


def norm_out(pos, ins, half, chunk, sums, proj_out, after):
    parts, rows, wide = ins[0][1][0].shape
    cols = divisor(half, 1024)
    n, kp, width = len(ins), proj_out.shape[0], proj_out.shape[1]
    with_b = proj_out if wide > half else None

    def kernel(pos_ref, *refs):
        square_ref, cross_ref = refs[6 * n], refs[6 * n + 1]
        if with_b is None:
            out_ref, held_ref, sem = refs[-3:]
        else:
            out_ref, held_ref, rest_ref, sem = refs[-4:]
        inv = lax.rsqrt(jnp.sum(square_ref[...], axis=-1, keepdims=True) / width + EPS)
        slope = inv * inv * inv * (jnp.sum(cross_ref[...], axis=-1, keepdims=True) / width)
        for j in range(n):
            to_ref = out_ref if j == 0 else rest_ref.at[j - 1]

            def step(i, carry):
                here = pl.ds(pl.multiple_of(i * cols, cols), cols)
                z, scaled = norm_terms(*refs[6 * j : 6 * j + 6], here)
                to_ref[:, here] = (inv * scaled - z * slope).astype(BF16)
                return carry

            lax.fori_loop(0, half // cols, step, 0)
        if with_b is not None:
            p_ref = refs[6 * n + 2]
            b = project_rows(out_ref[:, :half], p_ref[:, :half])
            for j in range(1, n):
                b = b + project_rows(rest_ref[j - 1], p_ref[:, j * half : (j + 1) * half])
            a = sum(refs[j][:, half:].astype(F32) for j in range(3))
            out_ref[:, half:] = (a + spread(b.astype(BF16), kp)).astype(BF16)
        own = pltpu.make_async_copy(out_ref, held_ref.at[pos_ref[0]], sem)
        own.start()
        own.wait()

    stat = pl.BlockSpec((rows, 128), lambda i, r: (0, 0))
    specs, args = [], []
    for at, one in ins:
        specs += norm_specs(one, half, chunk, at)
        args += one
    specs, args = specs + [stat, stat], args + list(sums)
    scratch = [pltpu.SemaphoreType.DMA]
    if with_b is not None:
        specs.append(pl.BlockSpec(proj_out.shape, lambda i, r: (0, 0)))
        args.append(proj_out)
        scratch = [pltpu.VMEM((max(1, n - 1), rows, half), BF16)] + scratch
    return pl.pallas_call(
        kernel,
        grid_spec=pltpu.PrefetchScalarGridSpec(
            num_scalar_prefetch=1,
            grid=(1,),
            in_specs=specs + [ANY] * len(after),
            out_specs=[pl.BlockSpec((rows, wide), lambda i, r: (0, 0)), ANY],
            scratch_shapes=scratch,
        ),
        out_shape=[
            jax.ShapeDtypeStruct((rows, wide), BF16),
            jax.ShapeDtypeStruct((parts, rows, wide), BF16),
        ],
        compiler_params=pltpu.CompilerParams(vmem_limit_bytes=LIMIT),
        cost_estimate=cost(SHORT),
        name="norm_out",
    )(pos, *args, *after)


def exchange(value_of, axis, size, rank):
    first = value_of(rank)
    out = jnp.zeros((size,) + first.shape, first.dtype)
    out = lax.dynamic_update_index_in_dim(out, first, rank, 0)
    for shift in range(1, size):
        got = lax.ppermute(
            value_of(lax.rem(rank + shift, size)), axis, [(d, (d + shift) % size) for d in range(size)]
        )
        out = lax.dynamic_update_index_in_dim(out, got, lax.rem(rank - shift + size, size), 0)
    return out


def body(inputs, residual, out_grad, norm_gain, w_out, proj_in, proj_out, queries, segment_ids):
    parts = lax.axis_size("tensor")
    rank = lax.axis_index("tensor")
    queriers = lax.axis_size("query")
    q_rank = lax.axis_index("query")
    tokens = inputs.shape[1]
    share = tokens // parts
    chunks = max(1, min(CHUNKS, share // 16))
    rows = share // chunks
    by_share = inputs.reshape(parts, chunks, rows, inputs.shape[2])
    gain = norm_gain.reshape(1, -1)
    half = w_out.shape[1] // HALVES
    kp = proj_out.shape[0]

    up = 1 - 2 * lax.rem(q_rank, 2)
    pos = jnp.stack([rank, up, jnp.where(up == 1, rank, parts - 1 - rank)]).astype(jnp.int32)

    def pairs(flow, low, high):
        out = []
        for q in range(queriers):
            way = 1 if (q % 2 == 0) == (flow == 0) else -1
            for t in range(parts):
                spot = t if way == 1 else parts - 1 - t
                if low <= spot <= min(high, parts - 2):
                    out.append((t * queriers + q, (t + way) * queriers + q))
        return out

    work, marks = [], []
    partials, totals, result = {}, {}, [None]

    def forward(c, h, piece, pieces, after):
        partials[c, h], mark = forward_piece(
            by_share,
            w_out,
            c,
            HALVES,
            h,
            2 * kp if h == 0 else 0,
            piece,
            pieces,
            partials.get((c, h)),
            after,
        )
        if h == 0 and piece == pieces - 1:
            partials[c, h] = forward_extra(by_share, proj_in, c, partials[c, h], [mark])
        return mark

    def backward(c, blocks, total, last, piece, pieces, after):
        held = result[0] if last else totals.get(c)
        done, mark = backward_piece(
            blocks, w_out, c, chunks, HALVES, piece, pieces, total, last, held, after
        )
        if last:
            result[0] = done
        else:
            totals[c] = done
        return mark

    def do_one(after):
        if work:
            marks[:] = [work.pop(0)[1](after)]

    def finish(key):
        while any(k == key for k, _ in work):
            do_one(list(marks))

    def add_forward(c, h, pieces):
        for piece in range(pieces):
            work.append(((c, h), functools.partial(forward, c, h, piece, pieces)))

    add_forward(0, 0, 1)
    finish((0, 0))
    gathered = []
    for slot in range(chunks + 1):
        rs, ag = slot < chunks, slot > 0
        came, held, sent, before = {}, {}, {}, None
        if ag:
            ins = [
                [partials[slot - 1, h], arrived[h, 0], arrived[h, 1], residual, out_grad, gain]
                for h in range(HALVES)
            ]
            sums = None
            for h in range(HALVES):
                sums = norm_sums(pos, ins[h], half, slot - 1, h, sums, list(marks))
            grad = [None] * HALVES
            grad[0], held[0] = norm_out(
                pos, list(enumerate(ins)), half, slot - 1, sums, proj_out, []
            )
        for k in range(parts):
            gather_now, reduce_now = ag and k <= parts - 2, rs and k >= 1
            if not gather_now and not reduce_now:
                continue
            for h in range(HALVES):
                if k == 0 and h > 0:
                    if rs:
                        add_forward(slot, h, 1)
                    do_one([sent[h - 1, 1]])
                    grad[h], held[h] = norm_out(
                        pos, [(h, ins[h])], half, slot - 1, sums, proj_out, list(marks)
                    )
                if reduce_now:
                    if slot == 0 and k == 1 and h > 0:
                        add_forward(0, h, 1)
                        do_one([sent[h - 1, 1]])
                    finish((slot, h))
                for flow in range(2):
                    if k == 0:
                        x = before = grad[h]
                    elif (h, flow) not in came:
                        way = up if flow == 0 else -up
                        x = take_block(
                            partials[slot, h], jnp.clip(rank + way * (parts - k), 0, parts - 1)
                        )
                    else:
                        x, held[h] = relay(
                            pos,
                            flow,
                            k,
                            partials[slot, h] if reduce_now else None,
                            came[h, flow],
                            held.get(h),
                            list(marks) + ([] if before is None else [before]),
                        )
                        before = x
                    came[h, flow] = lax.ppermute(
                        x,
                        ("tensor", "query"),
                        pairs(flow, 0 if reduce_now else k, parts - 2 if gather_now else k - 1),
                    )
                    sent[h, flow] = x
                    if k > 0 and (slot > 0 or k > 1):
                        do_one([x])
            if slot == 0 and k == 1 and chunks > 1:
                add_forward(1, 0, PIECES)
        if ag:
            if slot + 1 < chunks:
                add_forward(slot + 1, 0, PIECES)
            if rs:
                blocks = [(h, held[h]) for h in range(HALVES)]
                for piece in range(PIECES):
                    work.append(
                        (
                            ("b", slot - 1),
                            functools.partial(backward, slot - 1, blocks, None, True, piece, PIECES),
                        )
                    )
            else:
                while work:
                    do_one(list(marks))
                for h in range(HALVES):
                    for flow in range(2):
                        _, held[h] = relay(
                            pos, flow, parts - 1, None, came[h, flow], held[h], list(marks)
                        )
                    if h < HALVES - 1:
                        blocks = [(h, held[h])]
                        marks[:] = [backward(slot - 1, blocks, totals.get(slot - 1), False, 0, 1, [])]
            gathered.append(held[0][:, :, half:])
        arrived = came
    both = jnp.stack(gathered, axis=1).reshape(tokens, 2 * kp)
    member = segment_ids[0][None, :] == jnp.arange(EX_DEV, dtype=jnp.int32)[:, None]
    weighted = jnp.where(member[:, :, None], both[None, :, kp:], 0)
    sketch = lax.dot_general(
        weighted,
        jnp.broadcast_to(both[None, :, :kp], (EX_DEV, tokens, kp)),
        (((1,), (1,)), ((0,), (0,))),
        preferred_element_type=F32,
    )
    sketch_cols = lax.dynamic_slice_in_dim(sketch, rank * (kp // parts), kp // parts, 1)
    sketch_cols = sketch_cols.reshape(EX_DEV, kp // parts * kp)
    paired = exchange(lambda at: sketch_cols, "query", queriers, q_rank)
    paired = paired.reshape(queriers * EX_DEV, sketch_cols.shape[1])
    score_part = lax.dot_general(
        paired,
        queries.astype(F32),
        (((1,), (1,)), ((), ())),
        precision=lax.Precision.HIGHEST,
    )
    scores = jnp.sum(exchange(lambda at: score_part, "tensor", parts, rank), axis=0)
    blocks = [(HALVES - 1, held[HALVES - 1])]
    for piece in range(PIECES):
        after = [scores] if piece == PIECES - 1 else []
        backward(chunks - 1, blocks, totals.get(chunks - 1), True, piece, PIECES, after)
    return (result[0].reshape(1, tokens, -1), scores)


def solution(mesh):
    return jax.shard_map(
        body,
        mesh=mesh,
        in_specs=(
            P(("groups", "dp", "query"), None, "tensor"),
            P(("groups", "dp", "query"), "tensor", None),
            P(("groups", "dp", "query"), "tensor", None),
            P(),
            P("tensor", None),
            P(None, "tensor"),
            P(),
            P("query", "tensor"),
            P(("groups", "dp", "query"), None),
        ),
        out_specs=(P(("groups", "dp", "query"), None, "tensor"), P(("groups", "dp"), "query")),
        check_vma=False,
    )
```

time: 378 us -> 341 us (0.902)
  waiting for transfers between devices: 37.7 us -> 75.6 us
  Pallas kernels: 164 us -> 127 us
  local copies, waits for them, and re-layouts: 35.3 us -> 15.4 us
  starting transfers between devices: 133 us -> 118 us
    ppermute x40, waiting for transfers between devices: 23.6 us -> 73.1 us  [body(): lax.ppermute(x, ('tensor', 'query'), pairs(flow, 0 if reduce_now else k,...]
    ppermute x10 -> x4, starting transfers between devices: 33.9 us -> 10.1 us  [exchange(): lax.ppermute(value_of(lax.rem(rank + shift, size)), axis, [(d, (d + shift...]
    pallas_call x32, Pallas kernels: 50 us -> 30.2 us  [relay(): pl.pallas_call(kernel, grid_spec=pltpu.PrefetchScalarGridSpec(num_scalar_...]
    unnamed x183 -> x50, local copies, waits for them, and re-layouts: 31.1 us -> 12.5 us
    pallas_call x10 -> x5, Pallas kernels: 55.4 us -> 41.3 us  [backward_piece(): pl.pallas_call(kernel, grid=(steps,), in_specs=[pl.BlockSpec((parts, rows...]
    ppermute x10 -> x4, waiting for transfers between devices: 14 us -> 2.56 us  [exchange(): lax.ppermute(value_of(lax.rem(rank + shift, size)), axis, [(d, (d + shift...]
    ppermute x40, starting transfers between devices: 99.5 us -> 108 us  [body(): lax.ppermute(x, ('tensor', 'query'), pairs(flow, 0 if reduce_now else k,...]
    pallas_call x10 -> x5, Pallas kernels: 47.4 us -> 42.2 us  [forward_piece(): pl.pallas_call(kernel, grid=(steps,), in_specs=[pl.BlockSpec((parts, None...]
  transfers between devices with their start and end apart: 50 -> 44, of which waited for: 10 -> 19; matrix products, arithmetic and copies ran while one was open for 1% -> 1% of each run, Pallas kernels for 39% -> 30%
where the time goes in v4:
time: 341 us; the launch traced here: 339 us
  Pallas kernels  127 us (37%)
  starting transfers between devices  118 us (35%)
  waiting for transfers between devices  75.6 us (22%)
  local copies, waits for them, and re-layouts  15.4 us (5%)
    ppermute x40, starting transfers between devices, body(): lax.ppermute(x, ('tensor', 'query'), pairs(flow, 0 if reduce_now else k,...  108 us
    ppermute x40, waiting for transfers between devices, body(): lax.ppermute(x, ('tensor', 'query'), pairs(flow, 0 if reduce_now else k,...  73.1 us
    pallas_call x5, Pallas kernels, forward_piece(): pl.pallas_call(kernel, grid=(steps,), in_specs=[pl.BlockSpec((parts, None...  42.2 us
    pallas_call x5, Pallas kernels, backward_piece(): pl.pallas_call(kernel, grid=(steps,), in_specs=[pl.BlockSpec((parts, rows...  41.3 us
    pallas_call x32, Pallas kernels, relay(): pl.pallas_call(kernel, grid_spec=pltpu.PrefetchScalarGridSpec(num_scalar_...  30.2 us
    unnamed x50, local copies, waits for them, and re-layouts  12.5 us
    ppermute x4, starting transfers between devices, exchange(): lax.ppermute(value_of(lax.rem(rank + shift, size)), axis, [(d, (d + shift...  10.1 us
    pallas_call x4, Pallas kernels, norm_out(): pl.pallas_call(kernel, grid_spec=pltpu.PrefetchScalarGridSpec(num_scalar_...  7.48 us
  transfers between devices with their start and end apart: 44, of which 19 were waited for; matrix products, arithmetic and copies ran while one was open for 1% of the time, Pallas kernels for 30%

profile of v4, /device:TPU:0, one launch (start us, length us, event | category | flops | bytes accessed | tf_op | source)
XLA Modules:
  0.0 338.9 jit_solution(5257309729643549787)
XLA Ops:
  2.3 10.4 %forward_piece.5 = (bf16[4,64,4224]{2,1,0:T(8,128)(2,1)S(1)}, f32[8,128]{1,0:T(8,128)S(1)}) custom-call(bf16[4,2,64,2048]{3,2,1,0:T(8,128)(2,1)S(1)} %bitcast.31, bf16[2048,8192]{1,0:T(8,128)(2,1)} %refs_4_.25, bf16[2048,8192]{1,0:T(8,128)(2,1)} %refs_4_.25, bf16[2048,8192]{1,0:T(8,128)(2,1)} %refs_4_.25, bf16[2048,8192]{1,0:T(8,128)(2,1)} %refs_4_.25), custom_call_target="tpu_custom_call" | custom-call | bytes 720000 | tf_op jit(solution)/shard_map/forward_piece/pallas_call | solution.py:95
  14.6 5.7 %collective-permute-start = (bf16[64,4224]{1,0:T(8,128)(2,1)}, bf16[64,4224]{1,0:T(8,128)(2,1)}, u32[]{:S(2)}, u32[]{:S(2)}) collective-permute-start(bf16[64,4224]{1,0:T(8,128)(2,1)} %get-tuple-element.159), channel_id=1, source_target_pairs={{0,4},{13,9},{2,6},{15,11},{16,20},{29,25},{18,22},{31,27}} | collective-permute-start | bytes 1622024 | tf_op jit(solution)/shard_map/ppermute | solution.py:481
  21.8 10.2 %forward_piece.6 = (bf16[4,64,4096]{2,1,0:T(8,128)(2,1)S(1)}, f32[8,128]{1,0:T(8,128)S(1)}) custom-call(bf16[4,2,64,2048]{3,2,1,0:T(8,128)(2,1)S(1)} %bitcast.33, bf16[2048,8192]{1,0:T(8,128)(2,1)} %refs_4_.25, bf16[2048,8192]{1,0:T(8,128)(2,1)} %refs_4_.25, bf16[2048,8192]{1,0:T(8,128)(2,1)} %refs_4_.25, bf16[2048,8192]{1,0:T(8,128)(2,1)} %refs_4_.25, ...), custom_call_target="tpu_custom_call" | custom-call | bytes 720000 | tf_op jit(solution)/shard_map/forward_piece/pallas_call | solution.py:95
  39.8 5.6 %forward_piece.7 = (bf16[4,64,4224]{2,1,0:T(8,128)(2,1)S(1)}, f32[8,128]{1,0:T(8,128)S(1)}) custom-call(bf16[4,2,64,2048]{3,2,1,0:T(8,128)(2,1)S(1)} %bitcast.34, bf16[2048,8192]{1,0:T(8,128)(2,1)} %refs_4_.25, bf16[2048,8192]{1,0:T(8,128)(2,1)} %refs_4_.25, bf16[2048,8192]{1,0:T(8,128)(2,1)} %refs_4_.25, bf16[2048,8192]{1,0:T(8,128)(2,1)} %refs_4_.25, ...), custom_call_target="tpu_custom_call" | custom-call | bytes 720000 | tf_op jit(solution)/shard_map/forward_piece/pallas_call | solution.py:95
  49.0 5.7 %forward_piece.8 = (bf16[4,64,4224]{2,1,0:T(8,128)(2,1)S(1)}, f32[8,128]{1,0:T(8,128)S(1)}) custom-call(bf16[4,2,64,2048]{3,2,1,0:T(8,128)(2,1)S(1)} %bitcast.35, bf16[2048,8192]{1,0:T(8,128)(2,1)} %refs_4_.25, bf16[2048,8192]{1,0:T(8,128)(2,1)} %refs_4_.25, bf16[2048,8192]{1,0:T(8,128)(2,1)} %refs_4_.25, ...), custom_call_target="tpu_custom_call", output_to_operand_aliasing={{0}: (5, {})} | custom-call | bytes 720000 | tf_op jit(solution)/shard_map/forward_piece/pallas_call | solution.py:95
  63.8 5.8 %collective-permute-start.5 = (bf16[64,4224]{1,0:T(8,128)(2,1)S(1)}, bf16[64,4224]{1,0:T(8,128)(2,1)S(1)}, u32[]{:S(2)}, u32[]{:S(2)}) collective-permute-start(bf16[64,4224]{1,0:T(8,128)(2,1)S(1)} %relay.36.refs_3_), channel_id=1, source_target_pairs={{0,4},{4,8},{8,12},{5,1},{9,5},{13,9},{2,6},{6,10},{10,14},{7,3},{... | collective-permute-start | bytes 1622024 | tf_op jit(solution)/shard_map/ppermute | solution.py:481
  72.4 8.4 %collective-permute-start.9 = (bf16[64,4096]{1,0:T(8,128)(2,1)S(1)}, bf16[64,4096]{1,0:T(8,128)(2,1)S(1)}, u32[]{:S(2)}, u32[]{:S(2)}) collective-permute-start(bf16[64,4096]{1,0:T(8,128)(2,1)S(1)} %relay.38.refs_3_), channel_id=1, source_target_pairs={{0,4},{4,8},{8,12},{5,1},{9,5},{13,9},{2,6},{6,10},{10,14},{7,3},{... | collective-permute-start | bytes 1572872 | tf_op jit(solution)/shard_map/ppermute | solution.py:481
  83.5 7.5 %collective-permute-done.11.refs_2_.refs_8_ = bf16[64,4096]{1,0:T(8,128)(2,1)S(1)} collective-permute-done((bf16[64,4096]{1,0:T(8,128)(2,1)S(1)}, bf16[64,4096]{1,0:T(8,128)(2,1)S(1)}, u32[]{:S(2)}, u32[]{:S(2)}) %collective-permute-start.11) | collective-permute-done | bytes 524320 | tf_op jit(solution)/shard_map/ppermute | solution.py:481
  97.6 5.4 %collective-permute-start.14 = (bf16[64,4224]{1,0:T(8,128)(2,1)S(1)}, bf16[64,4224]{1,0:T(8,128)(2,1)S(1)}, u32[]{:S(2)}, u32[]{:S(2)}) collective-permute-start(bf16[64,4224]{1,0:T(8,128)(2,1)S(1)} %get-tuple-element.91.refs_4_), channel_id=1, source_target_pairs={{0,4},{4,8},{8,12},{5,1},{9,5},{13,9},{2,6},{6,10},{10,14},{7,3},{... | collective-permute-start | bytes 1622024 | tf_op jit(solution)/shard_map/ppermute | solution.py:481
  104.3 10.3 %forward_piece.9 = (bf16[4,64,4096]{2,1,0:T(8,128)(2,1)S(1)}, f32[8,128]{1,0:T(8,128)S(1)}) custom-call(bf16[4,2,64,2048]{3,2,1,0:T(8,128)(2,1)S(1)} %bitcast.36, bf16[2048,8192]{1,0:T(8,128)(2,1)} %refs_4_.25, bf16[2048,8192]{1,0:T(8,128)(2,1)} %refs_4_.25, bf16[2048,8192]{1,0:T(8,128)(2,1)} %refs_4_.25, bf16[2048,8192]{1,0:T(8,128)(2,1)} %refs_4_.25, ...), custom_call_target="tpu_custom_call" | custom-call | bytes 720000 | tf_op jit(solution)/shard_map/forward_piece/pallas_call | solution.py:95
  115.7 4.6 %collective-permute-start.12 = (bf16[64,4096]{1,0:T(8,128)(2,1)S(1)}, bf16[64,4096]{1,0:T(8,128)(2,1)S(1)}, u32[]{:S(2)}, u32[]{:S(2)}) collective-permute-start(bf16[64,4096]{1,0:T(8,128)(2,1)S(1)} %get-tuple-element.94.refs_4_), channel_id=1, source_target_pairs={{0,4},{4,8},{8,12},{5,1},{9,5},{13,9},{2,6},{6,10},{10,14},{7,3},{... | collective-permute-start | bytes 1572872 | tf_op jit(solution)/shard_map/ppermute | solution.py:481
  139.2 4.6 %collective-permute-done.18.refs_0_ = bf16[64,4224]{1,0:T(8,128)(2,1)S(1)} collective-permute-done((bf16[64,4224]{1,0:T(8,128)(2,1)S(1)}, bf16[64,4224]{1,0:T(8,128)(2,1)S(1)}, u32[]{:S(2)}, u32[]{:S(2)}) %collective-permute-start.18) | collective-permute-done | bytes 540704 | tf_op jit(solution)/shard_map/ppermute | solution.py:481
  173.0 4.6 %collective-permute-start.26 = (bf16[64,4224]{1,0:T(8,128)(2,1)S(1)}, bf16[64,4224]{1,0:T(8,128)(2,1)S(1)}, u32[]{:S(2)}, u32[]{:S(2)}) collective-permute-start(bf16[64,4224]{1,0:T(8,128)(2,1)S(1)} %get-tuple-element.115.refs_4_), channel_id=1, source_target_pairs={{0,4},{4,8},{8,12},{5,1},{9,5},{13,9},{2,6},{6,10},{10,14},{7,3},{... | collective-permute-start | bytes 1622024 | tf_op jit(solution)/shard_map/ppermute | solution.py:481
  180.4 5.1 %collective-permute-start.23 = (bf16[64,4096]{1,0:T(8,128)(2,1)S(1)}, bf16[64,4096]{1,0:T(8,128)(2,1)S(1)}, u32[]{:S(2)}, u32[]{:S(2)}) collective-permute-start(bf16[64,4096]{1,0:T(8,128)(2,1)S(1)} %get-tuple-element.117.refs_4_), channel_id=1, source_target_pairs={{0,4},{4,8},{8,12},{5,1},{9,5},{13,9},{2,6},{6,10},{10,14},{7,3},{... | collective-permute-start | bytes 1572872 | tf_op jit(solution)/shard_map/ppermute | solution.py:481
  191.5 8.9 %collective-permute-done.25.refs_2_.refs_8_ = bf16[64,4096]{1,0:T(8,128)(2,1)S(1)} collective-permute-done((bf16[64,4096]{1,0:T(8,128)(2,1)S(1)}, bf16[64,4096]{1,0:T(8,128)(2,1)S(1)}, u32[]{:S(2)}, u32[]{:S(2)}) %collective-permute-start.25) | collective-permute-done | bytes 524320 | tf_op jit(solution)/shard_map/ppermute | solution.py:481
  211.0 9.2 %backward_piece.5 = (bf16[4,2,64,2048]{3,2,1,0:T(8,128)(2,1)}, f32[8,128]{1,0:T(8,128)S(1)}) custom-call(bf16[4,64,4224]{2,1,0:T(8,128)(2,1)S(1)} %get-tuple-element.124.refs_0_, bf16[4,64,4096]{2,1,0:T(8,128)(2,1)S(1)} %get-tuple-element.125.refs_1_, bf16[2048,8192]{1,0:T(8,128)(2,1)} %refs_4_.25, bf16[2048,8192]{1,0:T(8,128)(2,1)} %refs_4_.25, ...), custom_call_target="tpu_custom_call" | custom-call | bytes 720000 | tf_op jit(solution)/shard_map/backward_piece/pallas_call | solution.py:147
  224.1 9.2 %backward_piece.6 = (bf16[4,2,64,2048]{3,2,1,0:T(8,128)(2,1)}, f32[8,128]{1,0:T(8,128)S(1)}) custom-call(bf16[4,64,4224]{2,1,0:T(8,128)(2,1)S(1)} %get-tuple-element.124.refs_0_, bf16[4,64,4096]{2,1,0:T(8,128)(2,1)S(1)} %get-tuple-element.125.refs_1_, bf16[2048,8192]{1,0:T(8,128)(2,1)} %refs_4_.25, ...), custom_call_target="tpu_custom_call", output_to_operand_aliasing={{0}: (10, {})} | custom-call | bytes 720000 | tf_op jit(solution)/shard_map/backward_piece/pallas_call | solution.py:147
  236.2 8.7 %collective-permute-start.29 = (bf16[64,4096]{1,0:T(8,128)(2,1)S(1)}, bf16[64,4096]{1,0:T(8,128)(2,1)}, u32[]{:S(2)}, u32[]{:S(2)}) collective-permute-start(bf16[64,4096]{1,0:T(8,128)(2,1)S(1)} %get-tuple-element.128.refs_3_), channel_id=1, source_target_pairs={{0,4},{4,8},{8,12},{5,1},{9,5},{13,9},{2,6},{6,10},{10,14},{7,3},{... | collective-permute-start | bytes 1572872 | tf_op jit(solution)/shard_map/ppermute | solution.py:481
  246.2 10.1 %collective-permute-done.29.refs_0_ = bf16[64,4096]{1,0:T(8,128)(2,1)} collective-permute-done((bf16[64,4096]{1,0:T(8,128)(2,1)S(1)}, bf16[64,4096]{1,0:T(8,128)(2,1)}, u32[]{:S(2)}, u32[]{:S(2)}) %collective-permute-start.29) | collective-permute-done | bytes 524320 | tf_op jit(solution)/shard_map/ppermute | solution.py:481
  275.7 12.4 %collective-permute-done.32.refs_0_ = bf16[64,4096]{1,0:T(8,128)(2,1)} collective-permute-done((bf16[64,4096]{1,0:T(8,128)(2,1)}, bf16[64,4096]{1,0:T(8,128)(2,1)}, u32[]{:S(2)}, u32[]{:S(2)}) %collective-permute-start.32) | collective-permute-done | bytes 524320 | tf_op jit(solution)/shard_map/ppermute | solution.py:481
  302.9 10.5 %backward_piece.7 = (f32[4,64,2048]{2,1,0:T(8,128)S(1)}, f32[8,128]{1,0:T(8,128)S(1)}) custom-call(bf16[4,64,4224]{2,1,0:T(8,128)(2,1)S(1)} %copy-done.14, bf16[2048,8192]{1,0:T(8,128)(2,1)} %refs_4_.25, bf16[2048,8192]{1,0:T(8,128)(2,1)} %refs_4_.25, bf16[2048,8192]{1,0:T(8,128)(2,1)} %refs_4_.25, bf16[2048,8192]{1,0:T(8,128)(2,1)} %refs_4_.25), custom_call_target="tpu_custom_call" | custom-call | bytes 720000 | tf_op jit(solution)/shard_map/backward_piece/pallas_call | solution.py:147
  315.6 6.2 %backward_piece.8 = (bf16[4,2,64,2048]{3,2,1,0:T(8,128)(2,1)}, f32[8,128]{1,0:T(8,128)}) custom-call(bf16[4,64,4096]{2,1,0:T(8,128)(2,1)S(1)} %get-tuple-element.153.refs_0_, bf16[2048,8192]{1,0:T(8,128)(2,1)} %refs_4_.25, bf16[2048,8192]{1,0:T(8,128)(2,1)} %refs_4_.25, bf16[2048,8192]{1,0:T(8,128)(2,1)} %refs_4_.25, ...), custom_call_target="tpu_custom_call", output_to_operand_aliasing={{0}: (6, {})} | custom-call | bytes 720000 | tf_op jit(solution)/shard_map/backward_piece/pallas_call | solution.py:147
  321.8 4.7 %collective-permute-start.42 = (f32[8,512]{1,0:T(8,128)S(1)}, f32[8,512]{1,0:T(8,128)S(1)}, u32[]{:S(2)}, u32[]{:S(2)}) collective-permute-start(f32[8,512]{1,0:T(8,128)S(1)} %get-tuple-element.165), channel_id=1, source_target_pairs={{0,8},{4,12},{8,0},{12,4},{1,9},{5,13},{9,1},{13,5},{2,10},{6,14},... | collective-permute-start | bytes 49160 | tf_op jit(solution)/shard_map/ppermute | solution.py:350
  332.5 6.2 %backward_piece.9 = (bf16[4,2,64,2048]{3,2,1,0:T(8,128)(2,1)}, f32[8,128]{1,0:T(8,128)}) custom-call(bf16[4,64,4096]{2,1,0:T(8,128)(2,1)S(1)} %get-tuple-element.153.refs_0_, bf16[2048,8192]{1,0:T(8,128)(2,1)} %refs_4_.25, bf16[2048,8192]{1,0:T(8,128)(2,1)} %refs_4_.25, bf16[2048,8192]{1,0:T(8,128)(2,1)} %refs_4_.25, ...), custom_call_target="tpu_custom_call", output_to_operand_aliasing={{0}: (6, {})} | custom-call | bytes 720000 | tf_op jit(solution)/shard_map/backward_piece/pallas_call | solution.py:147
  (192 shorter events, 157.0 us)
Async XLA Ops:
  14.6 23.4 %collective-permute-start = (bf16[64,4224]{1,0:T(8,128)(2,1)}, bf16[64,4224]{1,0:T(8,128)(2,1)}, u32[]{:S(2)}, u32[]{:S(2)}) collective-permute-start(bf16[64,4224]{1,0:T(8,128)(2,1)} %get-tuple-element.159), channel_id=1, source_target_pairs={{0,4},{13,9},{2,6},{15,11},{16,20},{29,25},{18,22},{31,27}} | collective-permute-start | bytes 1622024 | tf_op jit(solution)/shard_map/ppermute | solution.py:481
  20.3 26.3 %collective-permute-start.2 = (bf16[64,4224]{1,0:T(8,128)(2,1)}, bf16[64,4224]{1,0:T(8,128)(2,1)}, u32[]{:S(2)}, u32[]{:S(2)}) collective-permute-start(bf16[64,4224]{1,0:T(8,128)(2,1)} %get-tuple-element.158.refs_4_), channel_id=1, source_target_pairs={{12,8},{1,5},{14,10},{3,7},{28,24},{17,21},{30,26},{19,23}} | collective-permute-start | bytes 1622024 | tf_op jit(solution)/shard_map/ppermute | solution.py:481
  34.4 20.3 %collective-permute-start.4 = (bf16[64,4096]{1,0:T(8,128)(2,1)}, bf16[64,4096]{1,0:T(8,128)(2,1)}, u32[]{:S(2)}, u32[]{:S(2)}) collective-permute-start(bf16[64,4096]{1,0:T(8,128)(2,1)} %get-tuple-element.160), channel_id=1, source_target_pairs={{0,4},{13,9},{2,6},{15,11},{16,20},{29,25},{18,22},{31,27}} | collective-permute-start | bytes 1572872 | tf_op jit(solution)/shard_map/ppermute | solution.py:481
  36.5 22.4 %collective-permute-start.3 = (bf16[64,4096]{1,0:T(8,128)(2,1)}, bf16[64,4096]{1,0:T(8,128)(2,1)}, u32[]{:S(2)}, u32[]{:S(2)}) collective-permute-start(bf16[64,4096]{1,0:T(8,128)(2,1)} %get-tuple-element.161), channel_id=1, source_target_pairs={{12,8},{1,5},{14,10},{3,7},{28,24},{17,21},{30,26},{19,23}} | collective-permute-start | bytes 1572872 | tf_op jit(solution)/shard_map/ppermute | solution.py:481
  72.4 21.1 %collective-permute-start.9 = (bf16[64,4096]{1,0:T(8,128)(2,1)S(1)}, bf16[64,4096]{1,0:T(8,128)(2,1)S(1)}, u32[]{:S(2)}, u32[]{:S(2)}) collective-permute-start(bf16[64,4096]{1,0:T(8,128)(2,1)S(1)} %relay.38.refs_3_), channel_id=1, source_target_pairs={{0,4},{4,8},{8,12},{5,1},{9,5},{13,9},{2,6},{6,10},{10,14},{7,3},{... | collective-permute-start | bytes 1572872 | tf_op jit(solution)/shard_map/ppermute | solution.py:481
  97.6 24.6 %collective-permute-start.14 = (bf16[64,4224]{1,0:T(8,128)(2,1)S(1)}, bf16[64,4224]{1,0:T(8,128)(2,1)S(1)}, u32[]{:S(2)}, u32[]{:S(2)}) collective-permute-start(bf16[64,4224]{1,0:T(8,128)(2,1)S(1)} %get-tuple-element.91.refs_4_), channel_id=1, source_target_pairs={{0,4},{4,8},{8,12},{5,1},{9,5},{13,9},{2,6},{6,10},{10,14},{7,3},{... | collective-permute-start | bytes 1622024 | tf_op jit(solution)/shard_map/ppermute | solution.py:481
  103.0 24.5 %collective-permute-start.13 = (bf16[64,4224]{1,0:T(8,128)(2,1)S(1)}, bf16[64,4224]{1,0:T(8,128)(2,1)S(1)}, u32[]{:S(2)}, u32[]{:S(2)}) collective-permute-start(bf16[64,4224]{1,0:T(8,128)(2,1)S(1)} %get-tuple-element.91.refs_4_), channel_id=1, source_target_pairs={{4,0},{8,4},{12,8},{1,5},{5,9},{9,13},{6,2},{10,6},{14,10},{3,7},{... | collective-permute-start | bytes 1622024 | tf_op jit(solution)/shard_map/ppermute | solution.py:481
  122.9 20.8 %collective-permute-start.18 = (bf16[64,4224]{1,0:T(8,128)(2,1)S(1)}, bf16[64,4224]{1,0:T(8,128)(2,1)S(1)}, u32[]{:S(2)}, u32[]{:S(2)}) collective-permute-start(bf16[64,4224]{1,0:T(8,128)(2,1)S(1)} %get-tuple-element.99.refs_4_), channel_id=1, source_target_pairs={{0,4},{4,8},{8,12},{5,1},{9,5},{13,9},{2,6},{6,10},{10,14},{7,3},{... | collective-permute-start | bytes 1622024 | tf_op jit(solution)/shard_map/ppermute | solution.py:481
  128.1 20.7 %collective-permute-start.17 = (bf16[64,4224]{1,0:T(8,128)(2,1)S(1)}, bf16[64,4224]{1,0:T(8,128)(2,1)S(1)}, u32[]{:S(2)}, u32[]{:S(2)}) collective-permute-start(bf16[64,4224]{1,0:T(8,128)(2,1)S(1)} %get-tuple-element.100.refs_4_), channel_id=1, source_target_pairs={{4,0},{8,4},{12,8},{1,5},{5,9},{9,13},{6,2},{10,6},{14,10},{3,7},{... | collective-permute-start | bytes 1622024 | tf_op jit(solution)/shard_map/ppermute | solution.py:481
  132.8 22.1 %collective-permute-start.15 = (bf16[64,4096]{1,0:T(8,128)(2,1)S(1)}, bf16[64,4096]{1,0:T(8,128)(2,1)S(1)}, u32[]{:S(2)}, u32[]{:S(2)}) collective-permute-start(bf16[64,4096]{1,0:T(8,128)(2,1)S(1)} %get-tuple-element.101.refs_4_), channel_id=1, source_target_pairs={{0,4},{4,8},{8,12},{5,1},{9,5},{13,9},{2,6},{6,10},{10,14},{7,3},{... | collective-permute-start | bytes 1572872 | tf_op jit(solution)/shard_map/ppermute | solution.py:481
  137.9 22.2 %collective-permute-start.20 = (bf16[64,4096]{1,0:T(8,128)(2,1)S(1)}, bf16[64,4096]{1,0:T(8,128)(2,1)S(1)}, u32[]{:S(2)}, u32[]{:S(2)}) collective-permute-start(bf16[64,4096]{1,0:T(8,128)(2,1)S(1)} %get-tuple-element.105.refs_4_), channel_id=1, source_target_pairs={{4,0},{8,4},{12,8},{1,5},{5,9},{9,13},{6,2},{10,6},{14,10},{3,7},{... | collective-permute-start | bytes 1572872 | tf_op jit(solution)/shard_map/ppermute | solution.py:481
  144.4 22.1 %collective-permute-start.22 = (bf16[64,4224]{1,0:T(8,128)(2,1)S(1)}, bf16[64,4224]{1,0:T(8,128)(2,1)S(1)}, u32[]{:S(2)}, u32[]{:S(2)}) collective-permute-start(bf16[64,4224]{1,0:T(8,128)(2,1)S(1)} %get-tuple-element.107.refs_4_), channel_id=1, source_target_pairs={{0,4},{4,8},{8,12},{5,1},{9,5},{13,9},{2,6},{6,10},{10,14},{7,3},{... | collective-permute-start | bytes 1622024 | tf_op jit(solution)/shard_map/ppermute | solution.py:481
  149.5 21.4 %collective-permute-start.21 = (bf16[64,4224]{1,0:T(8,128)(2,1)S(1)}, bf16[64,4224]{1,0:T(8,128)(2,1)S(1)}, u32[]{:S(2)}, u32[]{:S(2)}) collective-permute-start(bf16[64,4224]{1,0:T(8,128)(2,1)S(1)} %get-tuple-element.108.refs_4_), channel_id=1, source_target_pairs={{4,0},{8,4},{12,8},{1,5},{5,9},{9,13},{6,2},{10,6},{14,10},{3,7},{... | collective-permute-start | bytes 1622024 | tf_op jit(solution)/shard_map/ppermute | solution.py:481
  155.7 22.1 %collective-permute-start.19 = (bf16[64,4096]{1,0:T(8,128)(2,1)S(1)}, bf16[64,4096]{1,0:T(8,128)(2,1)S(1)}, u32[]{:S(2)}, u32[]{:S(2)}) collective-permute-start(bf16[64,4096]{1,0:T(8,128)(2,1)S(1)} %get-tuple-element.109.refs_4_), channel_id=1, source_target_pairs={{0,4},{4,8},{8,12},{5,1},{9,5},{13,9},{2,6},{6,10},{10,14},{7,3},{... | collective-permute-start | bytes 1572872 | tf_op jit(solution)/shard_map/ppermute | solution.py:481
  179.1 21.2 %collective-permute-start.25 = (bf16[64,4096]{1,0:T(8,128)(2,1)S(1)}, bf16[64,4096]{1,0:T(8,128)(2,1)S(1)}, u32[]{:S(2)}, u32[]{:S(2)}) collective-permute-start(bf16[64,4096]{1,0:T(8,128)(2,1)S(1)} %get-tuple-element.119), channel_id=1, source_target_pairs={{4,0},{8,4},{12,8},{1,5},{5,9},{9,13},{6,2},{10,6},{14,10},{3,7},{... | collective-permute-start | bytes 1572872 | tf_op jit(solution)/shard_map/ppermute | solution.py:481
  180.4 20.6 %collective-permute-start.23 = (bf16[64,4096]{1,0:T(8,128)(2,1)S(1)}, bf16[64,4096]{1,0:T(8,128)(2,1)S(1)}, u32[]{:S(2)}, u32[]{:S(2)}) collective-permute-start(bf16[64,4096]{1,0:T(8,128)(2,1)S(1)} %get-tuple-element.117.refs_4_), channel_id=1, source_target_pairs={{0,4},{4,8},{8,12},{5,1},{9,5},{13,9},{2,6},{6,10},{10,14},{7,3},{... | collective-permute-start | bytes 1572872 | tf_op jit(solution)/shard_map/ppermute | solution.py:481
  209.7 23.6 %collective-permute-start.31 = (bf16[64,4224]{1,0:T(8,128)(2,1)}, bf16[64,4224]{1,0:T(8,128)(2,1)}, u32[]{:S(2)}, u32[]{:S(2)}) collective-permute-start(bf16[64,4224]{1,0:T(8,128)(2,1)} %get-tuple-element.126.refs_10_), channel_id=1, source_target_pairs={{4,0},{8,4},{12,8},{1,5},{5,9},{9,13},{6,2},{10,6},{14,10},{3,7},{... | collective-permute-start | bytes 1622024 | tf_op jit(solution)/shard_map/ppermute | solution.py:481
  222.7 39.9 %collective-permute-start.35 = (bf16[64,4224]{1,0:T(8,128)(2,1)S(1)}, bf16[64,4224]{1,0:T(8,128)(2,1)}, u32[]{:S(2)}, u32[]{:S(2)}) collective-permute-start(bf16[64,4224]{1,0:T(8,128)(2,1)S(1)} %get-tuple-element.132.refs_11_.refs_3_), channel_id=1, source_target_pairs={{4,8},{8,12},{5,1},{9,5},{6,10},{10,14},{7,3},{11,7},{20,24},{24,2... | collective-permute-start | bytes 1622024 | tf_op jit(solution)/shard_map/ppermute | solution.py:481
  234.9 29.9 %collective-permute-start.34 = (bf16[64,4224]{1,0:T(8,128)(2,1)}, bf16[64,4224]{1,0:T(8,128)(2,1)}, u32[]{:S(2)}, u32[]{:S(2)}) collective-permute-start(bf16[64,4224]{1,0:T(8,128)(2,1)} %get-tuple-element.135.refs_3_), channel_id=1, source_target_pairs={{4,0},{8,4},{5,9},{9,13},{6,2},{10,6},{7,11},{11,15},{20,16},{24,2... | collective-permute-start | bytes 1622024 | tf_op jit(solution)/shard_map/ppermute | solution.py:481
  263.2 29.1 %collective-permute-start.39 = (bf16[64,4224]{1,0:T(8,128)(2,1)}, bf16[64,4224]{1,0:T(8,128)(2,1)}, u32[]{:S(2)}, u32[]{:S(2)}) collective-permute-start(bf16[64,4224]{1,0:T(8,128)(2,1)} %get-tuple-element.142.refs_3_), channel_id=1, source_target_pairs={{8,12},{5,1},{10,14},{7,3},{24,28},{21,17},{26,30},{23,19}} | collective-permute-start | bytes 1622024 | tf_op jit(solution)/shard_map/ppermute | solution.py:481
  267.7 25.2 %collective-permute-start.38 = (bf16[64,4224]{1,0:T(8,128)(2,1)}, bf16[64,4224]{1,0:T(8,128)(2,1)}, u32[]{:S(2)}, u32[]{:S(2)}) collective-permute-start(bf16[64,4224]{1,0:T(8,128)(2,1)} %get-tuple-element.143.refs_3_), channel_id=1, source_target_pairs={{4,0},{9,13},{6,2},{11,15},{20,16},{25,29},{22,18},{27,31}} | collective-permute-start | bytes 1622024 | tf_op jit(solution)/shard_map/ppermute | solution.py:481
  274.0 39.4 %collective-permute-start.37 = (bf16[64,4096]{1,0:T(8,128)(2,1)}, bf16[64,4096]{1,0:T(8,128)(2,1)}, u32[]{:S(2)}, u32[]{:S(2)}) collective-permute-start(bf16[64,4096]{1,0:T(8,128)(2,1)} %get-tuple-element.145.refs_3_), channel_id=1, source_target_pairs={{8,12},{5,1},{10,14},{7,3},{24,28},{21,17},{26,30},{23,19}} | collective-permute-start | bytes 1572872 | tf_op jit(solution)/shard_map/ppermute | solution.py:481
  291.0 23.0 %collective-permute-start.36 = (bf16[64,4096]{1,0:T(8,128)(2,1)}, bf16[64,4096]{1,0:T(8,128)(2,1)}, u32[]{:S(2)}, u32[]{:S(2)}) collective-permute-start(bf16[64,4096]{1,0:T(8,128)(2,1)} %get-tuple-element.146), channel_id=1, source_target_pairs={{4,0},{9,13},{6,2},{11,15},{20,16},{25,29},{22,18},{27,31}} | collective-permute-start | bytes 1572872 | tf_op jit(solution)/shard_map/ppermute | solution.py:481
  298.8 30.7 %collective-permute-start.41 = (f32[8,512]{1,0:T(8,128)S(1)}, f32[8,512]{1,0:T(8,128)S(1)}, u32[]{:S(2)}, u32[]{:S(2)}) collective-permute-start(f32[8,512]{1,0:T(8,128)S(1)} %get-tuple-element.165), channel_id=1, source_target_pairs={{0,4},{4,8},{8,12},{12,0},{1,5},{5,9},{9,13},{13,1},{2,6},{6,10},{... | collective-permute-start | bytes 49160 | tf_op jit(solution)/shard_map/ppermute | solution.py:350
  (45 other events, 775.2 us)

commit v5 on v4

--- a/solution.py
+++ b/solution.py
@@ -185,18 +185,17 @@
             def _():
                 x_ref[...] = came_ref[...]
 
+        else:
+            x_ref[...] = came_ref[...]
         if held is not None:
             pl.when(place >= k)(store.wait)
 
     line = jax.ShapeDtypeStruct((rows, width), BF16)
-    args, out_shape, alias = [came], [line], {}
+    whole = pl.BlockSpec((rows, width), lambda i, w: (0, 0))
+    args, specs, out_specs, out_shape, alias = [came], [whole], [whole], [line], {}
     if partial is not None:
-        whole = pl.BlockSpec((rows, width), lambda i, w: (0, 0))
-        term = pl.BlockSpec((None, rows, width), lambda i, w: (far(w, parts - k), 0, 0))
-        specs, out_specs = [whole, term], [whole]
+        specs.append(pl.BlockSpec((None, rows, width), lambda i, w: (far(w, parts - k), 0, 0)))
         args.append(partial)
-    else:
-        specs, out_specs, alias = [ANY], [ANY], {1: 0}
     if held is not None:
         alias[1 + len(args)] = 1
         specs.append(ANY)
@@ -280,8 +279,8 @@
 def norm_out(pos, ins, half, chunk, sums, proj_out, after):
     parts, rows, wide = ins[0][1][0].shape
     cols = divisor(half, 1024)
-    n, kp, width = len(ins), proj_out.shape[0], proj_out.shape[1]
-    with_b = proj_out if wide > half else None
+    n, width = len(ins), ins[0][1][3].shape[2]
+    with_b = proj_out
 
     def kernel(pos_ref, *refs):
         square_ref, cross_ref = refs[6 * n], refs[6 * n + 1]
@@ -307,7 +306,9 @@
             for j in range(1, n):
                 b = b + project_rows(rest_ref[j - 1], p_ref[:, j * half : (j + 1) * half])
             a = sum(refs[j][:, half:].astype(F32) for j in range(3))
-            out_ref[:, half:] = (a + spread(b.astype(BF16), kp)).astype(BF16)
+            out_ref[:, half:] = (a + spread(b.astype(BF16), b.shape[1])).astype(BF16)
+        else:
+            out_ref[:, half:] = jnp.zeros((rows, wide - half), BF16)
         own = pltpu.make_async_copy(out_ref, held_ref.at[pos_ref[0]], sem)
         own.start()
         own.wait()
@@ -340,6 +341,39 @@
         cost_estimate=cost(SHORT),
         name="norm_out",
     )(pos, *args, *after)
+
+
+def tie(value, after):
+    def kernel(value_ref, *refs):
+        refs[-1][...] = value_ref[...]
+
+    whole = pl.BlockSpec(value.shape, lambda i: (0,) * value.ndim)
+    return pl.pallas_call(
+        kernel,
+        grid=(1,),
+        in_specs=[whole] + [ANY] * len(after),
+        out_specs=whole,
+        out_shape=jax.ShapeDtypeStruct(value.shape, value.dtype),
+        compiler_params=pltpu.CompilerParams(vmem_limit_bytes=LIMIT),
+        cost_estimate=cost(SHORT),
+        name="tie",
+    )(value, *after)
+
+
+def touch(x):
+    def kernel(x_ref, out_ref):
+        out_ref[...] = jnp.zeros_like(out_ref)
+
+    return pl.pallas_call(
+        kernel,
+        grid=(1,),
+        in_specs=[ANY],
+        out_specs=TOKEN_SPEC,
+        out_shape=TOKEN,
+        compiler_params=pltpu.CompilerParams(vmem_limit_bytes=LIMIT),
+        cost_estimate=cost(SHORT),
+        name="touch",
+    )(x)
 
 
 def exchange(value_of, axis, size, rank):
@@ -391,7 +425,7 @@
             c,
             HALVES,
             h,
-            2 * kp if h == 0 else 0,
+            2 * kp,
             piece,
             pieces,
             partials.get((c, h)),
@@ -412,20 +446,22 @@
             totals[c] = done
         return mark
 
-    def do_one(after):
+    def do_one(after, touching=False):
         if work:
             marks[:] = [work.pop(0)[1](after)]
-
-    def finish(key):
+        elif touching:
+            marks[:] = [touch(after[0])]
+
+    def finish(key, after):
         while any(k == key for k, _ in work):
-            do_one(list(marks))
+            do_one(list(marks) + after)
 
     def add_forward(c, h, pieces):
         for piece in range(pieces):
             work.append(((c, h), functools.partial(forward, c, h, piece, pieces)))
 
     add_forward(0, 0, 1)
-    finish((0, 0))
+    finish((0, 0), [])
     gathered = []
     for slot in range(chunks + 1):
         rs, ag = slot < chunks, slot > 0
@@ -449,16 +485,16 @@
             for h in range(HALVES):
                 if k == 0 and h > 0:
                     if rs:
-                        add_forward(slot, h, 1)
+                        add_forward(slot, h, PIECES)
                     do_one([sent[h - 1, 1]])
                     grad[h], held[h] = norm_out(
-                        pos, [(h, ins[h])], half, slot - 1, sums, proj_out, list(marks)
+                        pos, [(h, ins[h])], half, slot - 1, sums, None, list(marks)
                     )
                 if reduce_now:
                     if slot == 0 and k == 1 and h > 0:
                         add_forward(0, h, 1)
                         do_one([sent[h - 1, 1]])
-                    finish((slot, h))
+                    finish((slot, h), [sent[h - 1, 1]] if h > 0 else [])
                 for flow in range(2):
                     if k == 0:
                         x = before = grad[h]
@@ -484,10 +520,12 @@
                         pairs(flow, 0 if reduce_now else k, parts - 2 if gather_now else k - 1),
                     )
                     sent[h, flow] = x
-                    if k > 0 and (slot > 0 or k > 1):
-                        do_one([x])
-            if slot == 0 and k == 1 and chunks > 1:
-                add_forward(1, 0, PIECES)
+                    if slot == 0 and k == parts - 1 and (h, flow) == (HALVES - 1, 1) and chunks > 1:
+                        add_forward(1, 0, 1)
+                    if k > 0 and (slot > 0 or k > 1) and not (slot == 1 and work and k == 1 and flow == 0):
+                        do_one([x], slot == chunks)
+                if k == 0 and slot == chunks and h == HALVES - 1:
+                    marks[:] = [touch(sent[h, 1])]
         if ag:
             if slot + 1 < chunks:
                 add_forward(slot + 1, 0, PIECES)
@@ -503,14 +541,8 @@
             else:
                 while work:
                     do_one(list(marks))
-                for h in range(HALVES):
-                    for flow in range(2):
-                        _, held[h] = relay(
-                            pos, flow, parts - 1, None, came[h, flow], held[h], list(marks)
-                        )
-                    if h < HALVES - 1:
-                        blocks = [(h, held[h])]
-                        marks[:] = [backward(slot - 1, blocks, totals.get(slot - 1), False, 0, 1, [])]
+                for flow in range(2):
+                    _, held[0] = relay(pos, flow, parts - 1, None, came[0, flow], held[0], list(marks))
             gathered.append(held[0][:, :, half:])
         arrived = came
     both = jnp.stack(gathered, axis=1).reshape(tokens, 2 * kp)
@@ -524,19 +556,25 @@
     )
     sketch_cols = lax.dynamic_slice_in_dim(sketch, rank * (kp // parts), kp // parts, 1)
     sketch_cols = sketch_cols.reshape(EX_DEV, kp // parts * kp)
+
+    last = chunks - 1
+    marks[:] = [backward(last, [(0, held[0])], None, HALVES == 1, 0, 1, [sketch_cols])]
+    for h in range(1, HALVES):
+        for flow in range(2):
+            _, held[h] = relay(pos, flow, parts - 1, None, came[h, flow], held[h], list(marks))
     paired = exchange(lambda at: sketch_cols, "query", queriers, q_rank)
-    paired = paired.reshape(queriers * EX_DEV, sketch_cols.shape[1])
+    paired = tie(paired, list(marks)).reshape(queriers * EX_DEV, sketch_cols.shape[1])
     score_part = lax.dot_general(
         paired,
         queries.astype(F32),
         (((1,), (1,)), ((), ())),
         precision=lax.Precision.HIGHEST,
     )
-    scores = jnp.sum(exchange(lambda at: score_part, "tensor", parts, rank), axis=0)
-    blocks = [(HALVES - 1, held[HALVES - 1])]
-    for piece in range(PIECES):
-        after = [scores] if piece == PIECES - 1 else []
-        backward(chunks - 1, blocks, totals.get(chunks - 1), True, piece, PIECES, after)
+    for h in range(1, HALVES):
+        marks[:] = [
+            backward(last, [(h, held[h])], totals.get(last), h == HALVES - 1, 0, 1, [score_part])
+        ]
+    scores = jnp.sum(tie(exchange(lambda at: score_part, "tensor", parts, rank), list(marks)), axis=0)
     return (result[0].reshape(1, tokens, -1), scores)
 
 

time: 341 us -> 324 us (0.950)
  waiting for transfers between devices: 75.6 us -> 54.3 us
  starting transfers between devices: 118 us -> 104 us
  Pallas kernels: 127 us -> 137 us
  local copies, waits for them, and re-layouts: 15.4 us -> 22.6 us
    ppermute x40, waiting for transfers between devices: 73.1 us -> 54.3 us  [body(): lax.ppermute(x, ('tensor', 'query'), pairs(flow, 0 if reduce_now else k,...]
    pallas_call x32, Pallas kernels: 30.2 us -> 40.5 us  [relay(): pl.pallas_call(kernel, grid_spec=pltpu.PrefetchScalarGridSpec(num_scalar_...]
    ppermute x40, starting transfers between devices: 108 us -> 99.2 us  [body(): lax.ppermute(x, ('tensor', 'query'), pairs(flow, 0 if reduce_now else k,...]
    unnamed x50 -> x54, local copies, waits for them, and re-layouts: 12.5 us -> 18 us
    ppermute x4, starting transfers between devices: 10.1 us -> 5.02 us  [exchange(): lax.ppermute(value_of(lax.rem(rank + shift, size)), axis, [(d, (d + shift...]
    pallas_call x5 -> x4, Pallas kernels: 41.3 us -> 39.9 us  [backward_piece(): pl.pallas_call(kernel, grid=(steps,), in_specs=[pl.BlockSpec((parts, rows...]
  transfers between devices with their start and end apart: 44 -> 44, of which waited for: 19 -> 15; matrix products, arithmetic and copies ran while one was open for 1% -> 1% of each run, Pallas kernels for 30% -> 37%
where the time goes in v5:
time: 324 us; the launch traced here: 322 us
  Pallas kernels  137 us (42%)
  starting transfers between devices  104 us (32%)
  waiting for transfers between devices  54.3 us (17%)
  local copies, waits for them, and re-layouts  22.6 us (7%)
    ppermute x40, starting transfers between devices, body(): lax.ppermute(x, ('tensor', 'query'), pairs(flow, 0 if reduce_now else k,...  99.2 us
    ppermute x40, waiting for transfers between devices, body(): lax.ppermute(x, ('tensor', 'query'), pairs(flow, 0 if reduce_now else k,...  54.3 us
    pallas_call x5, Pallas kernels, forward_piece(): pl.pallas_call(kernel, grid=(steps,), in_specs=[pl.BlockSpec((parts, None...  43.1 us
    pallas_call x32, Pallas kernels, relay(): pl.pallas_call(kernel, grid_spec=pltpu.PrefetchScalarGridSpec(num_scalar_...  40.5 us
    pallas_call x4, Pallas kernels, backward_piece(): pl.pallas_call(kernel, grid=(steps,), in_specs=[pl.BlockSpec((parts, rows...  39.9 us
    unnamed x54, local copies, waits for them, and re-layouts  18 us
    pallas_call x4, Pallas kernels, norm_out(): pl.pallas_call(kernel, grid_spec=pltpu.PrefetchScalarGridSpec(num_scalar_...  7.57 us
  transfers between devices with their start and end apart: 44, of which 15 were waited for; matrix products, arithmetic and copies ran while one was open for 1% of the time, Pallas kernels for 37%

profile of v5, /device:TPU:0, one launch (start us, length us, event | category | flops | bytes accessed | tf_op | source)
XLA Modules:
  0.0 321.7 jit_solution(12680225213910215904)
XLA Ops:
  2.3 10.4 %forward_piece.5 = (bf16[4,64,4224]{2,1,0:T(8,128)(2,1)S(1)}, f32[8,128]{1,0:T(8,128)S(1)}) custom-call(bf16[4,2,64,2048]{3,2,1,0:T(8,128)(2,1)S(1)} %bitcast.31, bf16[2048,8192]{1,0:T(8,128)(2,1)} %refs_4_.23, bf16[2048,8192]{1,0:T(8,128)(2,1)} %refs_4_.23, bf16[2048,8192]{1,0:T(8,128)(2,1)} %refs_4_.23, bf16[2048,8192]{1,0:T(8,128)(2,1)} %refs_4_.23), custom_call_target="tpu_custom_call" | custom-call | bytes 720000 | tf_op jit(solution)/shard_map/forward_piece/pallas_call | solution.py:95
  14.5 5.7 %collective-permute-start = (bf16[64,4224]{1,0:T(8,128)(2,1)}, bf16[64,4224]{1,0:T(8,128)(2,1)}, u32[]{:S(2)}, u32[]{:S(2)}) collective-permute-start(bf16[64,4224]{1,0:T(8,128)(2,1)} %get-tuple-element.161), channel_id=1, source_target_pairs={{0,4},{13,9},{2,6},{15,11},{16,20},{29,25},{18,22},{31,27}} | collective-permute-start | bytes 1622024 | tf_op jit(solution)/shard_map/ppermute | solution.py:517
  21.7 10.4 %forward_piece.6 = (bf16[4,64,4224]{2,1,0:T(8,128)(2,1)S(1)}, f32[8,128]{1,0:T(8,128)S(1)}) custom-call(bf16[4,2,64,2048]{3,2,1,0:T(8,128)(2,1)S(1)} %bitcast.33, bf16[2048,8192]{1,0:T(8,128)(2,1)} %refs_4_.23, bf16[2048,8192]{1,0:T(8,128)(2,1)} %refs_4_.23, bf16[2048,8192]{1,0:T(8,128)(2,1)} %refs_4_.23, bf16[2048,8192]{1,0:T(8,128)(2,1)} %refs_4_.23, ...), custom_call_target="tpu_custom_call" | custom-call | bytes 720000 | tf_op jit(solution)/shard_map/forward_piece/pallas_call | solution.py:95
  49.0 4.4 %collective-permute-start.8 = (bf16[64,4224]{1,0:T(8,128)(2,1)S(1)}, bf16[64,4224]{1,0:T(8,128)(2,1)S(1)}, u32[]{:S(2)}, u32[]{:S(2)}) collective-permute-start(bf16[64,4224]{1,0:T(8,128)(2,1)S(1)} %relay.34.refs_3_), channel_id=1, source_target_pairs={{0,4},{4,8},{9,5},{13,9},{2,6},{6,10},{11,7},{15,11},{16,20},{20,2... | collective-permute-start | bytes 1622024 | tf_op jit(solution)/shard_map/ppermute | solution.py:517
  61.4 5.1 %collective-permute-start.5 = (bf16[64,4224]{1,0:T(8,128)(2,1)S(1)}, bf16[64,4224]{1,0:T(8,128)(2,1)S(1)}, u32[]{:S(2)}, u32[]{:S(2)}) collective-permute-start(bf16[64,4224]{1,0:T(8,128)(2,1)S(1)} %relay.36.refs_3_), channel_id=1, source_target_pairs={{0,4},{4,8},{8,12},{5,1},{9,5},{13,9},{2,6},{6,10},{10,14},{7,3},{... | collective-permute-start | bytes 1622024 | tf_op jit(solution)/shard_map/ppermute | solution.py:517
  73.1 5.0 %collective-permute-start.9 = (bf16[64,4224]{1,0:T(8,128)(2,1)S(1)}, bf16[64,4224]{1,0:T(8,128)(2,1)S(1)}, u32[]{:S(2)}, u32[]{:S(2)}) collective-permute-start(bf16[64,4224]{1,0:T(8,128)(2,1)S(1)} %relay.38.refs_3_), channel_id=1, source_target_pairs={{0,4},{4,8},{8,12},{5,1},{9,5},{13,9},{2,6},{6,10},{10,14},{7,3},{... | collective-permute-start | bytes 1622024 | tf_op jit(solution)/shard_map/ppermute | solution.py:517
  78.2 11.1 %forward_piece.7 = (bf16[4,64,4224]{2,1,0:T(8,128)(2,1)S(1)}, f32[8,128]{1,0:T(8,128)S(1)}) custom-call(bf16[4,2,64,2048]{3,2,1,0:T(8,128)(2,1)S(1)} %bitcast.34, bf16[2048,8192]{1,0:T(8,128)(2,1)} %refs_4_.23, bf16[2048,8192]{1,0:T(8,128)(2,1)} %refs_4_.23, bf16[2048,8192]{1,0:T(8,128)(2,1)} %refs_4_.23, bf16[2048,8192]{1,0:T(8,128)(2,1)} %refs_4_.23, ...), custom_call_target="tpu_custom_call" | custom-call | bytes 720000 | tf_op jit(solution)/shard_map/forward_piece/pallas_call | solution.py:95
  98.6 4.6 %collective-permute-start.13 = (bf16[64,4224]{1,0:T(8,128)(2,1)S(1)}, bf16[64,4224]{1,0:T(8,128)(2,1)S(1)}, u32[]{:S(2)}, u32[]{:S(2)}) collective-permute-start(bf16[64,4224]{1,0:T(8,128)(2,1)S(1)} %get-tuple-element.89.refs_4_), channel_id=1, source_target_pairs={{0,4},{4,8},{8,12},{5,1},{9,5},{13,9},{2,6},{6,10},{10,14},{7,3},{... | collective-permute-start | bytes 1622024 | tf_op jit(solution)/shard_map/ppermute | solution.py:517
  104.5 5.6 %forward_piece.8 = (bf16[4,64,4224]{2,1,0:T(8,128)(2,1)S(1)}, f32[8,128]{1,0:T(8,128)S(1)}) custom-call(bf16[4,2,64,2048]{3,2,1,0:T(8,128)(2,1)S(1)} %bitcast.35, bf16[2048,8192]{1,0:T(8,128)(2,1)} %refs_4_.23, bf16[2048,8192]{1,0:T(8,128)(2,1)} %refs_4_.23, bf16[2048,8192]{1,0:T(8,128)(2,1)} %refs_4_.23, bf16[2048,8192]{1,0:T(8,128)(2,1)} %refs_4_.23, ...), custom_call_target="tpu_custom_call" | custom-call | bytes 720000 | tf_op jit(solution)/shard_map/forward_piece/pallas_call | solution.py:95
  111.2 4.6 %collective-permute-start.14 = (bf16[64,4224]{1,0:T(8,128)(2,1)S(1)}, bf16[64,4224]{1,0:T(8,128)(2,1)S(1)}, u32[]{:S(2)}, u32[]{:S(2)}) collective-permute-start(bf16[64,4224]{1,0:T(8,128)(2,1)S(1)} %get-tuple-element.94.refs_4_), channel_id=1, source_target_pairs={{0,4},{4,8},{8,12},{5,1},{9,5},{13,9},{2,6},{6,10},{10,14},{7,3},{... | collective-permute-start | bytes 1622024 | tf_op jit(solution)/shard_map/ppermute | solution.py:517
  118.4 4.5 %collective-permute-start.18 = (bf16[64,4224]{1,0:T(8,128)(2,1)S(1)}, bf16[64,4224]{1,0:T(8,128)(2,1)S(1)}, u32[]{:S(2)}, u32[]{:S(2)}) collective-permute-start(bf16[64,4224]{1,0:T(8,128)(2,1)S(1)} %get-tuple-element.96.refs_4_), channel_id=1, source_target_pairs={{0,4},{4,8},{8,12},{5,1},{9,5},{13,9},{2,6},{6,10},{10,14},{7,3},{... | collective-permute-start | bytes 1622024 | tf_op jit(solution)/shard_map/ppermute | solution.py:517
  124.9 5.6 %forward_piece.9 = (bf16[4,64,4224]{2,1,0:T(8,128)(2,1)S(1)}, f32[8,128]{1,0:T(8,128)S(1)}) custom-call(bf16[4,2,64,2048]{3,2,1,0:T(8,128)(2,1)S(1)} %bitcast.37, bf16[2048,8192]{1,0:T(8,128)(2,1)} %refs_4_.23, bf16[2048,8192]{1,0:T(8,128)(2,1)} %refs_4_.23, bf16[2048,8192]{1,0:T(8,128)(2,1)} %refs_4_.23, ...), custom_call_target="tpu_custom_call", output_to_operand_aliasing={{0}: (5, {})} | custom-call | bytes 720000 | tf_op jit(solution)/shard_map/forward_piece/pallas_call | solution.py:95
  131.2 4.5 %collective-permute-start.15 = (bf16[64,4224]{1,0:T(8,128)(2,1)S(1)}, bf16[64,4224]{1,0:T(8,128)(2,1)S(1)}, u32[]{:S(2)}, u32[]{:S(2)}) collective-permute-start(bf16[64,4224]{1,0:T(8,128)(2,1)S(1)} %get-tuple-element.101.refs_4_), channel_id=1, source_target_pairs={{0,4},{4,8},{8,12},{5,1},{9,5},{13,9},{2,6},{6,10},{10,14},{7,3},{... | collective-permute-start | bytes 1622024 | tf_op jit(solution)/shard_map/ppermute | solution.py:517
  146.6 4.5 %collective-permute-done.15.refs_0_ = bf16[64,4224]{1,0:T(8,128)(2,1)S(1)} collective-permute-done((bf16[64,4224]{1,0:T(8,128)(2,1)S(1)}, bf16[64,4224]{1,0:T(8,128)(2,1)S(1)}, u32[]{:S(2)}, u32[]{:S(2)}) %collective-permute-start.15) | collective-permute-done | bytes 540704 | tf_op jit(solution)/shard_map/ppermute | solution.py:517
  158.2 4.5 %collective-permute-done.22.refs_0_ = bf16[64,4224]{1,0:T(8,128)(2,1)S(1)} collective-permute-done((bf16[64,4224]{1,0:T(8,128)(2,1)S(1)}, bf16[64,4224]{1,0:T(8,128)(2,1)S(1)}, u32[]{:S(2)}, u32[]{:S(2)}) %collective-permute-start.22) | collective-permute-done | bytes 540704 | tf_op jit(solution)/shard_map/ppermute | solution.py:517
  180.4 4.6 %collective-permute-start.23 = (bf16[64,4224]{1,0:T(8,128)(2,1)S(1)}, bf16[64,4224]{1,0:T(8,128)(2,1)S(1)}, u32[]{:S(2)}, u32[]{:S(2)}) collective-permute-start(bf16[64,4224]{1,0:T(8,128)(2,1)S(1)} %get-tuple-element.117.refs_4_), channel_id=1, source_target_pairs={{0,4},{4,8},{8,12},{5,1},{9,5},{13,9},{2,6},{6,10},{10,14},{7,3},{... | collective-permute-start | bytes 1622024 | tf_op jit(solution)/shard_map/ppermute | solution.py:517
  187.8 9.5 %collective-permute-done.25.refs_2_.refs_8_ = bf16[64,4224]{1,0:T(8,128)(2,1)S(1)} collective-permute-done((bf16[64,4224]{1,0:T(8,128)(2,1)S(1)}, bf16[64,4224]{1,0:T(8,128)(2,1)S(1)}, u32[]{:S(2)}, u32[]{:S(2)}) %collective-permute-start.25) | collective-permute-done | bytes 540704 | tf_op jit(solution)/shard_map/ppermute | solution.py:517
  201.8 4.4 %collective-permute-start.31 = (bf16[64,4224]{1,0:T(8,128)(2,1)}, bf16[64,4224]{1,0:T(8,128)(2,1)S(1)}, u32[]{:S(2)}, u32[]{:S(2)}) collective-permute-start(bf16[64,4224]{1,0:T(8,128)(2,1)} %get-tuple-element.126.refs_10_), channel_id=1, source_target_pairs={{0,4},{4,8},{8,12},{5,1},{9,5},{13,9},{2,6},{6,10},{10,14},{7,3},{... | collective-permute-start | bytes 1622024 | tf_op jit(solution)/shard_map/ppermute | solution.py:517
  207.6 9.2 %backward_piece.4 = (bf16[4,2,64,2048]{3,2,1,0:T(8,128)(2,1)}, f32[8,128]{1,0:T(8,128)S(1)}) custom-call(bf16[4,64,4224]{2,1,0:T(8,128)(2,1)S(1)} %get-tuple-element.124.refs_0_, bf16[4,64,4224]{2,1,0:T(8,128)(2,1)S(1)} %get-tuple-element.125.refs_1_, bf16[2048,8192]{1,0:T(8,128)(2,1)} %refs_4_.23, bf16[2048,8192]{1,0:T(8,128)(2,1)} %refs_4_.23, ...), custom_call_target="tpu_custom_call" | custom-call | bytes 720000 | tf_op jit(solution)/shard_map/backward_piece/pallas_call | solution.py:147
  217.9 4.6 %collective-permute-start.29 = (bf16[64,4224]{1,0:T(8,128)(2,1)S(1)}, bf16[64,4224]{1,0:T(8,128)(2,1)S(1)}, u32[]{:S(2)}, u32[]{:S(2)}) collective-permute-start(bf16[64,4224]{1,0:T(8,128)(2,1)S(1)} %get-tuple-element.128.x_ref.refs_3_), channel_id=1, source_target_pairs={{0,4},{4,8},{8,12},{5,1},{9,5},{13,9},{2,6},{6,10},{10,14},{7,3},{... | collective-permute-start | bytes 1622024 | tf_op jit(solution)/shard_map/ppermute | solution.py:517
  225.1 9.2 %backward_piece.5 = (bf16[4,2,64,2048]{3,2,1,0:T(8,128)(2,1)}, f32[8,128]{1,0:T(8,128)S(1)}) custom-call(bf16[4,64,4224]{2,1,0:T(8,128)(2,1)S(1)} %get-tuple-element.124.refs_0_, bf16[4,64,4224]{2,1,0:T(8,128)(2,1)S(1)} %get-tuple-element.125.refs_1_, bf16[2048,8192]{1,0:T(8,128)(2,1)} %refs_4_.23, ...), custom_call_target="tpu_custom_call", output_to_operand_aliasing={{0}: (10, {})} | custom-call | bytes 720000 | tf_op jit(solution)/shard_map/backward_piece/pallas_call | solution.py:147
  245.9 7.6 %collective-permute-done.34.refs_0_ = bf16[64,4224]{1,0:T(8,128)(2,1)S(1)} collective-permute-done((bf16[64,4224]{1,0:T(8,128)(2,1)S(1)}, bf16[64,4224]{1,0:T(8,128)(2,1)S(1)}, u32[]{:S(2)}, u32[]{:S(2)}) %collective-permute-start.34) | collective-permute-done | bytes 540704 | tf_op jit(solution)/shard_map/ppermute | solution.py:517
  282.6 10.4 %backward_piece.6 = (f32[4,64,2048]{2,1,0:T(8,128)S(1)}, f32[8,128]{1,0:T(8,128)S(1)}) custom-call(bf16[4,64,4224]{2,1,0:T(8,128)(2,1)S(1)} %get-tuple-element.150.refs_0_, bf16[2048,8192]{1,0:T(8,128)(2,1)} %refs_4_.23, bf16[2048,8192]{1,0:T(8,128)(2,1)} %refs_4_.23, bf16[2048,8192]{1,0:T(8,128)(2,1)} %refs_4_.23, bf16[2048,8192]{1,0:T(8,128)(2,1)} %refs_4_.23, ...), custom_call_target="tpu_custom_call" | custom-call | bytes 720000 | tf_op jit(solution)/shard_map/backward_piece/pallas_call | solution.py:147
  309.9 11.2 %backward_piece.7 = (bf16[4,2,64,2048]{3,2,1,0:T(8,128)(2,1)}, f32[8,128]{1,0:T(8,128)S(1)}) custom-call(bf16[4,64,4224]{2,1,0:T(8,128)(2,1)S(1)} %copy-done.18, bf16[2048,8192]{1,0:T(8,128)(2,1)} %refs_4_.23, bf16[2048,8192]{1,0:T(8,128)(2,1)} %refs_4_.23, bf16[2048,8192]{1,0:T(8,128)(2,1)} %refs_4_.23, ...), custom_call_target="tpu_custom_call", output_to_operand_aliasing={{0}: (6, {})} | custom-call | bytes 720000 | tf_op jit(solution)/shard_map/backward_piece/pallas_call | solution.py:147
  (205 shorter events, 158.6 us)
Async XLA Ops:
  14.5 22.6 %collective-permute-start = (bf16[64,4224]{1,0:T(8,128)(2,1)}, bf16[64,4224]{1,0:T(8,128)(2,1)}, u32[]{:S(2)}, u32[]{:S(2)}) collective-permute-start(bf16[64,4224]{1,0:T(8,128)(2,1)} %get-tuple-element.161), channel_id=1, source_target_pairs={{0,4},{13,9},{2,6},{15,11},{16,20},{29,25},{18,22},{31,27}} | collective-permute-start | bytes 1622024 | tf_op jit(solution)/shard_map/ppermute | solution.py:517
  20.3 21.5 %collective-permute-start.4 = (bf16[64,4224]{1,0:T(8,128)(2,1)}, bf16[64,4224]{1,0:T(8,128)(2,1)}, u32[]{:S(2)}, u32[]{:S(2)}) collective-permute-start(bf16[64,4224]{1,0:T(8,128)(2,1)} %get-tuple-element.160.refs_4_), channel_id=1, source_target_pairs={{12,8},{1,5},{14,10},{3,7},{28,24},{17,21},{30,26},{19,23}} | collective-permute-start | bytes 1622024 | tf_op jit(solution)/shard_map/ppermute | solution.py:517
  49.0 21.3 %collective-permute-start.8 = (bf16[64,4224]{1,0:T(8,128)(2,1)S(1)}, bf16[64,4224]{1,0:T(8,128)(2,1)S(1)}, u32[]{:S(2)}, u32[]{:S(2)}) collective-permute-start(bf16[64,4224]{1,0:T(8,128)(2,1)S(1)} %relay.34.refs_3_), channel_id=1, source_target_pairs={{0,4},{4,8},{9,5},{13,9},{2,6},{6,10},{11,7},{15,11},{16,20},{20,2... | collective-permute-start | bytes 1622024 | tf_op jit(solution)/shard_map/ppermute | solution.py:517
  60.1 29.3 %collective-permute-start.7 = (bf16[64,4224]{1,0:T(8,128)(2,1)S(1)}, bf16[64,4224]{1,0:T(8,128)(2,1)S(1)}, u32[]{:S(2)}, u32[]{:S(2)}) collective-permute-start(bf16[64,4224]{1,0:T(8,128)(2,1)S(1)} %relay.37.refs_3_), channel_id=1, source_target_pairs={{4,0},{8,4},{12,8},{1,5},{5,9},{9,13},{6,2},{10,6},{14,10},{3,7},{... | collective-permute-start | bytes 1622024 | tf_op jit(solution)/shard_map/ppermute | solution.py:517
  61.4 28.0 %collective-permute-start.5 = (bf16[64,4224]{1,0:T(8,128)(2,1)S(1)}, bf16[64,4224]{1,0:T(8,128)(2,1)S(1)}, u32[]{:S(2)}, u32[]{:S(2)}) collective-permute-start(bf16[64,4224]{1,0:T(8,128)(2,1)S(1)} %relay.36.refs_3_), channel_id=1, source_target_pairs={{0,4},{4,8},{8,12},{5,1},{9,5},{13,9},{2,6},{6,10},{10,14},{7,3},{... | collective-permute-start | bytes 1622024 | tf_op jit(solution)/shard_map/ppermute | solution.py:517
  73.1 20.4 %collective-permute-start.9 = (bf16[64,4224]{1,0:T(8,128)(2,1)S(1)}, bf16[64,4224]{1,0:T(8,128)(2,1)S(1)}, u32[]{:S(2)}, u32[]{:S(2)}) collective-permute-start(bf16[64,4224]{1,0:T(8,128)(2,1)S(1)} %relay.38.refs_3_), channel_id=1, source_target_pairs={{0,4},{4,8},{8,12},{5,1},{9,5},{13,9},{2,6},{6,10},{10,14},{7,3},{... | collective-permute-start | bytes 1622024 | tf_op jit(solution)/shard_map/ppermute | solution.py:517
  103.2 19.8 %collective-permute-start.12 = (bf16[64,4224]{1,0:T(8,128)(2,1)S(1)}, bf16[64,4224]{1,0:T(8,128)(2,1)S(1)}, u32[]{:S(2)}, u32[]{:S(2)}) collective-permute-start(bf16[64,4224]{1,0:T(8,128)(2,1)S(1)} %get-tuple-element.89.refs_4_), channel_id=1, source_target_pairs={{4,0},{8,4},{12,8},{1,5},{5,9},{9,13},{6,2},{10,6},{14,10},{3,7},{... | collective-permute-start | bytes 1622024 | tf_op jit(solution)/shard_map/ppermute | solution.py:517
  115.8 20.0 %collective-permute-start.16 = (bf16[64,4224]{1,0:T(8,128)(2,1)S(1)}, bf16[64,4224]{1,0:T(8,128)(2,1)S(1)}, u32[]{:S(2)}, u32[]{:S(2)}) collective-permute-start(bf16[64,4224]{1,0:T(8,128)(2,1)S(1)} %get-tuple-element.94.refs_4_), channel_id=1, source_target_pairs={{4,0},{8,4},{12,8},{1,5},{5,9},{9,13},{6,2},{10,6},{14,10},{3,7},{... | collective-permute-start | bytes 1622024 | tf_op jit(solution)/shard_map/ppermute | solution.py:517
  118.4 21.1 %collective-permute-start.18 = (bf16[64,4224]{1,0:T(8,128)(2,1)S(1)}, bf16[64,4224]{1,0:T(8,128)(2,1)S(1)}, u32[]{:S(2)}, u32[]{:S(2)}) collective-permute-start(bf16[64,4224]{1,0:T(8,128)(2,1)S(1)} %get-tuple-element.96.refs_4_), channel_id=1, source_target_pairs={{0,4},{4,8},{8,12},{5,1},{9,5},{13,9},{2,6},{6,10},{10,14},{7,3},{... | collective-permute-start | bytes 1622024 | tf_op jit(solution)/shard_map/ppermute | solution.py:517
  123.6 21.0 %collective-permute-start.17 = (bf16[64,4224]{1,0:T(8,128)(2,1)S(1)}, bf16[64,4224]{1,0:T(8,128)(2,1)S(1)}, u32[]{:S(2)}, u32[]{:S(2)}) collective-permute-start(bf16[64,4224]{1,0:T(8,128)(2,1)S(1)} %get-tuple-element.97.refs_5_.refs_4_), channel_id=1, source_target_pairs={{4,0},{8,4},{12,8},{1,5},{5,9},{9,13},{6,2},{10,6},{14,10},{3,7},{... | collective-permute-start | bytes 1622024 | tf_op jit(solution)/shard_map/ppermute | solution.py:517
  131.2 19.9 %collective-permute-start.15 = (bf16[64,4224]{1,0:T(8,128)(2,1)S(1)}, bf16[64,4224]{1,0:T(8,128)(2,1)S(1)}, u32[]{:S(2)}, u32[]{:S(2)}) collective-permute-start(bf16[64,4224]{1,0:T(8,128)(2,1)S(1)} %get-tuple-element.101.refs_4_), channel_id=1, source_target_pairs={{0,4},{4,8},{8,12},{5,1},{9,5},{13,9},{2,6},{6,10},{10,14},{7,3},{... | collective-permute-start | bytes 1622024 | tf_op jit(solution)/shard_map/ppermute | solution.py:517
  140.2 22.5 %collective-permute-start.22 = (bf16[64,4224]{1,0:T(8,128)(2,1)S(1)}, bf16[64,4224]{1,0:T(8,128)(2,1)S(1)}, u32[]{:S(2)}, u32[]{:S(2)}) collective-permute-start(bf16[64,4224]{1,0:T(8,128)(2,1)S(1)} %get-tuple-element.107.refs_4_), channel_id=1, source_target_pairs={{0,4},{4,8},{8,12},{5,1},{9,5},{13,9},{2,6},{6,10},{10,14},{7,3},{... | collective-permute-start | bytes 1622024 | tf_op jit(solution)/shard_map/ppermute | solution.py:517
  145.3 22.7 %collective-permute-start.21 = (bf16[64,4224]{1,0:T(8,128)(2,1)S(1)}, bf16[64,4224]{1,0:T(8,128)(2,1)S(1)}, u32[]{:S(2)}, u32[]{:S(2)}) collective-permute-start(bf16[64,4224]{1,0:T(8,128)(2,1)S(1)} %get-tuple-element.108.refs_4_), channel_id=1, source_target_pairs={{4,0},{8,4},{12,8},{1,5},{5,9},{9,13},{6,2},{10,6},{14,10},{3,7},{... | collective-permute-start | bytes 1622024 | tf_op jit(solution)/shard_map/ppermute | solution.py:517
  151.8 22.5 %collective-permute-start.19 = (bf16[64,4224]{1,0:T(8,128)(2,1)S(1)}, bf16[64,4224]{1,0:T(8,128)(2,1)S(1)}, u32[]{:S(2)}, u32[]{:S(2)}) collective-permute-start(bf16[64,4224]{1,0:T(8,128)(2,1)S(1)} %get-tuple-element.109.refs_4_), channel_id=1, source_target_pairs={{0,4},{4,8},{8,12},{5,1},{9,5},{13,9},{2,6},{6,10},{10,14},{7,3},{... | collective-permute-start | bytes 1622024 | tf_op jit(solution)/shard_map/ppermute | solution.py:517
  156.9 21.5 %collective-permute-start.24 = (bf16[64,4224]{1,0:T(8,128)(2,1)S(1)}, bf16[64,4224]{1,0:T(8,128)(2,1)S(1)}, u32[]{:S(2)}, u32[]{:S(2)}) collective-permute-start(bf16[64,4224]{1,0:T(8,128)(2,1)S(1)} %get-tuple-element.113.refs_4_), channel_id=1, source_target_pairs={{4,0},{8,4},{12,8},{1,5},{5,9},{9,13},{6,2},{10,6},{14,10},{3,7},{... | collective-permute-start | bytes 1622024 | tf_op jit(solution)/shard_map/ppermute | solution.py:517
  163.6 23.1 %collective-permute-start.26 = (bf16[64,4224]{1,0:T(8,128)(2,1)S(1)}, bf16[64,4224]{1,0:T(8,128)(2,1)S(1)}, u32[]{:S(2)}, u32[]{:S(2)}) collective-permute-start(bf16[64,4224]{1,0:T(8,128)(2,1)S(1)} %get-tuple-element.115.refs_4_), channel_id=1, source_target_pairs={{0,4},{4,8},{8,12},{5,1},{9,5},{13,9},{2,6},{6,10},{10,14},{7,3},{... | collective-permute-start | bytes 1622024 | tf_op jit(solution)/shard_map/ppermute | solution.py:517
  201.8 22.0 %collective-permute-start.31 = (bf16[64,4224]{1,0:T(8,128)(2,1)}, bf16[64,4224]{1,0:T(8,128)(2,1)S(1)}, u32[]{:S(2)}, u32[]{:S(2)}) collective-permute-start(bf16[64,4224]{1,0:T(8,128)(2,1)} %get-tuple-element.126.refs_10_), channel_id=1, source_target_pairs={{0,4},{4,8},{8,12},{5,1},{9,5},{13,9},{2,6},{6,10},{10,14},{7,3},{... | collective-permute-start | bytes 1622024 | tf_op jit(solution)/shard_map/ppermute | solution.py:517
  206.3 28.0 %collective-permute-start.30 = (bf16[64,4224]{1,0:T(8,128)(2,1)}, bf16[64,4224]{1,0:T(8,128)(2,1)}, u32[]{:S(2)}, u32[]{:S(2)}) collective-permute-start(bf16[64,4224]{1,0:T(8,128)(2,1)} %get-tuple-element.126.refs_10_), channel_id=1, source_target_pairs={{4,0},{8,4},{12,8},{1,5},{5,9},{9,13},{6,2},{10,6},{14,10},{3,7},{... | collective-permute-start | bytes 1622024 | tf_op jit(solution)/shard_map/ppermute | solution.py:517
  241.7 24.3 %collective-permute-start.32 = (bf16[64,4224]{1,0:T(8,128)(2,1)}, bf16[64,4224]{1,0:T(8,128)(2,1)}, u32[]{:S(2)}, u32[]{:S(2)}) collective-permute-start(bf16[64,4224]{1,0:T(8,128)(2,1)} %get-tuple-element.138.x_ref.refs_3_), channel_id=1, source_target_pairs={{4,0},{8,4},{5,9},{9,13},{6,2},{10,6},{7,11},{11,15},{20,16},{24,2... | collective-permute-start | bytes 1622024 | tf_op jit(solution)/shard_map/ppermute | solution.py:517
  244.4 28.3 %collective-permute-start.39 = (bf16[64,4224]{1,0:T(8,128)(2,1)}, bf16[64,4224]{1,0:T(8,128)(2,1)}, u32[]{:S(2)}, u32[]{:S(2)}) collective-permute-start(bf16[64,4224]{1,0:T(8,128)(2,1)} %get-tuple-element.142.x_ref.refs_3_), channel_id=1, source_target_pairs={{8,12},{5,1},{10,14},{7,3},{24,28},{21,17},{26,30},{23,19}} | collective-permute-start | bytes 1622024 | tf_op jit(solution)/shard_map/ppermute | solution.py:517
  256.4 21.2 %collective-permute-start.38 = (bf16[64,4224]{1,0:T(8,128)(2,1)}, bf16[64,4224]{1,0:T(8,128)(2,1)}, u32[]{:S(2)}, u32[]{:S(2)}) collective-permute-start(bf16[64,4224]{1,0:T(8,128)(2,1)} %get-tuple-element.143.x_ref.refs_3_), channel_id=1, source_target_pairs={{4,0},{9,13},{6,2},{11,15},{20,16},{25,29},{22,18},{27,31}} | collective-permute-start | bytes 1622024 | tf_op jit(solution)/shard_map/ppermute | solution.py:517
  263.1 33.2 %collective-permute-start.37 = (bf16[64,4224]{1,0:T(8,128)(2,1)}, bf16[64,4224]{1,0:T(8,128)(2,1)}, u32[]{:S(2)}, u32[]{:S(2)}) collective-permute-start(bf16[64,4224]{1,0:T(8,128)(2,1)} %get-tuple-element.145.x_ref.refs_3_), channel_id=1, source_target_pairs={{8,12},{5,1},{10,14},{7,3},{24,28},{21,17},{26,30},{23,19}} | collective-permute-start | bytes 1622024 | tf_op jit(solution)/shard_map/ppermute | solution.py:517
  271.5 29.0 %collective-permute-start.36 = (bf16[64,4224]{1,0:T(8,128)(2,1)}, bf16[64,4224]{1,0:T(8,128)(2,1)}, u32[]{:S(2)}, u32[]{:S(2)}) collective-permute-start(bf16[64,4224]{1,0:T(8,128)(2,1)} %get-tuple-element.146.x_ref), channel_id=1, source_target_pairs={{4,0},{9,13},{6,2},{11,15},{20,16},{25,29},{22,18},{27,31}} | collective-permute-start | bytes 1622024 | tf_op jit(solution)/shard_map/ppermute | solution.py:517
  295.3 25.7 %collective-permute-start.41 = (f32[8,512]{1,0:T(8,128)S(1)}, f32[8,512]{1,0:T(8,128)S(1)}, u32[]{:S(2)}, u32[]{:S(2)}) collective-permute-start(f32[8,512]{1,0:T(8,128)S(1)} %get-tuple-element.165.refs_7_), channel_id=1, source_target_pairs={{0,4},{4,8},{8,12},{12,0},{1,5},{5,9},{9,13},{13,1},{2,6},{6,10},{... | collective-permute-start | bytes 49160 | tf_op jit(solution)/shard_map/ppermute | solution.py:384
  (47 other events, 836.2 us)

commit v6 on v5

--- a/solution.py
+++ b/solution.py
@@ -14,7 +14,7 @@
 PIECES = 2
 SPLIT = 4
 SHORT, LONG = 0.2, 5.0
-LIMIT = 28 * 1024 * 1024
+LIMIT = 20 * 1024 * 1024
 
 F32, BF16 = jnp.float32, jnp.bfloat16
 ANY = pl.BlockSpec(memory_space=pl.ANY)
@@ -31,6 +31,10 @@
 
 def cost(microseconds):
     return pl.CostEstimate(flops=0, bytes_accessed=int(microseconds * 3.6e6), transcendentals=0)
+
+
+def in_hbm(x):
+    return pltpu.with_memory_space_constraint(x, pltpu.HBM)
 
 
 def project_rows(values, matrix):
@@ -107,7 +111,7 @@
         compiler_params=pltpu.CompilerParams(vmem_limit_bytes=LIMIT),
         cost_estimate=cost(SHORT),
         name="forward_piece",
-    )(by_share, *([w_out] * SPLIT), *more)
+    )(by_share, *([in_hbm(w_out)] * SPLIT), *more)
 
 
 def backward_piece(blocks, w_out, chunk, chunks, halves, piece, pieces, total, last, held, after):
@@ -157,7 +161,7 @@
         compiler_params=pltpu.CompilerParams(vmem_limit_bytes=LIMIT),
         cost_estimate=cost(SHORT),
         name="backward_piece",
-    )(*[g for _, g in blocks], *([w_out] * (n * SPLIT)), *sums, *extra)
+    )(*[in_hbm(g) for _, g in blocks], *([in_hbm(w_out)] * (n * SPLIT)), *sums, *extra)
 
 
 def relay(pos, flow, k, partial, came, held, after):
@@ -199,7 +203,7 @@
     if held is not None:
         alias[1 + len(args)] = 1
         specs.append(ANY)
-        args.append(held)
+        args.append(in_hbm(held))
         out_specs.append(ANY)
         out_shape.append(jax.ShapeDtypeStruct(held.shape, BF16))
     outs = pl.pallas_call(
@@ -218,6 +222,41 @@
         name="relay",
     )(pos, *args, *after)
     return outs[0], (outs[1] if held is not None else None)
+
+
+def store_last(pos, came, held, after):
+    parts = held.shape[0]
+
+    def kernel(pos_ref, a_ref, b_ref, *refs):
+        out_ref, sem = refs[-2:]
+        rank, way, place = pos_ref[0], pos_ref[1], pos_ref[2]
+        ends = (
+            (place == parts - 1, a_ref, rank - way * (parts - 1)),
+            (place == 0, b_ref, rank + way * (parts - 1)),
+        )
+        for at_end, came_ref, at in ends:
+            copy = pltpu.make_async_copy(came_ref, out_ref.at[lax.clamp(0, at, parts - 1)], sem)
+
+            @pl.when(at_end)
+            def _():
+                copy.start()
+                copy.wait()
+
+    return pl.pallas_call(
+        kernel,
+        grid_spec=pltpu.PrefetchScalarGridSpec(
+            num_scalar_prefetch=1,
+            grid=(1,),
+            in_specs=[ANY] * (3 + len(after)),
+            out_specs=ANY,
+            scratch_shapes=[pltpu.SemaphoreType.DMA],
+        ),
+        out_shape=jax.ShapeDtypeStruct(held.shape, BF16),
+        input_output_aliases={3: 0},
+        compiler_params=pltpu.CompilerParams(vmem_limit_bytes=LIMIT),
+        cost_estimate=cost(SHORT),
+        name="store_last",
+    )(pos, *came, in_hbm(held), *after)
 
 
 def take_block(partial, at):
@@ -335,7 +374,7 @@
         ),
         out_shape=[
             jax.ShapeDtypeStruct((rows, wide), BF16),
-            jax.ShapeDtypeStruct((parts, rows, wide), BF16),
+            pltpu.HBM((parts, rows, wide), BF16),
         ],
         compiler_params=pltpu.CompilerParams(vmem_limit_bytes=LIMIT),
         cost_estimate=cost(SHORT),
@@ -541,8 +580,8 @@
             else:
                 while work:
                     do_one(list(marks))
-                for flow in range(2):
-                    _, held[0] = relay(pos, flow, parts - 1, None, came[0, flow], held[0], list(marks))
+                marks[:] = [touch(came[0, 0])]
+                held[0] = store_last(pos, (came[0, 0], came[0, 1]), held[0], list(marks))
             gathered.append(held[0][:, :, half:])
         arrived = came
     both = jnp.stack(gathered, axis=1).reshape(tokens, 2 * kp)
@@ -560,8 +599,8 @@
     last = chunks - 1
     marks[:] = [backward(last, [(0, held[0])], None, HALVES == 1, 0, 1, [sketch_cols])]
     for h in range(1, HALVES):
-        for flow in range(2):
-            _, held[h] = relay(pos, flow, parts - 1, None, came[h, flow], held[h], list(marks))
+        marks[:] = [tie(marks[0], [came[h, 0]])]
+        held[h] = store_last(pos, (came[h, 0], came[h, 1]), held[h], list(marks))
     paired = exchange(lambda at: sketch_cols, "query", queriers, q_rank)
     paired = tie(paired, list(marks)).reshape(queriers * EX_DEV, sketch_cols.shape[1])
     score_part = lax.dot_general(

time: 324 us -> 338 us (1.043)
  Pallas kernels: 137 us -> 159 us
  local copies, waits for them, and re-layouts: 22.6 us -> 9.33 us
  waiting for transfers between devices: 54.3 us -> 60.9 us
    pallas_call x0 -> x2, Pallas kernels: none -> 19.4 us  [store_last(): pl.pallas_call(kernel, grid_spec=pltpu.PrefetchScalarGridSpec(num_scalar_...]
    unnamed x54 -> x28, local copies, waits for them, and re-layouts: 18 us -> 4.74 us
    ppermute x40, waiting for transfers between devices: 54.3 us -> 60.9 us  [body(): lax.ppermute(x, ('tensor', 'query'), pairs(flow, 0 if reduce_now else k,...]
    pallas_call x32 -> x28, Pallas kernels: 40.5 us -> 35.2 us  [relay(): pl.pallas_call(kernel, grid_spec=pltpu.PrefetchScalarGridSpec(num_scalar_...]
    pallas_call x4, Pallas kernels: 39.9 us -> 45.1 us  [backward_piece(): pl.pallas_call(kernel, grid=(steps,), in_specs=[pl.BlockSpec((parts, rows...]
  transfers between devices with their start and end apart: 44 -> 44, of which waited for: 15 -> 15; matrix products, arithmetic and copies ran while one was open for 1% -> 1% of each run, Pallas kernels for 37% -> 41%
where the time goes in v6:
time: 338 us; the launch traced here: 336 us
  Pallas kernels  159 us (47%)
  starting transfers between devices  103 us (30%)
  waiting for transfers between devices  60.9 us (18%)
  local copies, waits for them, and re-layouts  9.33 us (3%)
    ppermute x40, starting transfers between devices, body(): lax.ppermute(x, ('tensor', 'query'), pairs(flow, 0 if reduce_now else k,...  99 us
    ppermute x40, waiting for transfers between devices, body(): lax.ppermute(x, ('tensor', 'query'), pairs(flow, 0 if reduce_now else k,...  60.9 us
    pallas_call x4, Pallas kernels, backward_piece(): pl.pallas_call(kernel, grid=(steps,), in_specs=[pl.BlockSpec((parts, rows...  45.1 us
    pallas_call x5, Pallas kernels, forward_piece(): pl.pallas_call(kernel, grid=(steps,), in_specs=[pl.BlockSpec((parts, None...  43.1 us
    pallas_call x28, Pallas kernels, relay(): pl.pallas_call(kernel, grid_spec=pltpu.PrefetchScalarGridSpec(num_scalar_...  35.2 us
    pallas_call x2, Pallas kernels, store_last(): pl.pallas_call(kernel, grid_spec=pltpu.PrefetchScalarGridSpec(num_scalar_...  19.4 us
    pallas_call x4, Pallas kernels, norm_out(): pl.pallas_call(kernel, grid_spec=pltpu.PrefetchScalarGridSpec(num_scalar_...  10.6 us
  transfers between devices with their start and end apart: 44, of which 15 were waited for; matrix products, arithmetic and copies ran while one was open for 1% of the time, Pallas kernels for 41%

profile of v6, /device:TPU:0, one launch (start us, length us, event | category | flops | bytes accessed | tf_op | source)
XLA Modules:
  0.0 336.0 jit_solution(2329128966216986443)
XLA Ops:
  2.3 10.4 %forward_piece.5 = (bf16[4,64,4224]{2,1,0:T(8,128)(2,1)S(1)}, f32[8,128]{1,0:T(8,128)S(1)}) custom-call(bf16[4,2,64,2048]{3,2,1,0:T(8,128)(2,1)S(1)} %bitcast.31, bf16[2048,8192]{1,0:T(8,128)(2,1)} %refs_4_.23, bf16[2048,8192]{1,0:T(8,128)(2,1)} %refs_4_.23, bf16[2048,8192]{1,0:T(8,128)(2,1)} %refs_4_.23, bf16[2048,8192]{1,0:T(8,128)(2,1)} %refs_4_.23), custom_call_target="tpu_custom_call" | custom-call | bytes 720000 | tf_op jit(solution)/shard_map/forward_piece/pallas_call | solution.py:99
  14.6 5.7 %collective-permute-start = (bf16[64,4224]{1,0:T(8,128)(2,1)}, bf16[64,4224]{1,0:T(8,128)(2,1)}, u32[]{:S(2)}, u32[]{:S(2)}) collective-permute-start(bf16[64,4224]{1,0:T(8,128)(2,1)} %get-tuple-element.153), channel_id=1, source_target_pairs={{0,4},{13,9},{2,6},{15,11},{16,20},{29,25},{18,22},{31,27}} | collective-permute-start | bytes 1622024 | tf_op jit(solution)/shard_map/ppermute | solution.py:556
  21.8 10.4 %forward_piece.6 = (bf16[4,64,4224]{2,1,0:T(8,128)(2,1)S(1)}, f32[8,128]{1,0:T(8,128)S(1)}) custom-call(bf16[4,2,64,2048]{3,2,1,0:T(8,128)(2,1)S(1)} %bitcast.33, bf16[2048,8192]{1,0:T(8,128)(2,1)} %refs_4_.23, bf16[2048,8192]{1,0:T(8,128)(2,1)} %refs_4_.23, bf16[2048,8192]{1,0:T(8,128)(2,1)} %refs_4_.23, bf16[2048,8192]{1,0:T(8,128)(2,1)} %refs_4_.23, ...), custom_call_target="tpu_custom_call" | custom-call | bytes 720000 | tf_op jit(solution)/shard_map/forward_piece/pallas_call | solution.py:99
  61.3 5.1 %collective-permute-start.5 = (bf16[64,4224]{1,0:T(8,128)(2,1)S(1)}, bf16[64,4224]{1,0:T(8,128)(2,1)S(1)}, u32[]{:S(2)}, u32[]{:S(2)}) collective-permute-start(bf16[64,4224]{1,0:T(8,128)(2,1)S(1)} %relay.32.refs_3_), channel_id=1, source_target_pairs={{0,4},{4,8},{8,12},{5,1},{9,5},{13,9},{2,6},{6,10},{10,14},{7,3},{... | collective-permute-start | bytes 1622024 | tf_op jit(solution)/shard_map/ppermute | solution.py:556
  73.0 5.0 %collective-permute-start.9 = (bf16[64,4224]{1,0:T(8,128)(2,1)S(1)}, bf16[64,4224]{1,0:T(8,128)(2,1)S(1)}, u32[]{:S(2)}, u32[]{:S(2)}) collective-permute-start(bf16[64,4224]{1,0:T(8,128)(2,1)S(1)} %relay.34.refs_3_), channel_id=1, source_target_pairs={{0,4},{4,8},{8,12},{5,1},{9,5},{13,9},{2,6},{6,10},{10,14},{7,3},{... | collective-permute-start | bytes 1622024 | tf_op jit(solution)/shard_map/ppermute | solution.py:556
  78.1 11.1 %forward_piece.7 = (bf16[4,64,4224]{2,1,0:T(8,128)(2,1)S(1)}, f32[8,128]{1,0:T(8,128)S(1)}) custom-call(bf16[4,2,64,2048]{3,2,1,0:T(8,128)(2,1)S(1)} %bitcast.34, bf16[2048,8192]{1,0:T(8,128)(2,1)} %refs_4_.23, bf16[2048,8192]{1,0:T(8,128)(2,1)} %refs_4_.23, bf16[2048,8192]{1,0:T(8,128)(2,1)} %refs_4_.23, bf16[2048,8192]{1,0:T(8,128)(2,1)} %refs_4_.23, ...), custom_call_target="tpu_custom_call" | custom-call | bytes 720000 | tf_op jit(solution)/shard_map/forward_piece/pallas_call | solution.py:99
  103.4 5.6 %forward_piece.8 = (bf16[4,64,4224]{2,1,0:T(8,128)(2,1)S(1)}, f32[8,128]{1,0:T(8,128)S(1)}) custom-call(bf16[4,2,64,2048]{3,2,1,0:T(8,128)(2,1)S(1)} %bitcast.35, bf16[2048,8192]{1,0:T(8,128)(2,1)} %refs_4_.23, bf16[2048,8192]{1,0:T(8,128)(2,1)} %refs_4_.23, bf16[2048,8192]{1,0:T(8,128)(2,1)} %refs_4_.23, bf16[2048,8192]{1,0:T(8,128)(2,1)} %refs_4_.23, ...), custom_call_target="tpu_custom_call" | custom-call | bytes 720000 | tf_op jit(solution)/shard_map/forward_piece/pallas_call | solution.py:99
  110.9 4.6 %collective-permute-start.14 = (bf16[64,4224]{1,0:T(8,128)(2,1)S(1)}, bf16[64,4224]{1,0:T(8,128)(2,1)S(1)}, u32[]{:S(2)}, u32[]{:S(2)}) collective-permute-start(bf16[64,4224]{1,0:T(8,128)(2,1)S(1)} %get-tuple-element.90.refs_4_), channel_id=1, source_target_pairs={{0,4},{4,8},{8,12},{5,1},{9,5},{13,9},{2,6},{6,10},{10,14},{7,3},{... | collective-permute-start | bytes 1622024 | tf_op jit(solution)/shard_map/ppermute | solution.py:556
  118.1 5.3 %collective-permute-start.18 = (bf16[64,4224]{1,0:T(8,128)(2,1)S(1)}, bf16[64,4224]{1,0:T(8,128)(2,1)S(1)}, u32[]{:S(2)}, u32[]{:S(2)}) collective-permute-start(bf16[64,4224]{1,0:T(8,128)(2,1)S(1)} %get-tuple-element.92.refs_4_), channel_id=1, source_target_pairs={{0,4},{4,8},{8,12},{5,1},{9,5},{13,9},{2,6},{6,10},{10,14},{7,3},{... | collective-permute-start | bytes 1622024 | tf_op jit(solution)/shard_map/ppermute | solution.py:556
  126.1 5.6 %forward_piece.9 = (bf16[4,64,4224]{2,1,0:T(8,128)(2,1)S(1)}, f32[8,128]{1,0:T(8,128)S(1)}) custom-call(bf16[4,2,64,2048]{3,2,1,0:T(8,128)(2,1)S(1)} %bitcast.37, bf16[2048,8192]{1,0:T(8,128)(2,1)} %refs_4_.23, bf16[2048,8192]{1,0:T(8,128)(2,1)} %refs_4_.23, bf16[2048,8192]{1,0:T(8,128)(2,1)} %refs_4_.23, ...), custom_call_target="tpu_custom_call", output_to_operand_aliasing={{0}: (5, {})} | custom-call | bytes 720000 | tf_op jit(solution)/shard_map/forward_piece/pallas_call | solution.py:99
  132.4 5.3 %collective-permute-start.15 = (bf16[64,4224]{1,0:T(8,128)(2,1)S(1)}, bf16[64,4224]{1,0:T(8,128)(2,1)S(1)}, u32[]{:S(2)}, u32[]{:S(2)}) collective-permute-start(bf16[64,4224]{1,0:T(8,128)(2,1)S(1)} %get-tuple-element.97.refs_4_), channel_id=1, source_target_pairs={{0,4},{4,8},{8,12},{5,1},{9,5},{13,9},{2,6},{6,10},{10,14},{7,3},{... | collective-permute-start | bytes 1622024 | tf_op jit(solution)/shard_map/ppermute | solution.py:556
  141.0 4.6 %collective-permute-start.22 = (bf16[64,4224]{1,0:T(8,128)(2,1)S(1)}, bf16[64,4224]{1,0:T(8,128)(2,1)S(1)}, u32[]{:S(2)}, u32[]{:S(2)}) collective-permute-start(bf16[64,4224]{1,0:T(8,128)(2,1)S(1)} %get-tuple-element.103.refs_4_), channel_id=1, source_target_pairs={{0,4},{4,8},{8,12},{5,1},{9,5},{13,9},{2,6},{6,10},{10,14},{7,3},{... | collective-permute-start | bytes 1622024 | tf_op jit(solution)/shard_map/ppermute | solution.py:556
  174.7 4.6 %collective-permute-done.24.refs_0_ = bf16[64,4224]{1,0:T(8,128)(2,1)S(1)} collective-permute-done((bf16[64,4224]{1,0:T(8,128)(2,1)S(1)}, bf16[64,4224]{1,0:T(8,128)(2,1)S(1)}, u32[]{:S(2)}, u32[]{:S(2)}) %collective-permute-start.24) | collective-permute-done | bytes 540704 | tf_op jit(solution)/shard_map/ppermute | solution.py:556
  182.0 4.6 %collective-permute-start.23 = (bf16[64,4224]{1,0:T(8,128)(2,1)S(1)}, bf16[64,4224]{1,0:T(8,128)(2,1)S(1)}, u32[]{:S(2)}, u32[]{:S(2)}) collective-permute-start(bf16[64,4224]{1,0:T(8,128)(2,1)S(1)} %get-tuple-element.113.refs_4_), channel_id=1, source_target_pairs={{0,4},{4,8},{8,12},{5,1},{9,5},{13,9},{2,6},{6,10},{10,14},{7,3},{... | collective-permute-start | bytes 1622024 | tf_op jit(solution)/shard_map/ppermute | solution.py:556
  187.8 9.2 %collective-permute-done.25.refs_2_.refs_8_ = bf16[64,4224]{1,0:T(8,128)(2,1)S(1)} collective-permute-done((bf16[64,4224]{1,0:T(8,128)(2,1)S(1)}, bf16[64,4224]{1,0:T(8,128)(2,1)S(1)}, u32[]{:S(2)}, u32[]{:S(2)}) %collective-permute-start.25) | collective-permute-done | bytes 540704 | tf_op jit(solution)/shard_map/ppermute | solution.py:556
  202.6 4.5 %collective-permute-start.30 = (bf16[64,4224]{1,0:T(8,128)(2,1)}, bf16[64,4224]{1,0:T(8,128)(2,1)S(1)}, u32[]{:S(2)}, u32[]{:S(2)}) collective-permute-start(bf16[64,4224]{1,0:T(8,128)(2,1)} %get-tuple-element.122.refs_10_), channel_id=1, source_target_pairs={{0,4},{4,8},{8,12},{5,1},{9,5},{13,9},{2,6},{6,10},{10,14},{7,3},{... | collective-permute-start | bytes 1622024 | tf_op jit(solution)/shard_map/ppermute | solution.py:556
  208.4 11.0 %backward_piece.4 = (bf16[4,2,64,2048]{3,2,1,0:T(8,128)(2,1)}, f32[8,128]{1,0:T(8,128)S(1)}) custom-call(bf16[4,64,4224]{2,1,0:T(8,128)(2,1)} %get-tuple-element.120.refs_0_, bf16[4,64,4224]{2,1,0:T(8,128)(2,1)} %get-tuple-element.121.refs_1_, bf16[2048,8192]{1,0:T(8,128)(2,1)} %refs_4_.23, bf16[2048,8192]{1,0:T(8,128)(2,1)} %refs_4_.23, ...), custom_call_target="tpu_custom_call" | custom-call | bytes 720000 | tf_op jit(solution)/shard_map/backward_piece/pallas_call | solution.py:151
  221.3 4.6 %collective-permute-start.28 = (bf16[64,4224]{1,0:T(8,128)(2,1)S(1)}, bf16[64,4224]{1,0:T(8,128)(2,1)S(1)}, u32[]{:S(2)}, u32[]{:S(2)}) collective-permute-start(bf16[64,4224]{1,0:T(8,128)(2,1)S(1)} %get-tuple-element.124.x_ref.refs_3_), channel_id=1, source_target_pairs={{0,4},{4,8},{8,12},{5,1},{9,5},{13,9},{2,6},{6,10},{10,14},{7,3},{... | collective-permute-start | bytes 1622024 | tf_op jit(solution)/shard_map/ppermute | solution.py:556
  228.4 11.0 %backward_piece.5 = (bf16[4,2,64,2048]{3,2,1,0:T(8,128)(2,1)}, f32[8,128]{1,0:T(8,128)S(1)}) custom-call(bf16[4,64,4224]{2,1,0:T(8,128)(2,1)} %get-tuple-element.120.refs_0_, bf16[4,64,4224]{2,1,0:T(8,128)(2,1)} %get-tuple-element.121.refs_1_, bf16[2048,8192]{1,0:T(8,128)(2,1)} %refs_4_.23, ...), custom_call_target="tpu_custom_call", output_to_operand_aliasing={{0}: (10, {})} | custom-call | bytes 720000 | tf_op jit(solution)/shard_map/backward_piece/pallas_call | solution.py:151
  249.3 12.2 %collective-permute-done.33.refs_0_ = bf16[64,4224]{1,0:T(8,128)(2,1)S(1)} collective-permute-done((bf16[64,4224]{1,0:T(8,128)(2,1)S(1)}, bf16[64,4224]{1,0:T(8,128)(2,1)S(1)}, u32[]{:S(2)}, u32[]{:S(2)}) %collective-permute-start.33) | collective-permute-done | bytes 540704 | tf_op jit(solution)/shard_map/ppermute | solution.py:556
  277.7 7.0 %collective-permute-done.39.b_ref = bf16[64,4224]{1,0:T(8,128)(2,1)} collective-permute-done((bf16[64,4224]{1,0:T(8,128)(2,1)}, bf16[64,4224]{1,0:T(8,128)(2,1)}, u32[]{:S(2)}, u32[]{:S(2)}) %collective-permute-start.39) | collective-permute-done | bytes 540704 | tf_op jit(solution)/shard_map/ppermute | solution.py:556
  284.8 18.0 %store_last.2.refs_0_ = bf16[4,64,4224]{2,1,0:T(8,128)(2,1)} custom-call(s32[3]{0:T(128)S(1)} %pad_add_fusion.pos_ref, bf16[64,4224]{1,0:T(8,128)(2,1)S(1)} %collective-permute-done.38.x_ref.a_ref, bf16[64,4224]{1,0:T(8,128)(2,1)} %collective-permute-done.39.b_ref, bf16[4,64,4224]{2,1,0:T(8,128)(2,1)} %get-tuple-element.144.refs_0_, ...), custom_call_target="tpu_custom_call", output_to_operand_aliasing={{}: (3, {})} | custom-call | bytes 720000 | tf_op jit(solution)/shard_map/store_last/pallas_call | solution.py:245
  304.5 11.3 %backward_piece.6 = (f32[4,64,2048]{2,1,0:T(8,128)S(1)}, f32[8,128]{1,0:T(8,128)S(1)}) custom-call(bf16[4,64,4224]{2,1,0:T(8,128)(2,1)} %store_last.2.refs_0_, bf16[2048,8192]{1,0:T(8,128)(2,1)} %refs_4_.23, bf16[2048,8192]{1,0:T(8,128)(2,1)} %refs_4_.23, bf16[2048,8192]{1,0:T(8,128)(2,1)} %refs_4_.23, bf16[2048,8192]{1,0:T(8,128)(2,1)} %refs_4_.23, ...), custom_call_target="tpu_custom_call" | custom-call | bytes 720000 | tf_op jit(solution)/shard_map/backward_piece/pallas_call | solution.py:151
  323.4 11.9 %backward_piece.7 = (bf16[4,2,64,2048]{3,2,1,0:T(8,128)(2,1)}, f32[8,128]{1,0:T(8,128)S(1)}) custom-call(bf16[4,64,4224]{2,1,0:T(8,128)(2,1)} %store_last.3.refs_0_, bf16[2048,8192]{1,0:T(8,128)(2,1)} %refs_4_.23, bf16[2048,8192]{1,0:T(8,128)(2,1)} %refs_4_.23, bf16[2048,8192]{1,0:T(8,128)(2,1)} %refs_4_.23, ...), custom_call_target="tpu_custom_call", output_to_operand_aliasing={{0}: (6, {})} | custom-call | bytes 720000 | tf_op jit(solution)/shard_map/backward_piece/pallas_call | solution.py:151
  (178 shorter events, 145.7 us)
Async XLA Ops:
  14.6 22.3 %collective-permute-start = (bf16[64,4224]{1,0:T(8,128)(2,1)}, bf16[64,4224]{1,0:T(8,128)(2,1)}, u32[]{:S(2)}, u32[]{:S(2)}) collective-permute-start(bf16[64,4224]{1,0:T(8,128)(2,1)} %get-tuple-element.153), channel_id=1, source_target_pairs={{0,4},{13,9},{2,6},{15,11},{16,20},{29,25},{18,22},{31,27}} | collective-permute-start | bytes 1622024 | tf_op jit(solution)/shard_map/ppermute | solution.py:556
  20.3 21.3 %collective-permute-start.4 = (bf16[64,4224]{1,0:T(8,128)(2,1)}, bf16[64,4224]{1,0:T(8,128)(2,1)}, u32[]{:S(2)}, u32[]{:S(2)}) collective-permute-start(bf16[64,4224]{1,0:T(8,128)(2,1)} %get-tuple-element.152.refs_4_), channel_id=1, source_target_pairs={{12,8},{1,5},{14,10},{3,7},{28,24},{17,21},{30,26},{19,23}} | collective-permute-start | bytes 1622024 | tf_op jit(solution)/shard_map/ppermute | solution.py:556
  49.0 21.3 %collective-permute-start.8 = (bf16[64,4224]{1,0:T(8,128)(2,1)S(1)}, bf16[64,4224]{1,0:T(8,128)(2,1)S(1)}, u32[]{:S(2)}, u32[]{:S(2)}) collective-permute-start(bf16[64,4224]{1,0:T(8,128)(2,1)S(1)} %relay.30.refs_3_), channel_id=1, source_target_pairs={{0,4},{4,8},{9,5},{13,9},{2,6},{6,10},{11,7},{15,11},{16,20},{20,2... | collective-permute-start | bytes 1622024 | tf_op jit(solution)/shard_map/ppermute | solution.py:556
  60.0 29.3 %collective-permute-start.7 = (bf16[64,4224]{1,0:T(8,128)(2,1)S(1)}, bf16[64,4224]{1,0:T(8,128)(2,1)S(1)}, u32[]{:S(2)}, u32[]{:S(2)}) collective-permute-start(bf16[64,4224]{1,0:T(8,128)(2,1)S(1)} %relay.33.refs_3_), channel_id=1, source_target_pairs={{4,0},{8,4},{12,8},{1,5},{5,9},{9,13},{6,2},{10,6},{14,10},{3,7},{... | collective-permute-start | bytes 1622024 | tf_op jit(solution)/shard_map/ppermute | solution.py:556
  61.3 28.0 %collective-permute-start.5 = (bf16[64,4224]{1,0:T(8,128)(2,1)S(1)}, bf16[64,4224]{1,0:T(8,128)(2,1)S(1)}, u32[]{:S(2)}, u32[]{:S(2)}) collective-permute-start(bf16[64,4224]{1,0:T(8,128)(2,1)S(1)} %relay.32.refs_3_), channel_id=1, source_target_pairs={{0,4},{4,8},{8,12},{5,1},{9,5},{13,9},{2,6},{6,10},{10,14},{7,3},{... | collective-permute-start | bytes 1622024 | tf_op jit(solution)/shard_map/ppermute | solution.py:556
  102.1 21.3 %collective-permute-start.12 = (bf16[64,4224]{1,0:T(8,128)(2,1)S(1)}, bf16[64,4224]{1,0:T(8,128)(2,1)S(1)}, u32[]{:S(2)}, u32[]{:S(2)}) collective-permute-start(bf16[64,4224]{1,0:T(8,128)(2,1)S(1)} %get-tuple-element.85.refs_4_), channel_id=1, source_target_pairs={{4,0},{8,4},{12,8},{1,5},{5,9},{9,13},{6,2},{10,6},{14,10},{3,7},{... | collective-permute-start | bytes 1622024 | tf_op jit(solution)/shard_map/ppermute | solution.py:556
  110.9 20.8 %collective-permute-start.14 = (bf16[64,4224]{1,0:T(8,128)(2,1)S(1)}, bf16[64,4224]{1,0:T(8,128)(2,1)S(1)}, u32[]{:S(2)}, u32[]{:S(2)}) collective-permute-start(bf16[64,4224]{1,0:T(8,128)(2,1)S(1)} %get-tuple-element.90.refs_4_), channel_id=1, source_target_pairs={{0,4},{4,8},{8,12},{5,1},{9,5},{13,9},{2,6},{6,10},{10,14},{7,3},{... | collective-permute-start | bytes 1622024 | tf_op jit(solution)/shard_map/ppermute | solution.py:556
  115.5 22.1 %collective-permute-start.16 = (bf16[64,4224]{1,0:T(8,128)(2,1)S(1)}, bf16[64,4224]{1,0:T(8,128)(2,1)S(1)}, u32[]{:S(2)}, u32[]{:S(2)}) collective-permute-start(bf16[64,4224]{1,0:T(8,128)(2,1)S(1)} %get-tuple-element.90.refs_4_), channel_id=1, source_target_pairs={{4,0},{8,4},{12,8},{1,5},{5,9},{9,13},{6,2},{10,6},{14,10},{3,7},{... | collective-permute-start | bytes 1622024 | tf_op jit(solution)/shard_map/ppermute | solution.py:556
  118.1 22.2 %collective-permute-start.18 = (bf16[64,4224]{1,0:T(8,128)(2,1)S(1)}, bf16[64,4224]{1,0:T(8,128)(2,1)S(1)}, u32[]{:S(2)}, u32[]{:S(2)}) collective-permute-start(bf16[64,4224]{1,0:T(8,128)(2,1)S(1)} %get-tuple-element.92.refs_4_), channel_id=1, source_target_pairs={{0,4},{4,8},{8,12},{5,1},{9,5},{13,9},{2,6},{6,10},{10,14},{7,3},{... | collective-permute-start | bytes 1622024 | tf_op jit(solution)/shard_map/ppermute | solution.py:556
  124.8 20.8 %collective-permute-start.17 = (bf16[64,4224]{1,0:T(8,128)(2,1)S(1)}, bf16[64,4224]{1,0:T(8,128)(2,1)S(1)}, u32[]{:S(2)}, u32[]{:S(2)}) collective-permute-start(bf16[64,4224]{1,0:T(8,128)(2,1)S(1)} %get-tuple-element.93.refs_5_.refs_4_), channel_id=1, source_target_pairs={{4,0},{8,4},{12,8},{1,5},{5,9},{9,13},{6,2},{10,6},{14,10},{3,7},{... | collective-permute-start | bytes 1622024 | tf_op jit(solution)/shard_map/ppermute | solution.py:556
  141.0 21.4 %collective-permute-start.22 = (bf16[64,4224]{1,0:T(8,128)(2,1)S(1)}, bf16[64,4224]{1,0:T(8,128)(2,1)S(1)}, u32[]{:S(2)}, u32[]{:S(2)}) collective-permute-start(bf16[64,4224]{1,0:T(8,128)(2,1)S(1)} %get-tuple-element.103.refs_4_), channel_id=1, source_target_pairs={{0,4},{4,8},{8,12},{5,1},{9,5},{13,9},{2,6},{6,10},{10,14},{7,3},{... | collective-permute-start | bytes 1622024 | tf_op jit(solution)/shard_map/ppermute | solution.py:556
  147.0 20.7 %collective-permute-start.21 = (bf16[64,4224]{1,0:T(8,128)(2,1)S(1)}, bf16[64,4224]{1,0:T(8,128)(2,1)S(1)}, u32[]{:S(2)}, u32[]{:S(2)}) collective-permute-start(bf16[64,4224]{1,0:T(8,128)(2,1)S(1)} %get-tuple-element.104.refs_4_), channel_id=1, source_target_pairs={{4,0},{8,4},{12,8},{1,5},{5,9},{9,13},{6,2},{10,6},{14,10},{3,7},{... | collective-permute-start | bytes 1622024 | tf_op jit(solution)/shard_map/ppermute | solution.py:556
  151.5 22.5 %collective-permute-start.19 = (bf16[64,4224]{1,0:T(8,128)(2,1)S(1)}, bf16[64,4224]{1,0:T(8,128)(2,1)S(1)}, u32[]{:S(2)}, u32[]{:S(2)}) collective-permute-start(bf16[64,4224]{1,0:T(8,128)(2,1)S(1)} %get-tuple-element.105.refs_4_), channel_id=1, source_target_pairs={{0,4},{4,8},{8,12},{5,1},{9,5},{13,9},{2,6},{6,10},{10,14},{7,3},{... | collective-permute-start | bytes 1622024 | tf_op jit(solution)/shard_map/ppermute | solution.py:556
  157.5 21.8 %collective-permute-start.24 = (bf16[64,4224]{1,0:T(8,128)(2,1)S(1)}, bf16[64,4224]{1,0:T(8,128)(2,1)S(1)}, u32[]{:S(2)}, u32[]{:S(2)}) collective-permute-start(bf16[64,4224]{1,0:T(8,128)(2,1)S(1)} %get-tuple-element.109.refs_4_), channel_id=1, source_target_pairs={{4,0},{8,4},{12,8},{1,5},{5,9},{9,13},{6,2},{10,6},{14,10},{3,7},{... | collective-permute-start | bytes 1622024 | tf_op jit(solution)/shard_map/ppermute | solution.py:556
  163.1 23.5 %collective-permute-start.26 = (bf16[64,4224]{1,0:T(8,128)(2,1)S(1)}, bf16[64,4224]{1,0:T(8,128)(2,1)S(1)}, u32[]{:S(2)}, u32[]{:S(2)}) collective-permute-start(bf16[64,4224]{1,0:T(8,128)(2,1)S(1)} %get-tuple-element.111.refs_4_), channel_id=1, source_target_pairs={{0,4},{4,8},{8,12},{5,1},{9,5},{13,9},{2,6},{6,10},{10,14},{7,3},{... | collective-permute-start | bytes 1622024 | tf_op jit(solution)/shard_map/ppermute | solution.py:556
  202.6 24.6 %collective-permute-start.30 = (bf16[64,4224]{1,0:T(8,128)(2,1)}, bf16[64,4224]{1,0:T(8,128)(2,1)S(1)}, u32[]{:S(2)}, u32[]{:S(2)}) collective-permute-start(bf16[64,4224]{1,0:T(8,128)(2,1)} %get-tuple-element.122.refs_10_), channel_id=1, source_target_pairs={{0,4},{4,8},{8,12},{5,1},{9,5},{13,9},{2,6},{6,10},{10,14},{7,3},{... | collective-permute-start | bytes 1622024 | tf_op jit(solution)/shard_map/ppermute | solution.py:556
  207.1 32.4 %collective-permute-start.29 = (bf16[64,4224]{1,0:T(8,128)(2,1)}, bf16[64,4224]{1,0:T(8,128)(2,1)}, u32[]{:S(2)}, u32[]{:S(2)}) collective-permute-start(bf16[64,4224]{1,0:T(8,128)(2,1)} %get-tuple-element.122.refs_10_), channel_id=1, source_target_pairs={{4,0},{8,4},{12,8},{1,5},{5,9},{9,13},{6,2},{10,6},{14,10},{3,7},{... | collective-permute-start | bytes 1622024 | tf_op jit(solution)/shard_map/ppermute | solution.py:556
  221.3 21.9 %collective-permute-start.28 = (bf16[64,4224]{1,0:T(8,128)(2,1)S(1)}, bf16[64,4224]{1,0:T(8,128)(2,1)S(1)}, u32[]{:S(2)}, u32[]{:S(2)}) collective-permute-start(bf16[64,4224]{1,0:T(8,128)(2,1)S(1)} %get-tuple-element.124.x_ref.refs_3_), channel_id=1, source_target_pairs={{0,4},{4,8},{8,12},{5,1},{9,5},{13,9},{2,6},{6,10},{10,14},{7,3},{... | collective-permute-start | bytes 1622024 | tf_op jit(solution)/shard_map/ppermute | solution.py:556
  243.8 22.0 %collective-permute-start.31 = (bf16[64,4224]{1,0:T(8,128)(2,1)S(1)}, bf16[64,4224]{1,0:T(8,128)(2,1)}, u32[]{:S(2)}, u32[]{:S(2)}) collective-permute-start(bf16[64,4224]{1,0:T(8,128)(2,1)S(1)} %get-tuple-element.132.x_ref.refs_3_), channel_id=1, source_target_pairs={{4,8},{8,12},{5,1},{9,5},{6,10},{10,14},{7,3},{11,7},{20,24},{24,2... | collective-permute-start | bytes 1622024 | tf_op jit(solution)/shard_map/ppermute | solution.py:556
  246.6 26.5 %collective-permute-start.36 = (bf16[64,4224]{1,0:T(8,128)(2,1)S(1)}, bf16[64,4224]{1,0:T(8,128)(2,1)}, u32[]{:S(2)}, u32[]{:S(2)}) collective-permute-start(bf16[64,4224]{1,0:T(8,128)(2,1)S(1)} %get-tuple-element.136.x_ref.refs_3_), channel_id=1, source_target_pairs={{4,0},{8,4},{5,9},{9,13},{6,2},{10,6},{7,11},{11,15},{20,16},{24,2... | collective-permute-start | bytes 1622024 | tf_op jit(solution)/shard_map/ppermute | solution.py:556
  248.6 29.2 %collective-permute-start.38 = (bf16[64,4224]{1,0:T(8,128)(2,1)S(1)}, bf16[64,4224]{1,0:T(8,128)(2,1)S(1)}, u32[]{:S(2)}, u32[]{:S(2)}) collective-permute-start(bf16[64,4224]{1,0:T(8,128)(2,1)S(1)} %get-tuple-element.138.x_ref.refs_3_), channel_id=1, source_target_pairs={{8,12},{5,1},{10,14},{7,3},{24,28},{21,17},{26,30},{23,19}} | collective-permute-start | bytes 1622024 | tf_op jit(solution)/shard_map/ppermute | solution.py:556
  263.6 21.1 %collective-permute-start.39 = (bf16[64,4224]{1,0:T(8,128)(2,1)}, bf16[64,4224]{1,0:T(8,128)(2,1)}, u32[]{:S(2)}, u32[]{:S(2)}) collective-permute-start(bf16[64,4224]{1,0:T(8,128)(2,1)} %get-tuple-element.139.x_ref.refs_3_), channel_id=1, source_target_pairs={{4,0},{9,13},{6,2},{11,15},{20,16},{25,29},{22,18},{27,31}} | collective-permute-start | bytes 1622024 | tf_op jit(solution)/shard_map/ppermute | solution.py:556
  268.3 48.8 %collective-permute-start.35 = (bf16[64,4224]{1,0:T(8,128)(2,1)}, bf16[64,4224]{1,0:T(8,128)(2,1)S(1)}, u32[]{:S(2)}, u32[]{:S(2)}) collective-permute-start(bf16[64,4224]{1,0:T(8,128)(2,1)} %get-tuple-element.140.x_ref.refs_3_), channel_id=1, source_target_pairs={{8,12},{5,1},{10,14},{7,3},{24,28},{21,17},{26,30},{23,19}} | collective-permute-start | bytes 1622024 | tf_op jit(solution)/shard_map/ppermute | solution.py:556
  276.4 41.7 %collective-permute-start.37 = (bf16[64,4224]{1,0:T(8,128)(2,1)}, bf16[64,4224]{1,0:T(8,128)(2,1)S(1)}, u32[]{:S(2)}, u32[]{:S(2)}) collective-permute-start(bf16[64,4224]{1,0:T(8,128)(2,1)} %get-tuple-element.142), channel_id=1, source_target_pairs={{4,0},{9,13},{6,2},{11,15},{20,16},{25,29},{22,18},{27,31}} | collective-permute-start | bytes 1622024 | tf_op jit(solution)/shard_map/ppermute | solution.py:556
  (34 other events, 756.4 us)

commit v7 on v6

--- a/solution.py
+++ b/solution.py
@@ -161,7 +161,7 @@
         compiler_params=pltpu.CompilerParams(vmem_limit_bytes=LIMIT),
         cost_estimate=cost(SHORT),
         name="backward_piece",
-    )(*[in_hbm(g) for _, g in blocks], *([in_hbm(w_out)] * (n * SPLIT)), *sums, *extra)
+    )(*[g for _, g in blocks], *([in_hbm(w_out)] * (n * SPLIT)), *sums, *extra)
 
 
 def relay(pos, flow, k, partial, came, held, after):
@@ -203,7 +203,7 @@
     if held is not None:
         alias[1 + len(args)] = 1
         specs.append(ANY)
-        args.append(in_hbm(held))
+        args.append(held)
         out_specs.append(ANY)
         out_shape.append(jax.ShapeDtypeStruct(held.shape, BF16))
     outs = pl.pallas_call(
@@ -247,7 +247,7 @@
         grid_spec=pltpu.PrefetchScalarGridSpec(
             num_scalar_prefetch=1,
             grid=(1,),
-            in_specs=[ANY] * (3 + len(after)),
+            in_specs=[pl.BlockSpec(held.shape[1:], lambda i, w: (0, 0))] * 2 + [ANY] * (1 + len(after)),
             out_specs=ANY,
             scratch_shapes=[pltpu.SemaphoreType.DMA],
         ),
@@ -256,11 +256,32 @@
         compiler_params=pltpu.CompilerParams(vmem_limit_bytes=LIMIT),
         cost_estimate=cost(SHORT),
         name="store_last",
-    )(pos, *came, in_hbm(held), *after)
-
-
-def take_block(partial, at):
-    return lax.dynamic_index_in_dim(partial, at, 0, keepdims=False)
+    )(pos, *came, held, *after)
+
+
+def first_block(pos, flow, partial):
+    parts, rows, width = partial.shape
+
+    def there(i, w):
+        way = w[1] if flow == 0 else -w[1]
+        return lax.clamp(0, w[0] + way * (parts - 1), parts - 1), 0, 0
+
+    def kernel(pos_ref, p_ref, out_ref):
+        out_ref[...] = p_ref[...]
+
+    return pl.pallas_call(
+        kernel,
+        grid_spec=pltpu.PrefetchScalarGridSpec(
+            num_scalar_prefetch=1,
+            grid=(1,),
+            in_specs=[pl.BlockSpec((None, rows, width), there)],
+            out_specs=pl.BlockSpec((rows, width), lambda i, w: (0, 0)),
+        ),
+        out_shape=jax.ShapeDtypeStruct((rows, width), BF16),
+        compiler_params=pltpu.CompilerParams(vmem_limit_bytes=LIMIT),
+        cost_estimate=cost(SHORT),
+        name="first_block",
+    )(pos, partial)
 
 
 def norm_terms(p_ref, a_ref, b_ref, res_ref, grad_ref, gain_ref, at):
@@ -374,7 +395,7 @@
         ),
         out_shape=[
             jax.ShapeDtypeStruct((rows, wide), BF16),
-            pltpu.HBM((parts, rows, wide), BF16),
+            jax.ShapeDtypeStruct((parts, rows, wide), BF16),
         ],
         compiler_params=pltpu.CompilerParams(vmem_limit_bytes=LIMIT),
         cost_estimate=cost(SHORT),
@@ -415,16 +436,133 @@
     )(x)
 
 
-def exchange(value_of, axis, size, rank):
-    first = value_of(rank)
-    out = jnp.zeros((size,) + first.shape, first.dtype)
-    out = lax.dynamic_update_index_in_dim(out, first, rank, 0)
-    for shift in range(1, size):
-        got = lax.ppermute(
-            value_of(lax.rem(rank + shift, size)), axis, [(d, (d + shift) % size) for d in range(size)]
+def from_others(value, axis, size):
+    return [value] + [
+        lax.ppermute(value, axis, [(d, (d + shift) % size) for d in range(size)])
+        for shift in range(1, size)
+    ]
+
+
+def sketch_slice(pos, gathered, segment_ids, kp, after):
+    parts, rows, wide = gathered[0].shape
+    extra, mine = 2 * kp, kp // parts
+    chunks, tokens = len(gathered), segment_ids.shape[1]
+
+    def kernel(pos_ref, *refs):
+        out_ref, sum_ref = refs[-2:]
+        example = lax.broadcasted_iota(jnp.int32, (8, tokens), 0)
+        by_row = jnp.where(refs[chunks][...] == example, 1.0, 0.0).astype(BF16)
+        same = lax.broadcasted_iota(jnp.int32, (tokens, tokens), 0) == lax.broadcasted_iota(
+            jnp.int32, (tokens, tokens), 1
         )
-        out = lax.dynamic_update_index_in_dim(out, got, lax.rem(rank - shift + size, size), 0)
-    return out
+        weights = project_rows(jnp.where(same, 1.0, 0.0).astype(BF16), by_row)
+        weights = weights.reshape(parts, chunks, rows, 8)
+        for e in range(EX_DEV):
+            total = None
+            for c in range(chunks):
+                both = refs[c][...].reshape(parts * rows, extra)
+                weight = weights[:, c].reshape(parts * rows, 8)[:, e : e + 1]
+                part = (both.astype(F32) * weight).astype(BF16)
+                term = lax.dot_general(
+                    part, both, (((0,), (0,)), ((), ())), preferred_element_type=F32
+                )
+                total = term if total is None else total + term
+            sum_ref[e] = total
+        low = lax.broadcasted_iota(jnp.int32, (1, extra), 1) < kp
+        for r in range(parts):
+
+            @pl.when(pos_ref[0] == r)
+            def _():
+                for e in range(EX_DEV):
+                    for i in range(mine // 2):
+                        at = kp + r * mine + 2 * i
+                        left, right = sum_ref[e, at : at + 1, :], sum_ref[e, at + 1 : at + 2, :]
+                        out_ref[e : e + 1, i * extra : (i + 1) * extra] = jnp.where(
+                            low, left, pltpu.roll(right, kp, 1)
+                        )
+
+    return pl.pallas_call(
+        kernel,
+        grid_spec=pltpu.PrefetchScalarGridSpec(
+            num_scalar_prefetch=1,
+            grid=(1,),
+            in_specs=[pl.BlockSpec((parts, rows, extra), lambda i, w: (0, 0, wide // extra - 1))] * chunks
+            + [pl.BlockSpec(segment_ids.shape, lambda i, w: (0, 0))]
+            + [ANY] * len(after),
+            out_specs=pl.BlockSpec((EX_DEV, mine * kp), lambda i, w: (0, 0)),
+            scratch_shapes=[pltpu.VMEM((EX_DEV, extra, extra), F32)],
+        ),
+        out_shape=jax.ShapeDtypeStruct((EX_DEV, mine * kp), F32),
+        compiler_params=pltpu.CompilerParams(vmem_limit_bytes=LIMIT),
+        cost_estimate=cost(SHORT),
+        name="sketch_slice",
+    )(pos, *gathered, segment_ids, *after)
+
+
+def score_terms(pos, sketches, queries, after):
+    size = len(sketches)
+    n, depth = queries.shape
+
+    def kernel(pos_ref, *refs):
+        out_ref, all_ref = refs[-2:]
+        for back in range(size):
+            all_ref[lax.rem(pos_ref[3] - back + size, size)] = refs[back][...]
+        q = refs[size][...].astype(F32)
+        for d in range(size):
+            out_ref[d * EX_DEV : (d + 1) * EX_DEV, :] = lax.dot_general(
+                all_ref[d],
+                q,
+                (((1,), (1,)), ((), ())),
+                precision=lax.Precision.HIGHEST,
+                preferred_element_type=F32,
+            )
+
+    return pl.pallas_call(
+        kernel,
+        grid_spec=pltpu.PrefetchScalarGridSpec(
+            num_scalar_prefetch=1,
+            grid=(1,),
+            in_specs=[pl.BlockSpec((EX_DEV, depth), lambda i, w: (0, 0))] * size
+            + [pl.BlockSpec((n, depth), lambda i, w: (0, 0))]
+            + [ANY] * len(after),
+            out_specs=pl.BlockSpec((size * EX_DEV, n), lambda i, w: (0, 0)),
+            scratch_shapes=[pltpu.VMEM((size, EX_DEV, depth), F32)],
+        ),
+        out_shape=jax.ShapeDtypeStruct((size * EX_DEV, n), F32),
+        compiler_params=pltpu.CompilerParams(vmem_limit_bytes=LIMIT),
+        cost_estimate=cost(SHORT),
+        name="score_terms",
+    )(pos, *sketches, queries, *after)
+
+
+def score_sum(pos, terms, after):
+    size = len(terms)
+    shape = terms[0].shape
+
+    def kernel(pos_ref, *refs):
+        out_ref, all_ref = refs[-2:]
+        for back in range(size):
+            all_ref[lax.rem(pos_ref[0] - back + size, size)] = refs[back][...]
+        total = all_ref[0]
+        for d in range(1, size):
+            total = total + all_ref[d]
+        out_ref[...] = total
+
+    whole = pl.BlockSpec(shape, lambda i, w: (0, 0))
+    return pl.pallas_call(
+        kernel,
+        grid_spec=pltpu.PrefetchScalarGridSpec(
+            num_scalar_prefetch=1,
+            grid=(1,),
+            in_specs=[whole] * size + [ANY] * len(after),
+            out_specs=whole,
+            scratch_shapes=[pltpu.VMEM((size,) + shape, F32)],
+        ),
+        out_shape=jax.ShapeDtypeStruct(shape, F32),
+        compiler_params=pltpu.CompilerParams(vmem_limit_bytes=LIMIT),
+        cost_estimate=cost(SHORT),
+        name="score_sum",
+    )(pos, *terms, *after)
 
 
 def body(inputs, residual, out_grad, norm_gain, w_out, proj_in, proj_out, queries, segment_ids):
@@ -442,7 +580,7 @@
     kp = proj_out.shape[0]
 
     up = 1 - 2 * lax.rem(q_rank, 2)
-    pos = jnp.stack([rank, up, jnp.where(up == 1, rank, parts - 1 - rank)]).astype(jnp.int32)
+    pos = jnp.stack([rank, up, jnp.where(up == 1, rank, parts - 1 - rank), q_rank]).astype(jnp.int32)
 
     def pairs(flow, low, high):
         out = []
@@ -523,7 +661,7 @@
                 continue
             for h in range(HALVES):
                 if k == 0 and h > 0:
-                    if rs:
+                    if rs and slot > 1:
                         add_forward(slot, h, PIECES)
                     do_one([sent[h - 1, 1]])
                     grad[h], held[h] = norm_out(
@@ -538,10 +676,7 @@
                     if k == 0:
                         x = before = grad[h]
                     elif (h, flow) not in came:
-                        way = up if flow == 0 else -up
-                        x = take_block(
-                            partials[slot, h], jnp.clip(rank + way * (parts - k), 0, parts - 1)
-                        )
+                        x = first_block(pos, flow, partials[slot, h])
                     else:
                         x, held[h] = relay(
                             pos,
@@ -559,8 +694,14 @@
                         pairs(flow, 0 if reduce_now else k, parts - 2 if gather_now else k - 1),
                     )
                     sent[h, flow] = x
+                    if slot == 0 and k == 2 and (h, flow) == (HALVES - 1, 1) and chunks > 1 and HALVES > 1:
+                        add_forward(1, 1, PIECES)
+                        do_one([x])
+                        continue
                     if slot == 0 and k == parts - 1 and (h, flow) == (HALVES - 1, 1) and chunks > 1:
-                        add_forward(1, 0, 1)
+                        work.insert(0, ((1, 0), functools.partial(forward, 1, 0, 0, 1)))
+                    if slot == 0 and work and work[0][0] == (1, 1):
+                        continue
                     if k > 0 and (slot > 0 or k > 1) and not (slot == 1 and work and k == 1 and flow == 0):
                         do_one([x], slot == chunks)
                 if k == 0 and slot == chunks and h == HALVES - 1:
@@ -582,38 +723,18 @@
                     do_one(list(marks))
                 marks[:] = [touch(came[0, 0])]
                 held[0] = store_last(pos, (came[0, 0], came[0, 1]), held[0], list(marks))
-            gathered.append(held[0][:, :, half:])
+            gathered.append(held[0])
         arrived = came
-    both = jnp.stack(gathered, axis=1).reshape(tokens, 2 * kp)
-    member = segment_ids[0][None, :] == jnp.arange(EX_DEV, dtype=jnp.int32)[:, None]
-    weighted = jnp.where(member[:, :, None], both[None, :, kp:], 0)
-    sketch = lax.dot_general(
-        weighted,
-        jnp.broadcast_to(both[None, :, :kp], (EX_DEV, tokens, kp)),
-        (((1,), (1,)), ((0,), (0,))),
-        preferred_element_type=F32,
-    )
-    sketch_cols = lax.dynamic_slice_in_dim(sketch, rank * (kp // parts), kp // parts, 1)
-    sketch_cols = sketch_cols.reshape(EX_DEV, kp // parts * kp)
-
     last = chunks - 1
-    marks[:] = [backward(last, [(0, held[0])], None, HALVES == 1, 0, 1, [sketch_cols])]
+    sketch = sketch_slice(pos, gathered, segment_ids, kp, [])
+    marks[:] = [backward(last, [(0, held[0])], None, HALVES == 1, 0, 1, [sketch])]
     for h in range(1, HALVES):
         marks[:] = [tie(marks[0], [came[h, 0]])]
         held[h] = store_last(pos, (came[h, 0], came[h, 1]), held[h], list(marks))
-    paired = exchange(lambda at: sketch_cols, "query", queriers, q_rank)
-    paired = tie(paired, list(marks)).reshape(queriers * EX_DEV, sketch_cols.shape[1])
-    score_part = lax.dot_general(
-        paired,
-        queries.astype(F32),
-        (((1,), (1,)), ((), ())),
-        precision=lax.Precision.HIGHEST,
-    )
+    terms = score_terms(pos, from_others(sketch, "query", queriers), queries, list(marks))
     for h in range(1, HALVES):
-        marks[:] = [
-            backward(last, [(h, held[h])], totals.get(last), h == HALVES - 1, 0, 1, [score_part])
-        ]
-    scores = jnp.sum(tie(exchange(lambda at: score_part, "tensor", parts, rank), list(marks)), axis=0)
+        marks[:] = [backward(last, [(h, held[h])], totals.get(last), h == HALVES - 1, 0, 1, [terms])]
+    scores = score_sum(pos, from_others(terms, "tensor", parts), list(marks))
     return (result[0].reshape(1, tokens, -1), scores)
 
 

time: 338 us -> 309 us (0.914)
  Pallas kernels: 159 us -> 126 us
  waiting for transfers between devices: 60.9 us -> 80.6 us
  local copies, waits for them, and re-layouts: 9.33 us -> 1.77 us
  starting transfers between devices: 103 us -> 97.4 us
    ppermute x40, waiting for transfers between devices: 60.9 us -> 80.6 us  [body(): lax.ppermute(x, ('tensor', 'query'), pairs(flow, 0 if reduce_now else k,...]
    pallas_call x2, Pallas kernels: 19.4 us -> 1.24 us  [store_last(): pl.pallas_call(kernel, grid_spec=pltpu.PrefetchScalarGridSpec(num_scalar_...]
    pallas_call x28, Pallas kernels: 35.2 us -> 19.4 us  [relay(): pl.pallas_call(kernel, grid_spec=pltpu.PrefetchScalarGridSpec(num_scalar_...]
    pallas_call x0 -> x7, Pallas kernels: none -> 9.08 us  [the longest x1 3.88 us: score_terms(): pl.pallas_call(kernel, grid_spec=pltpu.PrefetchScalarGridSpec(num_scalar_...]
    ppermute x40, starting transfers between devices: 99 us -> 93.5 us  [body(): lax.ppermute(x, ('tensor', 'query'), pairs(flow, 0 if reduce_now else k,...]
    pallas_call x4, Pallas kernels: 45.1 us -> 40 us  [backward_piece(): pl.pallas_call(kernel, grid=(steps,), in_specs=[pl.BlockSpec((parts, rows...]
  transfers between devices with their start and end apart: 44 -> 44, of which waited for: 15 -> 16; matrix products, arithmetic and copies ran while one was open for 1% -> 0% of each run, Pallas kernels for 41% -> 34%
where the time goes in v7:
time: 309 us; the launch traced here: 307 us
  Pallas kernels  126 us (41%)
  starting transfers between devices  97.4 us (32%)
  waiting for transfers between devices  80.6 us (26%)
    ppermute x40, starting transfers between devices, body(): lax.ppermute(x, ('tensor', 'query'), pairs(flow, 0 if reduce_now else k,...  93.5 us
    ppermute x40, waiting for transfers between devices, body(): lax.ppermute(x, ('tensor', 'query'), pairs(flow, 0 if reduce_now else k,...  80.6 us
    pallas_call x5, Pallas kernels, forward_piece(): pl.pallas_call(kernel, grid=(steps,), in_specs=[pl.BlockSpec((parts, None...  42.6 us
    pallas_call x4, Pallas kernels, backward_piece(): pl.pallas_call(kernel, grid=(steps,), in_specs=[pl.BlockSpec((parts, rows...  40 us
    pallas_call x28, Pallas kernels, relay(): pl.pallas_call(kernel, grid_spec=pltpu.PrefetchScalarGridSpec(num_scalar_...  19.4 us
    pallas_call x4, Pallas kernels, norm_out(): pl.pallas_call(kernel, grid_spec=pltpu.PrefetchScalarGridSpec(num_scalar_...  7.57 us
  transfers between devices with their start and end apart: 44, of which 16 were waited for; matrix products, arithmetic and copies ran while one was open for 0% of the time, Pallas kernels for 34%

profile of v7, /device:TPU:0, one launch (start us, length us, event | category | flops | bytes accessed | tf_op | source)
XLA Modules:
  0.0 307.2 jit_solution(13040155723093199712)
XLA Ops:
  2.2 10.4 %forward_piece.5 = (bf16[4,64,4224]{2,1,0:T(8,128)(2,1)S(1)}, f32[8,128]{1,0:T(8,128)S(1)}) custom-call(bf16[4,2,64,2048]{3,2,1,0:T(8,128)(2,1)S(1)} %bitcast.6, bf16[2048,8192]{1,0:T(8,128)(2,1)} %refs_4_.23, bf16[2048,8192]{1,0:T(8,128)(2,1)} %refs_4_.23, bf16[2048,8192]{1,0:T(8,128)(2,1)} %refs_4_.23, bf16[2048,8192]{1,0:T(8,128)(2,1)} %refs_4_.23), custom_call_target="tpu_custom_call" | custom-call | bytes 720000 | tf_op jit(solution)/shard_map/forward_piece/pallas_call | solution.py:99
  13.9 5.0 %collective-permute-start.3 = (bf16[64,4224]{1,0:T(8,128)(2,1)S(1)}, bf16[64,4224]{1,0:T(8,128)(2,1)S(1)}, u32[]{:S(2)}, u32[]{:S(2)}) collective-permute-start(bf16[64,4224]{1,0:T(8,128)(2,1)S(1)} %first_block.7), channel_id=1, source_target_pairs={{0,4},{13,9},{2,6},{15,11},{16,20},{29,25},{18,22},{31,27}} | collective-permute-start | bytes 1622024 | tf_op jit(solution)/shard_map/ppermute | solution.py:691
  20.2 10.4 %forward_piece.6 = (bf16[4,64,4224]{2,1,0:T(8,128)(2,1)S(1)}, f32[8,128]{1,0:T(8,128)S(1)}) custom-call(bf16[4,2,64,2048]{3,2,1,0:T(8,128)(2,1)S(1)} %bitcast.8, bf16[2048,8192]{1,0:T(8,128)(2,1)} %refs_4_.23, bf16[2048,8192]{1,0:T(8,128)(2,1)} %refs_4_.23, bf16[2048,8192]{1,0:T(8,128)(2,1)} %refs_4_.23, bf16[2048,8192]{1,0:T(8,128)(2,1)} %refs_4_.23, ...), custom_call_target="tpu_custom_call" | custom-call | bytes 720000 | tf_op jit(solution)/shard_map/forward_piece/pallas_call | solution.py:99
  37.8 7.3 %collective-permute-done.1.refs_0_ = bf16[64,4224]{1,0:T(8,128)(2,1)S(1)} collective-permute-done((bf16[64,4224]{1,0:T(8,128)(2,1)S(1)}, bf16[64,4224]{1,0:T(8,128)(2,1)S(1)}, u32[]{:S(2)}, u32[]{:S(2)}) %collective-permute-start.1) | collective-permute-done | bytes 540704 | tf_op jit(solution)/shard_map/ppermute | solution.py:691
  45.7 4.6 %collective-permute-start.8 = (bf16[64,4224]{1,0:T(8,128)(2,1)S(1)}, bf16[64,4224]{1,0:T(8,128)(2,1)S(1)}, u32[]{:S(2)}, u32[]{:S(2)}) collective-permute-start(bf16[64,4224]{1,0:T(8,128)(2,1)S(1)} %relay.30.refs_3_), channel_id=1, source_target_pairs={{0,4},{4,8},{9,5},{13,9},{2,6},{6,10},{11,7},{15,11},{16,20},{20,2... | collective-permute-start | bytes 1622024 | tf_op jit(solution)/shard_map/ppermute | solution.py:691
  51.6 5.6 %forward_piece.7 = (bf16[4,64,4224]{2,1,0:T(8,128)(2,1)S(1)}, f32[8,128]{1,0:T(8,128)S(1)}) custom-call(bf16[4,2,64,2048]{3,2,1,0:T(8,128)(2,1)S(1)} %bitcast.9, bf16[2048,8192]{1,0:T(8,128)(2,1)} %refs_4_.23, bf16[2048,8192]{1,0:T(8,128)(2,1)} %refs_4_.23, bf16[2048,8192]{1,0:T(8,128)(2,1)} %refs_4_.23, bf16[2048,8192]{1,0:T(8,128)(2,1)} %refs_4_.23, ...), custom_call_target="tpu_custom_call" | custom-call | bytes 720000 | tf_op jit(solution)/shard_map/forward_piece/pallas_call | solution.py:99
  59.8 4.6 %collective-permute-start.5 = (bf16[64,4224]{1,0:T(8,128)(2,1)S(1)}, bf16[64,4224]{1,0:T(8,128)(2,1)S(1)}, u32[]{:S(2)}, u32[]{:S(2)}) collective-permute-start(bf16[64,4224]{1,0:T(8,128)(2,1)S(1)} %relay.32.refs_3_), channel_id=1, source_target_pairs={{0,4},{4,8},{8,12},{5,1},{9,5},{13,9},{2,6},{6,10},{10,14},{7,3},{... | collective-permute-start | bytes 1622024 | tf_op jit(solution)/shard_map/ppermute | solution.py:691
  70.8 5.1 %collective-permute-start.9 = (bf16[64,4224]{1,0:T(8,128)(2,1)S(1)}, bf16[64,4224]{1,0:T(8,128)(2,1)S(1)}, u32[]{:S(2)}, u32[]{:S(2)}) collective-permute-start(bf16[64,4224]{1,0:T(8,128)(2,1)S(1)} %relay.34.refs_3_), channel_id=1, source_target_pairs={{0,4},{4,8},{8,12},{5,1},{9,5},{13,9},{2,6},{6,10},{10,14},{7,3},{... | collective-permute-start | bytes 1622024 | tf_op jit(solution)/shard_map/ppermute | solution.py:691
  76.0 10.6 %forward_piece.8 = (bf16[4,64,4224]{2,1,0:T(8,128)(2,1)S(1)}, f32[8,128]{1,0:T(8,128)S(1)}) custom-call(bf16[4,2,64,2048]{3,2,1,0:T(8,128)(2,1)S(1)} %bitcast.10, bf16[2048,8192]{1,0:T(8,128)(2,1)} %refs_4_.23, bf16[2048,8192]{1,0:T(8,128)(2,1)} %refs_4_.23, bf16[2048,8192]{1,0:T(8,128)(2,1)} %refs_4_.23, bf16[2048,8192]{1,0:T(8,128)(2,1)} %refs_4_.23, ...), custom_call_target="tpu_custom_call" | custom-call | bytes 720000 | tf_op jit(solution)/shard_map/forward_piece/pallas_call | solution.py:99
  100.6 5.6 %forward_piece.9 = (bf16[4,64,4224]{2,1,0:T(8,128)(2,1)S(1)}, f32[8,128]{1,0:T(8,128)S(1)}) custom-call(bf16[4,2,64,2048]{3,2,1,0:T(8,128)(2,1)S(1)} %bitcast.11, bf16[2048,8192]{1,0:T(8,128)(2,1)} %refs_4_.23, bf16[2048,8192]{1,0:T(8,128)(2,1)} %refs_4_.23, bf16[2048,8192]{1,0:T(8,128)(2,1)} %refs_4_.23, ...), custom_call_target="tpu_custom_call", output_to_operand_aliasing={{0}: (5, {})} | custom-call | bytes 720000 | tf_op jit(solution)/shard_map/forward_piece/pallas_call | solution.py:99
  107.3 4.6 %collective-permute-start.12 = (bf16[64,4224]{1,0:T(8,128)(2,1)S(1)}, bf16[64,4224]{1,0:T(8,128)(2,1)S(1)}, u32[]{:S(2)}, u32[]{:S(2)}) collective-permute-start(bf16[64,4224]{1,0:T(8,128)(2,1)S(1)} %get-tuple-element.90.refs_4_), channel_id=1, source_target_pairs={{0,4},{4,8},{8,12},{5,1},{9,5},{13,9},{2,6},{6,10},{10,14},{7,3},{... | collective-permute-start | bytes 1622024 | tf_op jit(solution)/shard_map/ppermute | solution.py:691
  114.5 4.5 %collective-permute-start.18 = (bf16[64,4224]{1,0:T(8,128)(2,1)S(1)}, bf16[64,4224]{1,0:T(8,128)(2,1)S(1)}, u32[]{:S(2)}, u32[]{:S(2)}) collective-permute-start(bf16[64,4224]{1,0:T(8,128)(2,1)S(1)} %get-tuple-element.95.refs_4_), channel_id=1, source_target_pairs={{0,4},{4,8},{8,12},{5,1},{9,5},{13,9},{2,6},{6,10},{10,14},{7,3},{... | collective-permute-start | bytes 1622024 | tf_op jit(solution)/shard_map/ppermute | solution.py:691
  131.2 4.5 %collective-permute-done.18.refs_0_ = bf16[64,4224]{1,0:T(8,128)(2,1)S(1)} collective-permute-done((bf16[64,4224]{1,0:T(8,128)(2,1)S(1)}, bf16[64,4224]{1,0:T(8,128)(2,1)S(1)}, u32[]{:S(2)}, u32[]{:S(2)}) %collective-permute-start.18) | collective-permute-done | bytes 540704 | tf_op jit(solution)/shard_map/ppermute | solution.py:691
  154.4 4.5 %collective-permute-done.22.refs_0_ = bf16[64,4224]{1,0:T(8,128)(2,1)S(1)} collective-permute-done((bf16[64,4224]{1,0:T(8,128)(2,1)S(1)}, bf16[64,4224]{1,0:T(8,128)(2,1)S(1)}, u32[]{:S(2)}, u32[]{:S(2)}) %collective-permute-start.22) | collective-permute-done | bytes 540704 | tf_op jit(solution)/shard_map/ppermute | solution.py:691
  177.1 4.6 %collective-permute-start.23 = (bf16[64,4224]{1,0:T(8,128)(2,1)S(1)}, bf16[64,4224]{1,0:T(8,128)(2,1)S(1)}, u32[]{:S(2)}, u32[]{:S(2)}) collective-permute-start(bf16[64,4224]{1,0:T(8,128)(2,1)S(1)} %get-tuple-element.113.refs_4_), channel_id=1, source_target_pairs={{0,4},{4,8},{8,12},{5,1},{9,5},{13,9},{2,6},{6,10},{10,14},{7,3},{... | collective-permute-start | bytes 1622024 | tf_op jit(solution)/shard_map/ppermute | solution.py:691
  183.8 9.6 %collective-permute-done.25.refs_2_.refs_8_ = bf16[64,4224]{1,0:T(8,128)(2,1)S(1)} collective-permute-done((bf16[64,4224]{1,0:T(8,128)(2,1)S(1)}, bf16[64,4224]{1,0:T(8,128)(2,1)S(1)}, u32[]{:S(2)}, u32[]{:S(2)}) %collective-permute-start.25) | collective-permute-done | bytes 540704 | tf_op jit(solution)/shard_map/ppermute | solution.py:691
  204.0 9.2 %backward_piece.4 = (bf16[4,2,64,2048]{3,2,1,0:T(8,128)(2,1)}, f32[8,128]{1,0:T(8,128)S(1)}) custom-call(bf16[4,64,4224]{2,1,0:T(8,128)(2,1)S(1)} %get-tuple-element.120.refs_0_, bf16[4,64,4224]{2,1,0:T(8,128)(2,1)S(1)} %get-tuple-element.121.refs_1_, bf16[2048,8192]{1,0:T(8,128)(2,1)} %refs_4_.23, bf16[2048,8192]{1,0:T(8,128)(2,1)} %refs_4_.23, ...), custom_call_target="tpu_custom_call" | custom-call | bytes 720000 | tf_op jit(solution)/shard_map/backward_piece/pallas_call | solution.py:151
  214.3 4.6 %collective-permute-start.28 = (bf16[64,4224]{1,0:T(8,128)(2,1)S(1)}, bf16[64,4224]{1,0:T(8,128)(2,1)S(1)}, u32[]{:S(2)}, u32[]{:S(2)}) collective-permute-start(bf16[64,4224]{1,0:T(8,128)(2,1)S(1)} %get-tuple-element.124.x_ref.refs_3_), channel_id=1, source_target_pairs={{0,4},{4,8},{8,12},{5,1},{9,5},{13,9},{2,6},{6,10},{10,14},{7,3},{... | collective-permute-start | bytes 1622024 | tf_op jit(solution)/shard_map/ppermute | solution.py:691
  221.5 9.2 %backward_piece.5 = (bf16[4,2,64,2048]{3,2,1,0:T(8,128)(2,1)}, f32[8,128]{1,0:T(8,128)S(1)}) custom-call(bf16[4,64,4224]{2,1,0:T(8,128)(2,1)S(1)} %get-tuple-element.120.refs_0_, bf16[4,64,4224]{2,1,0:T(8,128)(2,1)S(1)} %get-tuple-element.121.refs_1_, bf16[2048,8192]{1,0:T(8,128)(2,1)} %refs_4_.23, ...), custom_call_target="tpu_custom_call", output_to_operand_aliasing={{0}: (10, {})} | custom-call | bytes 720000 | tf_op jit(solution)/shard_map/backward_piece/pallas_call | solution.py:151
  239.3 11.0 %collective-permute-done.33.refs_0_ = bf16[64,4224]{1,0:T(8,128)(2,1)S(1)} collective-permute-done((bf16[64,4224]{1,0:T(8,128)(2,1)S(1)}, bf16[64,4224]{1,0:T(8,128)(2,1)S(1)}, u32[]{:S(2)}, u32[]{:S(2)}) %collective-permute-start.33) | collective-permute-done | bytes 540704 | tf_op jit(solution)/shard_map/ppermute | solution.py:691
  253.6 8.3 %collective-permute-done.36.refs_0_ = bf16[64,4224]{1,0:T(8,128)(2,1)S(1)} collective-permute-done((bf16[64,4224]{1,0:T(8,128)(2,1)S(1)}, bf16[64,4224]{1,0:T(8,128)(2,1)S(1)}, u32[]{:S(2)}, u32[]{:S(2)}) %collective-permute-start.36) | collective-permute-done | bytes 540704 | tf_op jit(solution)/shard_map/ppermute | solution.py:691
  263.9 9.6 %collective-permute-done.39.b_ref = bf16[64,4224]{1,0:T(8,128)(2,1)S(1)} collective-permute-done((bf16[64,4224]{1,0:T(8,128)(2,1)S(1)}, bf16[64,4224]{1,0:T(8,128)(2,1)S(1)}, u32[]{:S(2)}, u32[]{:S(2)}) %collective-permute-start.39) | collective-permute-done | bytes 540704 | tf_op jit(solution)/shard_map/ppermute | solution.py:691
  275.9 10.5 %backward_piece.6 = (f32[4,64,2048]{2,1,0:T(8,128)S(1)}, f32[8,128]{1,0:T(8,128)S(1)}) custom-call(bf16[4,64,4224]{2,1,0:T(8,128)(2,1)S(1)} %store_last.2.refs_1_.refs_0_, bf16[2048,8192]{1,0:T(8,128)(2,1)} %refs_4_.23, bf16[2048,8192]{1,0:T(8,128)(2,1)} %refs_4_.23, bf16[2048,8192]{1,0:T(8,128)(2,1)} %refs_4_.23, bf16[2048,8192]{1,0:T(8,128)(2,1)} %refs_4_.23, ...), custom_call_target="tpu_custom_call" | custom-call | bytes 720000 | tf_op jit(solution)/shard_map/backward_piece/pallas_call | solution.py:151
  294.8 11.2 %backward_piece.7 = (bf16[4,2,64,2048]{3,2,1,0:T(8,128)(2,1)}, f32[8,128]{1,0:T(8,128)S(1)}) custom-call(bf16[4,64,4224]{2,1,0:T(8,128)(2,1)S(1)} %store_last.3.refs_0_, bf16[2048,8192]{1,0:T(8,128)(2,1)} %refs_4_.23, bf16[2048,8192]{1,0:T(8,128)(2,1)} %refs_4_.23, bf16[2048,8192]{1,0:T(8,128)(2,1)} %refs_4_.23, ...), custom_call_target="tpu_custom_call", output_to_operand_aliasing={{0}: (6, {})} | custom-call | bytes 720000 | tf_op jit(solution)/shard_map/backward_piece/pallas_call | solution.py:151
  (151 shorter events, 130.6 us)
Async XLA Ops:
  13.9 19.9 %collective-permute-start.3 = (bf16[64,4224]{1,0:T(8,128)(2,1)S(1)}, bf16[64,4224]{1,0:T(8,128)(2,1)S(1)}, u32[]{:S(2)}, u32[]{:S(2)}) collective-permute-start(bf16[64,4224]{1,0:T(8,128)(2,1)S(1)} %first_block.7), channel_id=1, source_target_pairs={{0,4},{13,9},{2,6},{15,11},{16,20},{29,25},{18,22},{31,27}} | collective-permute-start | bytes 1622024 | tf_op jit(solution)/shard_map/ppermute | solution.py:691
  34.6 22.6 %collective-permute-start.4 = (bf16[64,4224]{1,0:T(8,128)(2,1)S(1)}, bf16[64,4224]{1,0:T(8,128)(2,1)S(1)}, u32[]{:S(2)}, u32[]{:S(2)}) collective-permute-start(bf16[64,4224]{1,0:T(8,128)(2,1)S(1)} %relay.28.refs_3_), channel_id=1, source_target_pairs={{0,4},{4,8},{9,5},{13,9},{2,6},{6,10},{11,7},{15,11},{16,20},{20,2... | collective-permute-start | bytes 1622024 | tf_op jit(solution)/shard_map/ppermute | solution.py:691
  37.1 20.8 %collective-permute-start.6 = (bf16[64,4224]{1,0:T(8,128)(2,1)S(1)}, bf16[64,4224]{1,0:T(8,128)(2,1)S(1)}, u32[]{:S(2)}, u32[]{:S(2)}) collective-permute-start(bf16[64,4224]{1,0:T(8,128)(2,1)S(1)} %relay.29.refs_3_), channel_id=1, source_target_pairs={{8,4},{12,8},{1,5},{5,9},{10,6},{14,10},{3,7},{7,11},{24,20},{28,2... | collective-permute-start | bytes 1622024 | tf_op jit(solution)/shard_map/ppermute | solution.py:691
  45.7 22.5 %collective-permute-start.8 = (bf16[64,4224]{1,0:T(8,128)(2,1)S(1)}, bf16[64,4224]{1,0:T(8,128)(2,1)S(1)}, u32[]{:S(2)}, u32[]{:S(2)}) collective-permute-start(bf16[64,4224]{1,0:T(8,128)(2,1)S(1)} %relay.30.refs_3_), channel_id=1, source_target_pairs={{0,4},{4,8},{9,5},{13,9},{2,6},{6,10},{11,7},{15,11},{16,20},{20,2... | collective-permute-start | bytes 1622024 | tf_op jit(solution)/shard_map/ppermute | solution.py:691
  58.5 28.1 %collective-permute-start.7 = (bf16[64,4224]{1,0:T(8,128)(2,1)S(1)}, bf16[64,4224]{1,0:T(8,128)(2,1)S(1)}, u32[]{:S(2)}, u32[]{:S(2)}) collective-permute-start(bf16[64,4224]{1,0:T(8,128)(2,1)S(1)} %relay.33.refs_3_), channel_id=1, source_target_pairs={{4,0},{8,4},{12,8},{1,5},{5,9},{9,13},{6,2},{10,6},{14,10},{3,7},{... | collective-permute-start | bytes 1622024 | tf_op jit(solution)/shard_map/ppermute | solution.py:691
  59.8 26.8 %collective-permute-start.5 = (bf16[64,4224]{1,0:T(8,128)(2,1)S(1)}, bf16[64,4224]{1,0:T(8,128)(2,1)S(1)}, u32[]{:S(2)}, u32[]{:S(2)}) collective-permute-start(bf16[64,4224]{1,0:T(8,128)(2,1)S(1)} %relay.32.refs_3_), channel_id=1, source_target_pairs={{0,4},{4,8},{8,12},{5,1},{9,5},{13,9},{2,6},{6,10},{10,14},{7,3},{... | collective-permute-start | bytes 1622024 | tf_op jit(solution)/shard_map/ppermute | solution.py:691
  70.8 20.6 %collective-permute-start.9 = (bf16[64,4224]{1,0:T(8,128)(2,1)S(1)}, bf16[64,4224]{1,0:T(8,128)(2,1)S(1)}, u32[]{:S(2)}, u32[]{:S(2)}) collective-permute-start(bf16[64,4224]{1,0:T(8,128)(2,1)S(1)} %relay.34.refs_3_), channel_id=1, source_target_pairs={{0,4},{4,8},{8,12},{5,1},{9,5},{13,9},{2,6},{6,10},{10,14},{7,3},{... | collective-permute-start | bytes 1622024 | tf_op jit(solution)/shard_map/ppermute | solution.py:691
  99.3 19.8 %collective-permute-start.13 = (bf16[64,4224]{1,0:T(8,128)(2,1)S(1)}, bf16[64,4224]{1,0:T(8,128)(2,1)S(1)}, u32[]{:S(2)}, u32[]{:S(2)}) collective-permute-start(bf16[64,4224]{1,0:T(8,128)(2,1)S(1)} %get-tuple-element.87.refs_5_), channel_id=1, source_target_pairs={{4,0},{8,4},{12,8},{1,5},{5,9},{9,13},{6,2},{10,6},{14,10},{3,7},{... | collective-permute-start | bytes 1622024 | tf_op jit(solution)/shard_map/ppermute | solution.py:691
  114.5 21.2 %collective-permute-start.18 = (bf16[64,4224]{1,0:T(8,128)(2,1)S(1)}, bf16[64,4224]{1,0:T(8,128)(2,1)S(1)}, u32[]{:S(2)}, u32[]{:S(2)}) collective-permute-start(bf16[64,4224]{1,0:T(8,128)(2,1)S(1)} %get-tuple-element.95.refs_4_), channel_id=1, source_target_pairs={{0,4},{4,8},{8,12},{5,1},{9,5},{13,9},{2,6},{6,10},{10,14},{7,3},{... | collective-permute-start | bytes 1622024 | tf_op jit(solution)/shard_map/ppermute | solution.py:691
  119.7 21.1 %collective-permute-start.17 = (bf16[64,4224]{1,0:T(8,128)(2,1)S(1)}, bf16[64,4224]{1,0:T(8,128)(2,1)S(1)}, u32[]{:S(2)}, u32[]{:S(2)}) collective-permute-start(bf16[64,4224]{1,0:T(8,128)(2,1)S(1)} %get-tuple-element.96.refs_4_), channel_id=1, source_target_pairs={{4,0},{8,4},{12,8},{1,5},{5,9},{9,13},{6,2},{10,6},{14,10},{3,7},{... | collective-permute-start | bytes 1622024 | tf_op jit(solution)/shard_map/ppermute | solution.py:691
  124.8 22.5 %collective-permute-start.15 = (bf16[64,4224]{1,0:T(8,128)(2,1)S(1)}, bf16[64,4224]{1,0:T(8,128)(2,1)S(1)}, u32[]{:S(2)}, u32[]{:S(2)}) collective-permute-start(bf16[64,4224]{1,0:T(8,128)(2,1)S(1)} %get-tuple-element.97.refs_4_), channel_id=1, source_target_pairs={{0,4},{4,8},{8,12},{5,1},{9,5},{13,9},{2,6},{6,10},{10,14},{7,3},{... | collective-permute-start | bytes 1622024 | tf_op jit(solution)/shard_map/ppermute | solution.py:691
  129.9 22.5 %collective-permute-start.20 = (bf16[64,4224]{1,0:T(8,128)(2,1)S(1)}, bf16[64,4224]{1,0:T(8,128)(2,1)S(1)}, u32[]{:S(2)}, u32[]{:S(2)}) collective-permute-start(bf16[64,4224]{1,0:T(8,128)(2,1)S(1)} %get-tuple-element.101.refs_4_), channel_id=1, source_target_pairs={{4,0},{8,4},{12,8},{1,5},{5,9},{9,13},{6,2},{10,6},{14,10},{3,7},{... | collective-permute-start | bytes 1622024 | tf_op jit(solution)/shard_map/ppermute | solution.py:691
  136.4 22.5 %collective-permute-start.22 = (bf16[64,4224]{1,0:T(8,128)(2,1)S(1)}, bf16[64,4224]{1,0:T(8,128)(2,1)S(1)}, u32[]{:S(2)}, u32[]{:S(2)}) collective-permute-start(bf16[64,4224]{1,0:T(8,128)(2,1)S(1)} %get-tuple-element.103.refs_4_), channel_id=1, source_target_pairs={{0,4},{4,8},{8,12},{5,1},{9,5},{13,9},{2,6},{6,10},{10,14},{7,3},{... | collective-permute-start | bytes 1622024 | tf_op jit(solution)/shard_map/ppermute | solution.py:691
  141.5 22.7 %collective-permute-start.21 = (bf16[64,4224]{1,0:T(8,128)(2,1)S(1)}, bf16[64,4224]{1,0:T(8,128)(2,1)S(1)}, u32[]{:S(2)}, u32[]{:S(2)}) collective-permute-start(bf16[64,4224]{1,0:T(8,128)(2,1)S(1)} %get-tuple-element.104.refs_4_), channel_id=1, source_target_pairs={{4,0},{8,4},{12,8},{1,5},{5,9},{9,13},{6,2},{10,6},{14,10},{3,7},{... | collective-permute-start | bytes 1622024 | tf_op jit(solution)/shard_map/ppermute | solution.py:691
  148.0 22.5 %collective-permute-start.19 = (bf16[64,4224]{1,0:T(8,128)(2,1)S(1)}, bf16[64,4224]{1,0:T(8,128)(2,1)S(1)}, u32[]{:S(2)}, u32[]{:S(2)}) collective-permute-start(bf16[64,4224]{1,0:T(8,128)(2,1)S(1)} %get-tuple-element.105.refs_4_), channel_id=1, source_target_pairs={{0,4},{4,8},{8,12},{5,1},{9,5},{13,9},{2,6},{6,10},{10,14},{7,3},{... | collective-permute-start | bytes 1622024 | tf_op jit(solution)/shard_map/ppermute | solution.py:691
  153.1 22.1 %collective-permute-start.24 = (bf16[64,4224]{1,0:T(8,128)(2,1)S(1)}, bf16[64,4224]{1,0:T(8,128)(2,1)S(1)}, u32[]{:S(2)}, u32[]{:S(2)}) collective-permute-start(bf16[64,4224]{1,0:T(8,128)(2,1)S(1)} %get-tuple-element.109.refs_4_), channel_id=1, source_target_pairs={{4,0},{8,4},{12,8},{1,5},{5,9},{9,13},{6,2},{10,6},{14,10},{3,7},{... | collective-permute-start | bytes 1622024 | tf_op jit(solution)/shard_map/ppermute | solution.py:691
  159.7 23.0 %collective-permute-start.26 = (bf16[64,4224]{1,0:T(8,128)(2,1)S(1)}, bf16[64,4224]{1,0:T(8,128)(2,1)S(1)}, u32[]{:S(2)}, u32[]{:S(2)}) collective-permute-start(bf16[64,4224]{1,0:T(8,128)(2,1)S(1)} %get-tuple-element.111.refs_4_), channel_id=1, source_target_pairs={{0,4},{4,8},{8,12},{5,1},{9,5},{13,9},{2,6},{6,10},{10,14},{7,3},{... | collective-permute-start | bytes 1622024 | tf_op jit(solution)/shard_map/ppermute | solution.py:691
  198.3 22.0 %collective-permute-start.30 = (bf16[64,4224]{1,0:T(8,128)(2,1)}, bf16[64,4224]{1,0:T(8,128)(2,1)S(1)}, u32[]{:S(2)}, u32[]{:S(2)}) collective-permute-start(bf16[64,4224]{1,0:T(8,128)(2,1)} %get-tuple-element.122.refs_10_), channel_id=1, source_target_pairs={{0,4},{4,8},{8,12},{5,1},{9,5},{13,9},{2,6},{6,10},{10,14},{7,3},{... | collective-permute-start | bytes 1622024 | tf_op jit(solution)/shard_map/ppermute | solution.py:691
  202.7 28.0 %collective-permute-start.29 = (bf16[64,4224]{1,0:T(8,128)(2,1)}, bf16[64,4224]{1,0:T(8,128)(2,1)}, u32[]{:S(2)}, u32[]{:S(2)}) collective-permute-start(bf16[64,4224]{1,0:T(8,128)(2,1)} %get-tuple-element.122.refs_10_), channel_id=1, source_target_pairs={{4,0},{8,4},{12,8},{1,5},{5,9},{9,13},{6,2},{10,6},{14,10},{3,7},{... | collective-permute-start | bytes 1622024 | tf_op jit(solution)/shard_map/ppermute | solution.py:691
  236.7 25.2 %collective-permute-start.36 = (bf16[64,4224]{1,0:T(8,128)(2,1)S(1)}, bf16[64,4224]{1,0:T(8,128)(2,1)S(1)}, u32[]{:S(2)}, u32[]{:S(2)}) collective-permute-start(bf16[64,4224]{1,0:T(8,128)(2,1)S(1)} %get-tuple-element.136.x_ref.refs_3_), channel_id=1, source_target_pairs={{4,0},{8,4},{5,9},{9,13},{6,2},{10,6},{7,11},{11,15},{20,16},{24,2... | collective-permute-start | bytes 1622024 | tf_op jit(solution)/shard_map/ppermute | solution.py:691
  238.6 25.2 %collective-permute-start.38 = (bf16[64,4224]{1,0:T(8,128)(2,1)S(1)}, bf16[64,4224]{1,0:T(8,128)(2,1)S(1)}, u32[]{:S(2)}, u32[]{:S(2)}) collective-permute-start(bf16[64,4224]{1,0:T(8,128)(2,1)S(1)} %get-tuple-element.138.x_ref.refs_3_), channel_id=1, source_target_pairs={{8,12},{5,1},{10,14},{7,3},{24,28},{21,17},{26,30},{23,19}} | collective-permute-start | bytes 1622024 | tf_op jit(solution)/shard_map/ppermute | solution.py:691
  251.0 22.5 %collective-permute-start.39 = (bf16[64,4224]{1,0:T(8,128)(2,1)S(1)}, bf16[64,4224]{1,0:T(8,128)(2,1)S(1)}, u32[]{:S(2)}, u32[]{:S(2)}) collective-permute-start(bf16[64,4224]{1,0:T(8,128)(2,1)S(1)} %get-tuple-element.139.x_ref.refs_3_), channel_id=1, source_target_pairs={{4,0},{9,13},{6,2},{11,15},{20,16},{25,29},{22,18},{27,31}} | collective-permute-start | bytes 1622024 | tf_op jit(solution)/shard_map/ppermute | solution.py:691
  252.9 33.5 %collective-permute-start.35 = (bf16[64,4224]{1,0:T(8,128)(2,1)S(1)}, bf16[64,4224]{1,0:T(8,128)(2,1)S(1)}, u32[]{:S(2)}, u32[]{:S(2)}) collective-permute-start(bf16[64,4224]{1,0:T(8,128)(2,1)S(1)} %get-tuple-element.140.x_ref.refs_3_), channel_id=1, source_target_pairs={{8,12},{5,1},{10,14},{7,3},{24,28},{21,17},{26,30},{23,19}} | collective-permute-start | bytes 1622024 | tf_op jit(solution)/shard_map/ppermute | solution.py:691
  262.6 31.6 %collective-permute-start.37 = (bf16[64,4224]{1,0:T(8,128)(2,1)S(1)}, bf16[64,4224]{1,0:T(8,128)(2,1)S(1)}, u32[]{:S(2)}, u32[]{:S(2)}) collective-permute-start(bf16[64,4224]{1,0:T(8,128)(2,1)S(1)} %get-tuple-element.142), channel_id=1, source_target_pairs={{4,0},{9,13},{6,2},{11,15},{20,16},{25,29},{22,18},{27,31}} | collective-permute-start | bytes 1622024 | tf_op jit(solution)/shard_map/ppermute | solution.py:691
  (30 other events, 402.4 us)

commit v8 on v7

--- a/solution.py
+++ b/solution.py
@@ -14,7 +14,8 @@
 PIECES = 2
 SPLIT = 4
 SHORT, LONG = 0.2, 5.0
-LIMIT = 20 * 1024 * 1024
+SMALL, LIMIT = 6 * 1024 * 1024, 14 * 1024 * 1024
+QUARTERS = 4
 
 F32, BF16 = jnp.float32, jnp.bfloat16
 ANY = pl.BlockSpec(memory_space=pl.ANY)
@@ -114,54 +115,81 @@
     )(by_share, *([in_hbm(w_out)] * SPLIT), *more)
 
 
-def backward_piece(blocks, w_out, chunk, chunks, halves, piece, pieces, total, last, held, after):
+def load_weights(w_out, piece, pieces, after):
+    rows = w_out.shape[0] // pieces
+    width = w_out.shape[1]
+
+    def kernel(w_ref, *refs):
+        out_ref, sem = refs[-2:]
+        copy = pltpu.make_async_copy(w_ref.at[pl.ds(piece * rows, rows)], out_ref, sem)
+        copy.start()
+        copy.wait()
+
+    return pl.pallas_call(
+        kernel,
+        in_specs=[ANY] * (1 + len(after)),
+        out_specs=pl.BlockSpec(memory_space=pltpu.VMEM),
+        out_shape=pltpu.VMEM((rows, width), BF16),
+        scratch_shapes=[pltpu.SemaphoreType.DMA],
+        compiler_params=pltpu.CompilerParams(vmem_limit_bytes=SMALL),
+        cost_estimate=cost(SHORT),
+        name="load_weights",
+    )(in_hbm(w_out), *after)
+
+
+def backward_piece(blocks, weights, chunk, chunks, halves, piece, pieces, total, last, held, after):
     parts, rows, _ = blocks[0][1].shape
-    half = w_out.shape[1] // halves
-    depth = w_out.shape[0]
-    span = depth // pieces
-    cols = divisor(span, 256)
-    steps = span // cols
-    cut = half // SPLIT
-    n = len(blocks)
+    some, width = weights[0].shape
+    half, span = width // halves, some * len(weights)
+    cols = divisor(some, 256)
+    n, m = len(blocks), len(weights)
 
     def kernel(*refs):
         out_ref, tok_ref = refs[-2:]
-        y = None if total is None else refs[n + n * SPLIT][...].reshape(parts * rows, cols)
-        for b in range(n):
-            g = refs[b][...].reshape(parts * rows, half)
-            for s in range(SPLIT):
-                term = project_rows(g[:, s * cut : (s + 1) * cut], refs[n + b * SPLIT + s][...])
-                y = term if y is None else y + term
-        out_ref[...] = y.astype(out_ref.dtype).reshape(parts, rows, cols)
+        for j in range(m):
+
+            def step(i, carry):
+                here = pl.ds(pl.multiple_of(i * cols, cols), cols)
+                there = pl.ds(pl.multiple_of(j * some + i * cols, cols), cols)
+                y = None if total is None else refs[n + m][:, :, there].reshape(parts * rows, cols)
+                for b, (at, _) in enumerate(blocks):
+                    g = refs[b][...].reshape(parts * rows, half)
+                    term = project_rows(g, refs[n + j][here, at * half : (at + 1) * half])
+                    y = term if y is None else y + term
+                out_ref[:, :, there] = y.astype(out_ref.dtype).reshape(parts, rows, cols)
+                return carry
+
+            lax.fori_loop(0, some // cols, step, 0)
         tok_ref[...] = jnp.zeros_like(tok_ref)
 
-    here = pl.BlockSpec((parts, rows, cols), lambda i: (0, 0, piece * steps + i))
+    once = pl.Buffered(1)
+    here = pl.BlockSpec((parts, rows, span), lambda i: (0, 0, piece))
     if last:
-        out_spec = pl.BlockSpec((parts, None, rows, cols), lambda i: (0, chunk, 0, piece * steps + i))
-        out_shape = jax.ShapeDtypeStruct((parts, chunks, rows, depth), BF16)
+        out_spec = pl.BlockSpec((parts, None, rows, span), lambda i: (0, chunk, 0, piece))
+        out_shape = jax.ShapeDtypeStruct((parts, chunks, rows, span * pieces), BF16)
     else:
-        out_spec, out_shape = here, jax.ShapeDtypeStruct((parts, rows, depth), F32)
-    weights = [
-        pl.BlockSpec((cols, cut), lambda i, at=at * SPLIT + s: (piece * steps + i, at))
-        for at, _ in blocks
-        for s in range(SPLIT)
-    ]
+        out_spec, out_shape = here, jax.ShapeDtypeStruct((parts, rows, span * pieces), F32)
     sums = [] if total is None else [total]
     extra = ([] if held is None else [held]) + after
     return pl.pallas_call(
         kernel,
-        grid=(steps,),
-        in_specs=[pl.BlockSpec((parts, rows, half), lambda i: (0, 0, 0))] * n
-        + weights
-        + [here] * len(sums)
+        grid=(1,),
+        in_specs=[pl.BlockSpec((parts, rows, half), lambda i: (0, 0, 0), pipeline_mode=once)] * n
+        + [pl.BlockSpec(memory_space=pltpu.VMEM)] * m
+        + [pl.BlockSpec((parts, rows, span), lambda i: (0, 0, piece), pipeline_mode=once)] * len(sums)
         + [ANY] * len(extra),
         out_specs=[out_spec, TOKEN_SPEC],
         out_shape=[out_shape, TOKEN],
-        input_output_aliases={} if held is None else {n + n * SPLIT + len(sums): 0},
+        input_output_aliases={} if held is None else {n + m + len(sums): 0},
         compiler_params=pltpu.CompilerParams(vmem_limit_bytes=LIMIT),
         cost_estimate=cost(SHORT),
         name="backward_piece",
-    )(*[g for _, g in blocks], *([in_hbm(w_out)] * (n * SPLIT)), *sums, *extra)
+    )(
+        *[g for _, g in blocks],
+        *[pltpu.with_memory_space_constraint(w, pltpu.VMEM) for w in weights],
+        *sums,
+        *extra,
+    )
 
 
 def relay(pos, flow, k, partial, came, held, after):
@@ -195,10 +223,15 @@
             pl.when(place >= k)(store.wait)
 
     line = jax.ShapeDtypeStruct((rows, width), BF16)
-    whole = pl.BlockSpec((rows, width), lambda i, w: (0, 0))
+    whole = pl.BlockSpec((rows, width), lambda i, w: (0, 0), pipeline_mode=pl.Buffered(1))
     args, specs, out_specs, out_shape, alias = [came], [whole], [whole], [line], {}
     if partial is not None:
-        specs.append(pl.BlockSpec((None, rows, width), lambda i, w: (far(w, parts - k), 0, 0)))
+        term = pl.BlockSpec(
+            (None, rows, width),
+            lambda i, w: (far(w, parts - k), 0, 0),
+            pipeline_mode=pl.Buffered(1),
+        )
+        specs.append(term)
         args.append(partial)
     if held is not None:
         alias[1 + len(args)] = 1
@@ -217,7 +250,7 @@
         ),
         out_shape=out_shape,
         input_output_aliases=alias,
-        compiler_params=pltpu.CompilerParams(vmem_limit_bytes=LIMIT),
+        compiler_params=pltpu.CompilerParams(vmem_limit_bytes=SMALL),
         cost_estimate=cost(LONG),
         name="relay",
     )(pos, *args, *after)
@@ -253,7 +286,7 @@
         ),
         out_shape=jax.ShapeDtypeStruct(held.shape, BF16),
         input_output_aliases={3: 0},
-        compiler_params=pltpu.CompilerParams(vmem_limit_bytes=LIMIT),
+        compiler_params=pltpu.CompilerParams(vmem_limit_bytes=SMALL),
         cost_estimate=cost(SHORT),
         name="store_last",
     )(pos, *came, held, *after)
@@ -278,7 +311,7 @@
             out_specs=pl.BlockSpec((rows, width), lambda i, w: (0, 0)),
         ),
         out_shape=jax.ShapeDtypeStruct((rows, width), BF16),
-        compiler_params=pltpu.CompilerParams(vmem_limit_bytes=LIMIT),
+        compiler_params=pltpu.CompilerParams(vmem_limit_bytes=SMALL),
         cost_estimate=cost(SHORT),
         name="first_block",
     )(pos, partial)
@@ -293,9 +326,10 @@
 
 def norm_specs(ins, half, chunk, at):
     _, rows, wide = ins[0].shape
-    whole = pl.BlockSpec((rows, wide), lambda i, r: (0, 0))
-    own = pl.BlockSpec((None, rows, half), lambda i, r: (0, chunk, at))
-    mine = pl.BlockSpec((None, rows, wide), lambda i, r: (r[0], 0, 0))
+    once = pl.Buffered(1)
+    whole = pl.BlockSpec((rows, wide), lambda i, r: (0, 0), pipeline_mode=once)
+    own = pl.BlockSpec((None, rows, half), lambda i, r: (0, chunk, at), pipeline_mode=once)
+    mine = pl.BlockSpec((None, rows, wide), lambda i, r: (r[0], 0, 0), pipeline_mode=once)
     return [mine, whole, whole, own, own, pl.BlockSpec((1, half), lambda i, r: (0, at))]
 
 
@@ -414,7 +448,7 @@
         in_specs=[whole] + [ANY] * len(after),
         out_specs=whole,
         out_shape=jax.ShapeDtypeStruct(value.shape, value.dtype),
-        compiler_params=pltpu.CompilerParams(vmem_limit_bytes=LIMIT),
+        compiler_params=pltpu.CompilerParams(vmem_limit_bytes=SMALL),
         cost_estimate=cost(SHORT),
         name="tie",
     )(value, *after)
@@ -430,7 +464,7 @@
         in_specs=[ANY],
         out_specs=TOKEN_SPEC,
         out_shape=TOKEN,
-        compiler_params=pltpu.CompilerParams(vmem_limit_bytes=LIMIT),
+        compiler_params=pltpu.CompilerParams(vmem_limit_bytes=SMALL),
         cost_estimate=cost(SHORT),
         name="touch",
     )(x)
@@ -507,15 +541,14 @@
         out_ref, all_ref = refs[-2:]
         for back in range(size):
             all_ref[lax.rem(pos_ref[3] - back + size, size)] = refs[back][...]
-        q = refs[size][...].astype(F32)
         for d in range(size):
-            out_ref[d * EX_DEV : (d + 1) * EX_DEV, :] = lax.dot_general(
-                all_ref[d],
-                q,
-                (((1,), (1,)), ((), ())),
-                precision=lax.Precision.HIGHEST,
-                preferred_element_type=F32,
-            )
+            rest, total = all_ref[d], None
+            for _ in range(3):
+                part = rest.astype(BF16)
+                rest = rest - part.astype(F32)
+                term = project_rows(part, refs[size][...])
+                total = term if total is None else total + term
+            out_ref[d * EX_DEV : (d + 1) * EX_DEV, :] = total
 
     return pl.pallas_call(
         kernel,
@@ -559,7 +592,7 @@
             scratch_shapes=[pltpu.VMEM((size,) + shape, F32)],
         ),
         out_shape=jax.ShapeDtypeStruct(shape, F32),
-        compiler_params=pltpu.CompilerParams(vmem_limit_bytes=LIMIT),
+        compiler_params=pltpu.CompilerParams(vmem_limit_bytes=SMALL),
         cost_estimate=cost(SHORT),
         name="score_sum",
     )(pos, *terms, *after)
@@ -592,7 +625,7 @@
                     out.append((t * queriers + q, (t + way) * queriers + q))
         return out
 
-    work, marks = [], []
+    work, marks, resident = [], [], []
     partials, totals, result = {}, {}, [None]
 
     def forward(c, h, piece, pieces, after):
@@ -614,8 +647,9 @@
 
     def backward(c, blocks, total, last, piece, pieces, after):
         held = result[0] if last else totals.get(c)
+        some = resident[piece * QUARTERS // pieces : (piece + 1) * QUARTERS // pieces]
         done, mark = backward_piece(
-            blocks, w_out, c, chunks, HALVES, piece, pieces, total, last, held, after
+            blocks, some, c, chunks, HALVES, piece, pieces, total, last, held, after
         )
         if last:
             result[0] = done
@@ -632,6 +666,12 @@
     def finish(key, after):
         while any(k == key for k, _ in work):
             do_one(list(marks) + after)
+
+    def load(count, after):
+        for _ in range(count):
+            resident.append(load_weights(w_out, len(resident), QUARTERS, after))
+            after = [resident[-1]]
+        marks[:] = after
 
     def add_forward(c, h, pieces):
         for piece in range(pieces):
@@ -664,6 +704,8 @@
                     if rs and slot > 1:
                         add_forward(slot, h, PIECES)
                     do_one([sent[h - 1, 1]])
+                    if not rs:
+                        finish(("b", slot - 2), [])
                     grad[h], held[h] = norm_out(
                         pos, [(h, ins[h])], half, slot - 1, sums, None, list(marks)
                     )
@@ -694,6 +736,13 @@
                         pairs(flow, 0 if reduce_now else k, parts - 2 if gather_now else k - 1),
                     )
                     sent[h, flow] = x
+                    if slot == chunks - 1 and flow == 1 and slot > 0:
+                        if (k, h) in ((parts - 2, HALVES - 1), (parts - 1, 0)):
+                            load(1, [x])
+                            continue
+                        if (k, h) == (parts - 1, HALVES - 1):
+                            load(QUARTERS - len(resident), [x])
+                            continue
                     if slot == 0 and k == 2 and (h, flow) == (HALVES - 1, 1) and chunks > 1 and HALVES > 1:
                         add_forward(1, 1, PIECES)
                         do_one([x])

time: 309 us -> 302 us (0.977)
  waiting for transfers between devices: 80.6 us -> 72.3 us
  local copies, waits for them, and re-layouts: 1.77 us -> 5.15 us
    ppermute x40, waiting for transfers between devices: 80.6 us -> 72.3 us  [body(): lax.ppermute(x, ('tensor', 'query'), pairs(flow, 0 if reduce_now else k,...]
    unnamed x20 -> x44, local copies, waits for them, and re-layouts: 1.75 us -> 5.13 us
    pallas_call x4 -> x8, Pallas kernels: 40 us -> 42.1 us  [the longest x4 25.5 us: backward_piece(): pl.pallas_call(kernel, grid=(1,), in_specs=[pl.BlockSpec((parts, rows, ha...]
  transfers between devices with their start and end apart: 44 -> 44, of which waited for: 16 -> 14; matrix products, arithmetic and copies ran while one was open for 0% -> 0% of each run, Pallas kernels for 34% -> 35%
where the time goes in v8:
time: 302 us; the launch traced here: 301 us
  Pallas kernels  125 us (41%)
  starting transfers between devices  96.5 us (32%)
  waiting for transfers between devices  72.3 us (24%)
  local copies, waits for them, and re-layouts  5.15 us (2%)
    ppermute x40, starting transfers between devices, body(): lax.ppermute(x, ('tensor', 'query'), pairs(flow, 0 if reduce_now else k,...  92.5 us
    ppermute x40, waiting for transfers between devices, body(): lax.ppermute(x, ('tensor', 'query'), pairs(flow, 0 if reduce_now else k,...  72.3 us
    pallas_call x5, Pallas kernels, forward_piece(): pl.pallas_call(kernel, grid=(steps,), in_specs=[pl.BlockSpec((parts, None...  42.6 us
    pallas_call x4, Pallas kernels, backward_piece(): pl.pallas_call(kernel, grid=(1,), in_specs=[pl.BlockSpec((parts, rows, ha...  25.5 us
    pallas_call x28, Pallas kernels, relay(): pl.pallas_call(kernel, grid_spec=pltpu.PrefetchScalarGridSpec(num_scalar_...  18.4 us
    pallas_call x4, Pallas kernels, load_weights(): pl.pallas_call(kernel, in_specs=[ANY] * (1 + len(after)), out_specs=pl.Bl...  16.6 us
    pallas_call x4, Pallas kernels, norm_out(): pl.pallas_call(kernel, grid_spec=pltpu.PrefetchScalarGridSpec(num_scalar_...  6.78 us
  transfers between devices with their start and end apart: 44, of which 14 were waited for; matrix products, arithmetic and copies ran while one was open for 0% of the time, Pallas kernels for 35%

profile of v8, /device:TPU:0, one launch (start us, length us, event | category | flops | bytes accessed | tf_op | source)
XLA Modules:
  0.0 300.6 jit_solution(15749858069026817769)
XLA Ops:
  2.2 10.4 %forward_piece.5 = (bf16[4,64,4224]{2,1,0:T(8,128)(2,1)S(1)}, f32[8,128]{1,0:T(8,128)S(1)}) custom-call(bf16[4,2,64,2048]{3,2,1,0:T(8,128)(2,1)S(1)} %bitcast.14, bf16[2048,8192]{1,0:T(8,128)(2,1)} %w_ref.7, bf16[2048,8192]{1,0:T(8,128)(2,1)} %w_ref.7, bf16[2048,8192]{1,0:T(8,128)(2,1)} %w_ref.7, bf16[2048,8192]{1,0:T(8,128)(2,1)} %w_ref.7), custom_call_target="tpu_custom_call" | custom-call | bytes 720000 | tf_op jit(solution)/shard_map/forward_piece/pallas_call | solution.py:100
  13.9 5.0 %collective-permute-start.3 = (bf16[64,4224]{1,0:T(8,128)(2,1)S(1)}, bf16[64,4224]{1,0:T(8,128)(2,1)S(1)}, u32[]{:S(2)}, u32[]{:S(2)}) collective-permute-start(bf16[64,4224]{1,0:T(8,128)(2,1)S(1)} %first_block.7), channel_id=1, source_target_pairs={{0,4},{13,9},{2,6},{15,11},{16,20},{29,25},{18,22},{31,27}} | collective-permute-start | bytes 1622024 | tf_op jit(solution)/shard_map/ppermute | solution.py:733
  20.2 10.4 %forward_piece.6 = (bf16[4,64,4224]{2,1,0:T(8,128)(2,1)S(1)}, f32[8,128]{1,0:T(8,128)S(1)}) custom-call(bf16[4,2,64,2048]{3,2,1,0:T(8,128)(2,1)S(1)} %bitcast.16, bf16[2048,8192]{1,0:T(8,128)(2,1)} %w_ref.7, bf16[2048,8192]{1,0:T(8,128)(2,1)} %w_ref.7, bf16[2048,8192]{1,0:T(8,128)(2,1)} %w_ref.7, bf16[2048,8192]{1,0:T(8,128)(2,1)} %w_ref.7, ...), custom_call_target="tpu_custom_call" | custom-call | bytes 720000 | tf_op jit(solution)/shard_map/forward_piece/pallas_call | solution.py:100
  37.8 7.2 %collective-permute-done.1.refs_0_ = bf16[64,4224]{1,0:T(8,128)(2,1)S(1)} collective-permute-done((bf16[64,4224]{1,0:T(8,128)(2,1)S(1)}, bf16[64,4224]{1,0:T(8,128)(2,1)S(1)}, u32[]{:S(2)}, u32[]{:S(2)}) %collective-permute-start.1) | collective-permute-done | bytes 540704 | tf_op jit(solution)/shard_map/ppermute | solution.py:733
  51.5 5.6 %forward_piece.7 = (bf16[4,64,4224]{2,1,0:T(8,128)(2,1)S(1)}, f32[8,128]{1,0:T(8,128)S(1)}) custom-call(bf16[4,2,64,2048]{3,2,1,0:T(8,128)(2,1)S(1)} %bitcast.17, bf16[2048,8192]{1,0:T(8,128)(2,1)} %w_ref.7, bf16[2048,8192]{1,0:T(8,128)(2,1)} %w_ref.7, bf16[2048,8192]{1,0:T(8,128)(2,1)} %w_ref.7, bf16[2048,8192]{1,0:T(8,128)(2,1)} %w_ref.7, ...), custom_call_target="tpu_custom_call" | custom-call | bytes 720000 | tf_op jit(solution)/shard_map/forward_piece/pallas_call | solution.py:100
  59.7 4.7 %collective-permute-start.5 = (bf16[64,4224]{1,0:T(8,128)(2,1)S(1)}, bf16[64,4224]{1,0:T(8,128)(2,1)S(1)}, u32[]{:S(2)}, u32[]{:S(2)}) collective-permute-start(bf16[64,4224]{1,0:T(8,128)(2,1)S(1)} %relay.32.refs_3_), channel_id=1, source_target_pairs={{0,4},{4,8},{8,12},{5,1},{9,5},{13,9},{2,6},{6,10},{10,14},{7,3},{... | collective-permute-start | bytes 1622024 | tf_op jit(solution)/shard_map/ppermute | solution.py:733
  70.8 5.1 %collective-permute-start.9 = (bf16[64,4224]{1,0:T(8,128)(2,1)S(1)}, bf16[64,4224]{1,0:T(8,128)(2,1)S(1)}, u32[]{:S(2)}, u32[]{:S(2)}) collective-permute-start(bf16[64,4224]{1,0:T(8,128)(2,1)S(1)} %relay.34.refs_3_), channel_id=1, source_target_pairs={{0,4},{4,8},{8,12},{5,1},{9,5},{13,9},{2,6},{6,10},{10,14},{7,3},{... | collective-permute-start | bytes 1622024 | tf_op jit(solution)/shard_map/ppermute | solution.py:733
  76.0 10.6 %forward_piece.8 = (bf16[4,64,4224]{2,1,0:T(8,128)(2,1)S(1)}, f32[8,128]{1,0:T(8,128)S(1)}) custom-call(bf16[4,2,64,2048]{3,2,1,0:T(8,128)(2,1)S(1)} %bitcast.18, bf16[2048,8192]{1,0:T(8,128)(2,1)} %w_ref.7, bf16[2048,8192]{1,0:T(8,128)(2,1)} %w_ref.7, bf16[2048,8192]{1,0:T(8,128)(2,1)} %w_ref.7, bf16[2048,8192]{1,0:T(8,128)(2,1)} %w_ref.7, ...), custom_call_target="tpu_custom_call" | custom-call | bytes 720000 | tf_op jit(solution)/shard_map/forward_piece/pallas_call | solution.py:100
  100.6 5.6 %forward_piece.9 = (bf16[4,64,4224]{2,1,0:T(8,128)(2,1)S(1)}, f32[8,128]{1,0:T(8,128)S(1)}) custom-call(bf16[4,2,64,2048]{3,2,1,0:T(8,128)(2,1)S(1)} %bitcast.19, bf16[2048,8192]{1,0:T(8,128)(2,1)} %w_ref.7, bf16[2048,8192]{1,0:T(8,128)(2,1)} %w_ref.7, bf16[2048,8192]{1,0:T(8,128)(2,1)} %w_ref.7, ...), custom_call_target="tpu_custom_call", output_to_operand_aliasing={{0}: (5, {})} | custom-call | bytes 720000 | tf_op jit(solution)/shard_map/forward_piece/pallas_call | solution.py:100
  107.4 4.6 %collective-permute-start.12 = (bf16[64,4224]{1,0:T(8,128)(2,1)S(1)}, bf16[64,4224]{1,0:T(8,128)(2,1)S(1)}, u32[]{:S(2)}, u32[]{:S(2)}) collective-permute-start(bf16[64,4224]{1,0:T(8,128)(2,1)S(1)} %get-tuple-element.90.refs_4_), channel_id=1, source_target_pairs={{0,4},{4,8},{8,12},{5,1},{9,5},{13,9},{2,6},{6,10},{10,14},{7,3},{... | collective-permute-start | bytes 1622024 | tf_op jit(solution)/shard_map/ppermute | solution.py:733
  114.5 4.5 %collective-permute-start.18 = (bf16[64,4224]{1,0:T(8,128)(2,1)S(1)}, bf16[64,4224]{1,0:T(8,128)(2,1)S(1)}, u32[]{:S(2)}, u32[]{:S(2)}) collective-permute-start(bf16[64,4224]{1,0:T(8,128)(2,1)S(1)} %get-tuple-element.95.refs_4_), channel_id=1, source_target_pairs={{0,4},{4,8},{8,12},{5,1},{9,5},{13,9},{2,6},{6,10},{10,14},{7,3},{... | collective-permute-start | bytes 1622024 | tf_op jit(solution)/shard_map/ppermute | solution.py:733
  131.2 4.5 %collective-permute-done.18.refs_0_ = bf16[64,4224]{1,0:T(8,128)(2,1)S(1)} collective-permute-done((bf16[64,4224]{1,0:T(8,128)(2,1)S(1)}, bf16[64,4224]{1,0:T(8,128)(2,1)S(1)}, u32[]{:S(2)}, u32[]{:S(2)}) %collective-permute-start.18) | collective-permute-done | bytes 540704 | tf_op jit(solution)/shard_map/ppermute | solution.py:733
  169.0 4.6 %collective-permute-start.26 = (bf16[64,4224]{1,0:T(8,128)(2,1)S(1)}, bf16[64,4224]{1,0:T(8,128)(2,1)S(1)}, u32[]{:S(2)}, u32[]{:S(2)}) collective-permute-start(bf16[64,4224]{1,0:T(8,128)(2,1)S(1)} %get-tuple-element.111.refs_4_), channel_id=1, source_target_pairs={{0,4},{4,8},{8,12},{5,1},{9,5},{13,9},{2,6},{6,10},{10,14},{7,3},{... | collective-permute-start | bytes 1622024 | tf_op jit(solution)/shard_map/ppermute | solution.py:733
  176.2 4.6 %collective-permute-start.23 = (bf16[64,4224]{1,0:T(8,128)(2,1)S(1)}, bf16[64,4224]{1,0:T(8,128)(2,1)S(1)}, u32[]{:S(2)}, u32[]{:S(2)}) collective-permute-start(bf16[64,4224]{1,0:T(8,128)(2,1)S(1)} %get-tuple-element.113.refs_4_), channel_id=1, source_target_pairs={{0,4},{4,8},{8,12},{5,1},{9,5},{13,9},{2,6},{6,10},{10,14},{7,3},{... | collective-permute-start | bytes 1622024 | tf_op jit(solution)/shard_map/ppermute | solution.py:733
  184.2 6.4 %load_weights.7.refs_6_.refs_8_.refs_3_.refs_4_ = bf16[512,8192]{1,0:T(8,128)(2,1)S(1)} custom-call(bf16[2048,8192]{1,0:T(8,128)(2,1)} %w_ref.7, bf16[512,8192]{1,0:T(8,128)(2,1)S(1)} %load_weights.6.refs_0_.refs_2_.refs_3_), custom_call_target="tpu_custom_call" | custom-call | bytes 720000 | tf_op jit(solution)/shard_map/load_weights/pallas_call | solution.py:128
  203.3 6.2 %backward_piece.4 = (bf16[4,2,64,2048]{3,2,1,0:T(8,128)(2,1)}, f32[8,128]{1,0:T(8,128)S(1)}) custom-call(bf16[4,64,4224]{2,1,0:T(8,128)(2,1)S(1)} %get-tuple-element.120.refs_0_, bf16[4,64,4224]{2,1,0:T(8,128)(2,1)S(1)} %get-tuple-element.121.refs_1_, bf16[512,8192]{1,0:T(8,128)(2,1)S(1)} %load_weights.4.refs_3_.refs_2_.refs_1_, ...), custom_call_target="tpu_custom_call" | custom-call | bytes 720000 | tf_op jit(solution)/shard_map/backward_piece/pallas_call | solution.py:174
  212.9 6.2 %backward_piece.5 = (bf16[4,2,64,2048]{3,2,1,0:T(8,128)(2,1)}, f32[8,128]{1,0:T(8,128)S(1)}) custom-call(bf16[4,64,4224]{2,1,0:T(8,128)(2,1)S(1)} %get-tuple-element.120.refs_0_, bf16[4,64,4224]{2,1,0:T(8,128)(2,1)S(1)} %get-tuple-element.121.refs_1_, bf16[512,8192]{1,0:T(8,128)(2,1)S(1)} %copy-done.5, ...), custom_call_target="tpu_custom_call", output_to_operand_aliasing={{0}: (4, {})} | custom-call | bytes 720000 | tf_op jit(solution)/shard_map/backward_piece/pallas_call | solution.py:174
  220.3 4.6 %collective-permute-start.28 = (bf16[64,4224]{1,0:T(8,128)(2,1)S(1)}, bf16[64,4224]{1,0:T(8,128)(2,1)S(1)}, u32[]{:S(2)}, u32[]{:S(2)}) collective-permute-start(bf16[64,4224]{1,0:T(8,128)(2,1)S(1)} %get-tuple-element.126.x_ref.refs_3_), channel_id=1, source_target_pairs={{0,4},{4,8},{8,12},{5,1},{9,5},{13,9},{2,6},{6,10},{10,14},{7,3},{... | collective-permute-start | bytes 1622024 | tf_op jit(solution)/shard_map/ppermute | solution.py:733
  229.6 6.7 %collective-permute-done.28.refs_0_ = bf16[64,4224]{1,0:T(8,128)(2,1)S(1)} collective-permute-done((bf16[64,4224]{1,0:T(8,128)(2,1)S(1)}, bf16[64,4224]{1,0:T(8,128)(2,1)S(1)}, u32[]{:S(2)}, u32[]{:S(2)}) %collective-permute-start.28) | collective-permute-done | bytes 540704 | tf_op jit(solution)/shard_map/ppermute | solution.py:733
  245.4 8.1 %collective-permute-done.33.refs_0_ = bf16[64,4224]{1,0:T(8,128)(2,1)S(1)} collective-permute-done((bf16[64,4224]{1,0:T(8,128)(2,1)S(1)}, bf16[64,4224]{1,0:T(8,128)(2,1)S(1)}, u32[]{:S(2)}, u32[]{:S(2)}) %collective-permute-start.33) | collective-permute-done | bytes 540704 | tf_op jit(solution)/shard_map/ppermute | solution.py:733
  257.1 8.0 %collective-permute-done.36.refs_0_ = bf16[64,4224]{1,0:T(8,128)(2,1)S(1)} collective-permute-done((bf16[64,4224]{1,0:T(8,128)(2,1)S(1)}, bf16[64,4224]{1,0:T(8,128)(2,1)S(1)}, u32[]{:S(2)}, u32[]{:S(2)}) %collective-permute-start.36) | collective-permute-done | bytes 540704 | tf_op jit(solution)/shard_map/ppermute | solution.py:733
  267.2 9.5 %collective-permute-done.39.b_ref = bf16[64,4224]{1,0:T(8,128)(2,1)S(1)} collective-permute-done((bf16[64,4224]{1,0:T(8,128)(2,1)S(1)}, bf16[64,4224]{1,0:T(8,128)(2,1)S(1)}, u32[]{:S(2)}, u32[]{:S(2)}) %collective-permute-start.39) | collective-permute-done | bytes 540704 | tf_op jit(solution)/shard_map/ppermute | solution.py:733
  279.5 6.1 %backward_piece.6 = (f32[4,64,2048]{2,1,0:T(8,128)S(1)}, f32[8,128]{1,0:T(8,128)S(1)}) custom-call(bf16[4,64,4224]{2,1,0:T(8,128)(2,1)S(1)} %store_last.2.refs_1_.refs_0_, bf16[512,8192]{1,0:T(8,128)(2,1)S(1)} %load_weights.4.refs_3_.refs_2_.refs_1_, bf16[512,8192]{1,0:T(8,128)(2,1)S(1)} %bitcast.7, bf16[512,8192]{1,0:T(8,128)(2,1)S(1)} %bitcast.13, ...), custom_call_target="tpu_custom_call" | custom-call | bytes 720000 | tf_op jit(solution)/shard_map/backward_piece/pallas_call | solution.py:174
  292.3 7.1 %backward_piece.7 = (bf16[4,2,64,2048]{3,2,1,0:T(8,128)(2,1)}, f32[8,128]{1,0:T(8,128)S(1)}) custom-call(bf16[4,64,4224]{2,1,0:T(8,128)(2,1)S(1)} %store_last.3.refs_0_, bf16[512,8192]{1,0:T(8,128)(2,1)S(1)} %load_weights.4.refs_3_.refs_2_.refs_1_, bf16[512,8192]{1,0:T(8,128)(2,1)S(1)} %bitcast.7, ...), custom_call_target="tpu_custom_call", output_to_operand_aliasing={{0}: (6, {})} | custom-call | bytes 720000 | tf_op jit(solution)/shard_map/backward_piece/pallas_call | solution.py:174
  (184 shorter events, 142.3 us)
Async XLA Ops:
  34.6 22.5 %collective-permute-start.4 = (bf16[64,4224]{1,0:T(8,128)(2,1)S(1)}, bf16[64,4224]{1,0:T(8,128)(2,1)S(1)}, u32[]{:S(2)}, u32[]{:S(2)}) collective-permute-start(bf16[64,4224]{1,0:T(8,128)(2,1)S(1)} %relay.28.refs_3_), channel_id=1, source_target_pairs={{0,4},{4,8},{9,5},{13,9},{2,6},{6,10},{11,7},{15,11},{16,20},{20,2... | collective-permute-start | bytes 1622024 | tf_op jit(solution)/shard_map/ppermute | solution.py:733
  37.1 20.7 %collective-permute-start.6 = (bf16[64,4224]{1,0:T(8,128)(2,1)S(1)}, bf16[64,4224]{1,0:T(8,128)(2,1)S(1)}, u32[]{:S(2)}, u32[]{:S(2)}) collective-permute-start(bf16[64,4224]{1,0:T(8,128)(2,1)S(1)} %relay.29.refs_3_), channel_id=1, source_target_pairs={{8,4},{12,8},{1,5},{5,9},{10,6},{14,10},{3,7},{7,11},{24,20},{28,2... | collective-permute-start | bytes 1622024 | tf_op jit(solution)/shard_map/ppermute | solution.py:733
  45.7 22.5 %collective-permute-start.8 = (bf16[64,4224]{1,0:T(8,128)(2,1)S(1)}, bf16[64,4224]{1,0:T(8,128)(2,1)S(1)}, u32[]{:S(2)}, u32[]{:S(2)}) collective-permute-start(bf16[64,4224]{1,0:T(8,128)(2,1)S(1)} %relay.30.refs_3_), channel_id=1, source_target_pairs={{0,4},{4,8},{9,5},{13,9},{2,6},{6,10},{11,7},{15,11},{16,20},{20,2... | collective-permute-start | bytes 1622024 | tf_op jit(solution)/shard_map/ppermute | solution.py:733
  58.4 28.3 %collective-permute-start.7 = (bf16[64,4224]{1,0:T(8,128)(2,1)S(1)}, bf16[64,4224]{1,0:T(8,128)(2,1)S(1)}, u32[]{:S(2)}, u32[]{:S(2)}) collective-permute-start(bf16[64,4224]{1,0:T(8,128)(2,1)S(1)} %relay.33.refs_3_), channel_id=1, source_target_pairs={{4,0},{8,4},{12,8},{1,5},{5,9},{9,13},{6,2},{10,6},{14,10},{3,7},{... | collective-permute-start | bytes 1622024 | tf_op jit(solution)/shard_map/ppermute | solution.py:733
  59.7 27.0 %collective-permute-start.5 = (bf16[64,4224]{1,0:T(8,128)(2,1)S(1)}, bf16[64,4224]{1,0:T(8,128)(2,1)S(1)}, u32[]{:S(2)}, u32[]{:S(2)}) collective-permute-start(bf16[64,4224]{1,0:T(8,128)(2,1)S(1)} %relay.32.refs_3_), channel_id=1, source_target_pairs={{0,4},{4,8},{8,12},{5,1},{9,5},{13,9},{2,6},{6,10},{10,14},{7,3},{... | collective-permute-start | bytes 1622024 | tf_op jit(solution)/shard_map/ppermute | solution.py:733
  114.5 21.2 %collective-permute-start.18 = (bf16[64,4224]{1,0:T(8,128)(2,1)S(1)}, bf16[64,4224]{1,0:T(8,128)(2,1)S(1)}, u32[]{:S(2)}, u32[]{:S(2)}) collective-permute-start(bf16[64,4224]{1,0:T(8,128)(2,1)S(1)} %get-tuple-element.95.refs_4_), channel_id=1, source_target_pairs={{0,4},{4,8},{8,12},{5,1},{9,5},{13,9},{2,6},{6,10},{10,14},{7,3},{... | collective-permute-start | bytes 1622024 | tf_op jit(solution)/shard_map/ppermute | solution.py:733
  119.8 21.1 %collective-permute-start.17 = (bf16[64,4224]{1,0:T(8,128)(2,1)S(1)}, bf16[64,4224]{1,0:T(8,128)(2,1)S(1)}, u32[]{:S(2)}, u32[]{:S(2)}) collective-permute-start(bf16[64,4224]{1,0:T(8,128)(2,1)S(1)} %get-tuple-element.96.refs_4_), channel_id=1, source_target_pairs={{4,0},{8,4},{12,8},{1,5},{5,9},{9,13},{6,2},{10,6},{14,10},{3,7},{... | collective-permute-start | bytes 1622024 | tf_op jit(solution)/shard_map/ppermute | solution.py:733
  124.8 22.5 %collective-permute-start.15 = (bf16[64,4224]{1,0:T(8,128)(2,1)S(1)}, bf16[64,4224]{1,0:T(8,128)(2,1)S(1)}, u32[]{:S(2)}, u32[]{:S(2)}) collective-permute-start(bf16[64,4224]{1,0:T(8,128)(2,1)S(1)} %get-tuple-element.97.refs_4_), channel_id=1, source_target_pairs={{0,4},{4,8},{8,12},{5,1},{9,5},{13,9},{2,6},{6,10},{10,14},{7,3},{... | collective-permute-start | bytes 1622024 | tf_op jit(solution)/shard_map/ppermute | solution.py:733
  129.9 22.5 %collective-permute-start.20 = (bf16[64,4224]{1,0:T(8,128)(2,1)S(1)}, bf16[64,4224]{1,0:T(8,128)(2,1)S(1)}, u32[]{:S(2)}, u32[]{:S(2)}) collective-permute-start(bf16[64,4224]{1,0:T(8,128)(2,1)S(1)} %get-tuple-element.101.refs_4_), channel_id=1, source_target_pairs={{4,0},{8,4},{12,8},{1,5},{5,9},{9,13},{6,2},{10,6},{14,10},{3,7},{... | collective-permute-start | bytes 1622024 | tf_op jit(solution)/shard_map/ppermute | solution.py:733
  136.4 22.5 %collective-permute-start.22 = (bf16[64,4224]{1,0:T(8,128)(2,1)S(1)}, bf16[64,4224]{1,0:T(8,128)(2,1)S(1)}, u32[]{:S(2)}, u32[]{:S(2)}) collective-permute-start(bf16[64,4224]{1,0:T(8,128)(2,1)S(1)} %get-tuple-element.103.refs_4_), channel_id=1, source_target_pairs={{0,4},{4,8},{8,12},{5,1},{9,5},{13,9},{2,6},{6,10},{10,14},{7,3},{... | collective-permute-start | bytes 1622024 | tf_op jit(solution)/shard_map/ppermute | solution.py:733
  141.5 22.1 %collective-permute-start.21 = (bf16[64,4224]{1,0:T(8,128)(2,1)S(1)}, bf16[64,4224]{1,0:T(8,128)(2,1)S(1)}, u32[]{:S(2)}, u32[]{:S(2)}) collective-permute-start(bf16[64,4224]{1,0:T(8,128)(2,1)S(1)} %get-tuple-element.104.refs_4_), channel_id=1, source_target_pairs={{4,0},{8,4},{12,8},{1,5},{5,9},{9,13},{6,2},{10,6},{14,10},{3,7},{... | collective-permute-start | bytes 1622024 | tf_op jit(solution)/shard_map/ppermute | solution.py:733
  148.0 25.6 %collective-permute-start.19 = (bf16[64,4224]{1,0:T(8,128)(2,1)S(1)}, bf16[64,4224]{1,0:T(8,128)(2,1)S(1)}, u32[]{:S(2)}, u32[]{:S(2)}) collective-permute-start(bf16[64,4224]{1,0:T(8,128)(2,1)S(1)} %get-tuple-element.105.refs_4_), channel_id=1, source_target_pairs={{0,4},{4,8},{8,12},{5,1},{9,5},{13,9},{2,6},{6,10},{10,14},{7,3},{... | collective-permute-start | bytes 1622024 | tf_op jit(solution)/shard_map/ppermute | solution.py:733
  153.1 21.2 %collective-permute-start.24 = (bf16[64,4224]{1,0:T(8,128)(2,1)S(1)}, bf16[64,4224]{1,0:T(8,128)(2,1)S(1)}, u32[]{:S(2)}, u32[]{:S(2)}) collective-permute-start(bf16[64,4224]{1,0:T(8,128)(2,1)S(1)} %get-tuple-element.109.refs_0_.refs_4_), channel_id=1, source_target_pairs={{4,0},{8,4},{12,8},{1,5},{5,9},{9,13},{6,2},{10,6},{14,10},{3,7},{... | collective-permute-start | bytes 1622024 | tf_op jit(solution)/shard_map/ppermute | solution.py:733
  167.7 23.0 %collective-permute-start.27 = (bf16[64,4224]{1,0:T(8,128)(2,1)S(1)}, bf16[64,4224]{1,0:T(8,128)(2,1)S(1)}, u32[]{:S(2)}, u32[]{:S(2)}) collective-permute-start(bf16[64,4224]{1,0:T(8,128)(2,1)S(1)} %get-tuple-element.112.refs_0_.refs_4_), channel_id=1, source_target_pairs={{4,0},{8,4},{12,8},{1,5},{5,9},{9,13},{6,2},{10,6},{14,10},{3,7},{... | collective-permute-start | bytes 1622024 | tf_op jit(solution)/shard_map/ppermute | solution.py:733
  169.0 21.8 %collective-permute-start.26 = (bf16[64,4224]{1,0:T(8,128)(2,1)S(1)}, bf16[64,4224]{1,0:T(8,128)(2,1)S(1)}, u32[]{:S(2)}, u32[]{:S(2)}) collective-permute-start(bf16[64,4224]{1,0:T(8,128)(2,1)S(1)} %get-tuple-element.111.refs_4_), channel_id=1, source_target_pairs={{0,4},{4,8},{8,12},{5,1},{9,5},{13,9},{2,6},{6,10},{10,14},{7,3},{... | collective-permute-start | bytes 1622024 | tf_op jit(solution)/shard_map/ppermute | solution.py:733
  174.9 20.9 %collective-permute-start.25 = (bf16[64,4224]{1,0:T(8,128)(2,1)S(1)}, bf16[64,4224]{1,0:T(8,128)(2,1)S(1)}, u32[]{:S(2)}, u32[]{:S(2)}) collective-permute-start(bf16[64,4224]{1,0:T(8,128)(2,1)S(1)} %get-tuple-element.115.refs_0_), channel_id=1, source_target_pairs={{4,0},{8,4},{12,8},{1,5},{5,9},{9,13},{6,2},{10,6},{14,10},{3,7},{... | collective-permute-start | bytes 1622024 | tf_op jit(solution)/shard_map/ppermute | solution.py:733
  199.3 26.9 %collective-permute-start.30 = (bf16[64,4224]{1,0:T(8,128)(2,1)S(1)}, bf16[64,4224]{1,0:T(8,128)(2,1)S(1)}, u32[]{:S(2)}, u32[]{:S(2)}) collective-permute-start(bf16[64,4224]{1,0:T(8,128)(2,1)S(1)} %get-tuple-element.122.refs_4_), channel_id=1, source_target_pairs={{0,4},{4,8},{8,12},{5,1},{9,5},{13,9},{2,6},{6,10},{10,14},{7,3},{... | collective-permute-start | bytes 1622024 | tf_op jit(solution)/shard_map/ppermute | solution.py:733
  202.0 25.5 %collective-permute-start.29 = (bf16[64,4224]{1,0:T(8,128)(2,1)S(1)}, bf16[64,4224]{1,0:T(8,128)(2,1)S(1)}, u32[]{:S(2)}, u32[]{:S(2)}) collective-permute-start(bf16[64,4224]{1,0:T(8,128)(2,1)S(1)} %get-tuple-element.122.refs_4_), channel_id=1, source_target_pairs={{4,0},{8,4},{12,8},{1,5},{5,9},{9,13},{6,2},{10,6},{14,10},{3,7},{... | collective-permute-start | bytes 1622024 | tf_op jit(solution)/shard_map/ppermute | solution.py:733
  228.2 25.4 %collective-permute-start.33 = (bf16[64,4224]{1,0:T(8,128)(2,1)S(1)}, bf16[64,4224]{1,0:T(8,128)(2,1)S(1)}, u32[]{:S(2)}, u32[]{:S(2)}) collective-permute-start(bf16[64,4224]{1,0:T(8,128)(2,1)S(1)} %get-tuple-element.131.x_ref.refs_3_), channel_id=1, source_target_pairs={{4,0},{8,4},{5,9},{9,13},{6,2},{10,6},{7,11},{11,15},{20,16},{24,2... | collective-permute-start | bytes 1622024 | tf_op jit(solution)/shard_map/ppermute | solution.py:733
  242.6 22.5 %collective-permute-start.36 = (bf16[64,4224]{1,0:T(8,128)(2,1)S(1)}, bf16[64,4224]{1,0:T(8,128)(2,1)S(1)}, u32[]{:S(2)}, u32[]{:S(2)}) collective-permute-start(bf16[64,4224]{1,0:T(8,128)(2,1)S(1)} %get-tuple-element.136.x_ref.refs_3_), channel_id=1, source_target_pairs={{4,0},{8,4},{5,9},{9,13},{6,2},{10,6},{7,11},{11,15},{20,16},{24,2... | collective-permute-start | bytes 1622024 | tf_op jit(solution)/shard_map/ppermute | solution.py:733
  244.6 22.7 %collective-permute-start.38 = (bf16[64,4224]{1,0:T(8,128)(2,1)S(1)}, bf16[64,4224]{1,0:T(8,128)(2,1)S(1)}, u32[]{:S(2)}, u32[]{:S(2)}) collective-permute-start(bf16[64,4224]{1,0:T(8,128)(2,1)S(1)} %get-tuple-element.138.x_ref.refs_3_), channel_id=1, source_target_pairs={{8,12},{5,1},{10,14},{7,3},{24,28},{21,17},{26,30},{23,19}} | collective-permute-start | bytes 1622024 | tf_op jit(solution)/shard_map/ppermute | solution.py:733
  254.2 22.5 %collective-permute-start.39 = (bf16[64,4224]{1,0:T(8,128)(2,1)S(1)}, bf16[64,4224]{1,0:T(8,128)(2,1)S(1)}, u32[]{:S(2)}, u32[]{:S(2)}) collective-permute-start(bf16[64,4224]{1,0:T(8,128)(2,1)S(1)} %get-tuple-element.139.x_ref.refs_3_), channel_id=1, source_target_pairs={{4,0},{9,13},{6,2},{11,15},{20,16},{25,29},{22,18},{27,31}} | collective-permute-start | bytes 1622024 | tf_op jit(solution)/shard_map/ppermute | solution.py:733
  256.3 29.2 %collective-permute-start.35 = (bf16[64,4224]{1,0:T(8,128)(2,1)S(1)}, bf16[64,4224]{1,0:T(8,128)(2,1)S(1)}, u32[]{:S(2)}, u32[]{:S(2)}) collective-permute-start(bf16[64,4224]{1,0:T(8,128)(2,1)S(1)} %get-tuple-element.140.x_ref.refs_3_), channel_id=1, source_target_pairs={{8,12},{5,1},{10,14},{7,3},{24,28},{21,17},{26,30},{23,19}} | collective-permute-start | bytes 1622024 | tf_op jit(solution)/shard_map/ppermute | solution.py:733
  265.8 25.9 %collective-permute-start.37 = (bf16[64,4224]{1,0:T(8,128)(2,1)S(1)}, bf16[64,4224]{1,0:T(8,128)(2,1)S(1)}, u32[]{:S(2)}, u32[]{:S(2)}) collective-permute-start(bf16[64,4224]{1,0:T(8,128)(2,1)S(1)} %get-tuple-element.142), channel_id=1, source_target_pairs={{4,0},{9,13},{6,2},{11,15},{20,16},{25,29},{22,18},{27,31}} | collective-permute-start | bytes 1622024 | tf_op jit(solution)/shard_map/ppermute | solution.py:733
  (42 other events, 626.9 us)
